TPU v7x, 32 devices: a whole 2x2x4 slice. The times are simulated.
32 devices in a mesh: fsdp: 2 (over core), ctx: 4 (over y, x), tp: 4 (over z).
Axes of the slice: x: 2, y: 2, z: 4, core: 2. Of those that a mesh axis runs over, the one named last changes fastest.
Arguments:
- inputs: bfloat16 [2, 1024, 1024], P('fsdp', 'ctx'), may hold values from -6 to 6
- query_weight: float32 [2, 1024, 1024], P(None, 'fsdp', 'tp'), may hold values from -0.1875 to 0.1875
- key_weight: float32 [2, 1024, 1024], P(None, 'fsdp', 'tp'), may hold values from -0.1875 to 0.1875
- value_weight: float32 [2, 1024, 1024], P(None, 'fsdp', 'tp'), may hold values from -0.1875 to 0.1875
- attention_weight: float32 [2, 1024, 1024], P(None, 'tp', 'fsdp'), may hold values from -4 to 4
- lookup_weight: float32 [2, 1024, 512], P(None, 'fsdp', 'tp'), may hold values from -0.1875 to 0.1875
- gate_weight: float32 [2, 1024, 1024], P(None, 'fsdp', 'tp'), may hold values from -0.1875 to 0.1875
- memory_weight: float32 [2, 1024, 1024], P(None, 'tp', 'fsdp'), may hold values from -0.75 to 0.75
- first_table: float32 [2, 4, 256, 64], P(None, 'tp', 'fsdp'), may hold values from -0.25 to 0.25
- second_table: float32 [2, 4, 256, 64], P(None, 'tp', 'fsdp'), may hold values from -0.25 to 0.25
- attention_gain: float32 [2, 1024], P(None, 'fsdp'), may hold values from 0.5 to 1.5
- memory_gain: float32 [2, 1024], P(None, 'fsdp'), may hold values from 0.5 to 1.5
- memory_values: bfloat16 [2, 65536, 1024], P(None, ('fsdp', 'ctx', 'tp')), may hold values from -6 to 6
- blocks: int32 [2, 1024], P('fsdp'), may hold values from 0 to 3, never falling along the last dimension, each value on 1 to 512 neighbouring positions
- first_picks: int32 [2, 2, 4, 1024, 4], P(None, 'fsdp', 'tp', 'ctx'), may hold values from 0 to 255, all different within a row; in each aligned block of 256 rows (0 to 255, 256 to 511, ..., all dimensions but the last counted through in order) at most 8 rows name the same one
- second_picks: int32 [2, 2, 4, 1024, 4, 8], P(None, 'fsdp', 'tp', 'ctx'), may hold values from 0 to 255, all different within a row
- cotangent: bfloat16 [2, 1024, 1024], P('fsdp', 'ctx'), may hold values from -6 to 6
Outputs:
- output: bfloat16 [2, 1024, 1024], P('fsdp', 'ctx')
- input_gradient: float32 [2, 1024, 1024], P('fsdp', 'ctx')
- query_gradient: float32 [2, 1024, 1024], P(None, 'fsdp', 'tp')
- key_gradient: float32 [2, 1024, 1024], P(None, 'fsdp', 'tp')
- value_gradient: float32 [2, 1024, 1024], P(None, 'fsdp', 'tp')
- attention_gradient: float32 [2, 1024, 1024], P(None, 'tp', 'fsdp')
- lookup_gradient: float32 [2, 1024, 512], P(None, 'fsdp', 'tp')
- gate_gradient: float32 [2, 1024, 1024], P(None, 'fsdp', 'tp')
- memory_gradient: float32 [2, 1024, 1024], P(None, 'tp', 'fsdp')
- first_gradient: float32 [2, 4, 256, 64], P(None, 'tp', 'fsdp')
- second_gradient: float32 [2, 4, 256, 64], P(None, 'tp', 'fsdp')
- attention_gain_gradient: float32 [2, 1024], P(None, 'fsdp')
- memory_gain_gradient: float32 [2, 1024], P(None, 'fsdp')
- values_gradient: float32 [2, 65536, 1024], P(None, ('fsdp', 'ctx', 'tp'))
Inputs may be any that keep to these rules, and one draw needn't show every extreme that they name: `first_picks`: the 4 first sub-keys of a token and memory head differ. In each aligned block of 256 positions of one block l, sequence and memory head, no first sub-key is named by more than 8 positions, a bound that some block reaches. `second_picks`: the 8 second sub-keys under one first pick differ. `blocks`: block numbers never fall along a sequence and every number occurs; a block holds 1 to 512 positions, and some block holds exactly 512.
All inputs are finite; a program needn't handle non-finite values.
Results may differ from a plain program's by a relative error of at most 0.035.
Values may be sent and summed in bfloat16 or wider, within the bound.
No kernel may reach another device: no remote copies, remote signals or barrier semaphores. Data moves between devices by JAX's collectives and lax.ppermute only.
A program may use at most 192 MiB of HBM per device.

v0:
```python
import jax
import jax.numpy as jnp
from jax import lax
from jax.sharding import PartitionSpec as P

HD = 64
NSUB = 256
CAP = 8


norm_eps = 1e-05
neg_fill = -1e30


def plain_dot(left_side, right_side):
    return jnp.dot(left_side, right_side, preferred_element_type=jnp.float32)


def dot_last(left_side, right_side):
    return lax.dot_general(
        left_side, right_side, (((1,), (1,)), ((), ())), preferred_element_type=jnp.float32
    )


def dot_first(left_side, right_side):
    return lax.dot_general(
        left_side, right_side, (((0,), (0,)), ((), ())), preferred_element_type=jnp.float32
    )


def silu_slope(gate_values):
    sigmoid = jax.nn.sigmoid(gate_values)
    return sigmoid * (1.0 + gate_values * (1.0 - sigmoid))


def norm_back(hidden, factor, gain_row, upstream):
    scaled = upstream * gain_row
    return factor * scaled - hidden * factor**3 * jnp.mean(scaled * hidden, axis=1, keepdims=True)


def tensor_total(partial_sum):
    return lax.psum(partial_sum.astype(jnp.bfloat16), "tp").astype(jnp.float32)


def slot_ranks(first_flat, table_width):
    onehot = (first_flat[:, None] == lax.iota(jnp.int32, table_width)[None, :]).astype(jnp.int32)
    running = jnp.cumsum(onehot, axis=0)
    return jnp.take_along_axis(running, first_flat[:, None], axis=1)[:, 0] - 1


def split_heads(queries, key_rows, value_rows, head_count):
    head_size = queries.shape[1] // head_count
    return (
        queries.reshape(queries.shape[0], head_count, head_size),
        key_rows.reshape(key_rows.shape[0], head_count, head_size),
        value_rows.reshape(value_rows.shape[0], head_count, head_size),
        head_size ** (-0.5),
    )


def attend_block(queries, key_rows, value_rows, query_ids, key_ids, head_count):
    query_heads, key_heads, value_heads, score_scale = split_heads(
        queries, key_rows, value_rows, head_count
    )
    raw_scores = (
        jnp.einsum("qhd,khd->hqk", query_heads, key_heads, preferred_element_type=jnp.float32)
        * score_scale
    )
    visible = key_ids[None, :] <= query_ids[:, None]
    raw_scores = jnp.where(visible[None], raw_scores, neg_fill)
    row_max = jnp.max(raw_scores, axis=2, keepdims=True)
    exponent = jnp.exp(raw_scores - row_max)
    row_total = jnp.sum(exponent, axis=2, keepdims=True)
    attention_weights = (exponent / row_total).astype(jnp.bfloat16)
    blended = jnp.einsum(
        "hqk,khd->qhd", attention_weights, value_heads, preferred_element_type=jnp.float32
    )
    log_total = row_max[:, :, 0] + jnp.log(row_total[:, :, 0])
    return (blended.reshape(queries.shape[0], -1).astype(jnp.bfloat16), log_total)


def attend_back(queries, key_rows, value_rows, upstream, log_total, query_ids, key_ids, head_count):
    query_heads, key_heads, value_heads, score_scale = split_heads(
        queries, key_rows, value_rows, head_count
    )
    raw_scores = (
        jnp.einsum("qhd,khd->hqk", query_heads, key_heads, preferred_element_type=jnp.float32)
        * score_scale
    )
    visible = key_ids[None, :] <= query_ids[:, None]
    attention_weights = jnp.where(visible[None], jnp.exp(raw_scores - log_total[:, :, None]), 0.0)
    upstream_heads = upstream.reshape(queries.shape[0], head_count, -1)
    weight_adjoint = jnp.einsum(
        "qhd,khd->hqk", upstream_heads, value_heads, preferred_element_type=jnp.float32
    )
    centre = jnp.sum(attention_weights * weight_adjoint, axis=2, keepdims=True)
    score_adjoint = (attention_weights * (weight_adjoint - centre)).astype(jnp.bfloat16)
    query_adjoint = (
        jnp.einsum("hqk,khd->qhd", score_adjoint, key_heads, preferred_element_type=jnp.float32)
        * score_scale
    )
    key_adjoint = (
        jnp.einsum("hqk,qhd->khd", score_adjoint, query_heads, preferred_element_type=jnp.float32)
        * score_scale
    )
    value_adjoint = jnp.einsum(
        "hqk,qhd->khd",
        attention_weights.astype(jnp.bfloat16),
        upstream_heads,
        preferred_element_type=jnp.float32,
    )
    return (
        query_adjoint.reshape(queries.shape[0], -1),
        key_adjoint.reshape(key_rows.shape[0], -1),
        value_adjoint.reshape(key_rows.shape[0], -1),
    )


def attention_forward(queries, key_rows, value_rows, query_ids, key_ids, head_count, block_rows):
    block_count = queries.shape[0] // block_rows

    def one_block(operands):
        return attend_block(operands[0], key_rows, value_rows, operands[1], key_ids, head_count)

    blended, log_total = lax.map(
        one_block,
        (queries.reshape(block_count, block_rows, -1), query_ids.reshape(block_count, block_rows)),
    )
    return (blended.reshape(queries.shape[0], -1), log_total)


def attention_backward(
    queries, key_rows, value_rows, upstream, log_total, query_ids, key_ids, head_count, block_rows
):
    block_count = queries.shape[0] // block_rows

    def one_block(carried, operands):
        query_adjoint, key_adjoint, value_adjoint = attend_back(
            operands[0],
            key_rows,
            value_rows,
            operands[1],
            operands[2],
            operands[3],
            key_ids,
            head_count,
        )
        return ((carried[0] + key_adjoint, carried[1] + value_adjoint), query_adjoint)

    zero_rows = jnp.zeros(key_rows.shape, jnp.float32)
    (key_total, value_total), query_total = lax.scan(
        one_block,
        (zero_rows, zero_rows),
        (
            queries.reshape(block_count, block_rows, -1),
            upstream.reshape(block_count, block_rows, -1),
            log_total,
            query_ids.reshape(block_count, block_rows),
        ),
    )
    return (query_total.reshape(queries.shape[0], -1), key_total, value_total)


def reduce_parts(
    query_part,
    key_part,
    value_part,
    attention_part,
    lookup_part,
    gate_part,
    memory_part,
    first_part,
    second_part,
    gain_one,
    gain_two,
):
    (
        query_share,
        key_share,
        value_share,
        attention_share,
        lookup_share,
        gate_share,
        memory_share,
        first_share,
        second_share,
        share_one,
        share_two,
    ) = (
        lax.psum_scatter(
            query_part.astype(jnp.bfloat16), "fsdp", scatter_dimension=1, tiled=True
        ).astype(jnp.float32),
        lax.psum_scatter(
            key_part.astype(jnp.bfloat16), "fsdp", scatter_dimension=1, tiled=True
        ).astype(jnp.float32),
        lax.psum_scatter(
            value_part.astype(jnp.bfloat16), "fsdp", scatter_dimension=1, tiled=True
        ).astype(jnp.float32),
        lax.psum_scatter(
            attention_part.astype(jnp.bfloat16), "fsdp", scatter_dimension=2, tiled=True
        ).astype(jnp.float32),
        lax.psum_scatter(
            lookup_part.astype(jnp.bfloat16), "fsdp", scatter_dimension=1, tiled=True
        ).astype(jnp.float32),
        lax.psum_scatter(
            gate_part.astype(jnp.bfloat16), "fsdp", scatter_dimension=1, tiled=True
        ).astype(jnp.float32),
        lax.psum_scatter(
            memory_part.astype(jnp.bfloat16), "fsdp", scatter_dimension=2, tiled=True
        ).astype(jnp.float32),
        lax.psum_scatter(
            first_part.astype(jnp.bfloat16), "fsdp", scatter_dimension=2, tiled=True
        ).astype(jnp.float32),
        lax.psum_scatter(
            second_part.astype(jnp.bfloat16), "fsdp", scatter_dimension=2, tiled=True
        ).astype(jnp.float32),
        lax.psum_scatter(
            gain_one.astype(jnp.bfloat16), "fsdp", scatter_dimension=1, tiled=True
        ).astype(jnp.float32),
        lax.psum_scatter(
            gain_two.astype(jnp.bfloat16), "fsdp", scatter_dimension=1, tiled=True
        ).astype(jnp.float32),
    )
    return (
        lax.psum(query_share.astype(jnp.bfloat16), "ctx").astype(jnp.float32),
        lax.psum(key_share.astype(jnp.bfloat16), "ctx").astype(jnp.float32),
        lax.psum(value_share.astype(jnp.bfloat16), "ctx").astype(jnp.float32),
        lax.psum(attention_share.astype(jnp.bfloat16), "ctx").astype(jnp.float32),
        lax.psum(lookup_share.astype(jnp.bfloat16), "ctx").astype(jnp.float32),
        lax.psum(gate_share.astype(jnp.bfloat16), "ctx").astype(jnp.float32),
        lax.psum(memory_share.astype(jnp.bfloat16), "ctx").astype(jnp.float32),
        lax.psum(first_share.astype(jnp.bfloat16), "ctx").astype(jnp.float32),
        lax.psum(second_share.astype(jnp.bfloat16), "ctx").astype(jnp.float32),
        lax.psum(share_one.astype(jnp.bfloat16), "ctx").astype(jnp.float32),
        lax.psum(share_two.astype(jnp.bfloat16), "ctx").astype(jnp.float32),
    )


def body(
    inputs,
    query_weight,
    key_weight,
    value_weight,
    attention_weight,
    lookup_weight,
    gate_weight,
    memory_weight,
    first_table,
    second_table,
    attention_gain,
    memory_gain,
    memory_values,
    blocks,
    first_picks,
    second_picks,
    cotangent,
):
    layer_count = query_weight.shape[0]
    tokens = inputs.shape[1]
    model_width = inputs.shape[2]
    head_count = query_weight.shape[2] // HD
    block_rows = min(512, tokens)
    fsdp_ctx = lax.axis_size("fsdp") * lax.axis_size("ctx")
    tp_size = lax.axis_size("tp")
    devices = fsdp_ctx * tp_size
    rows_dev = memory_values.shape[1]
    groups = rows_dev // NSUB
    sub_index = lax.iota(jnp.int32, NSUB)
    (
        full_query,
        full_key,
        full_value,
        full_attention,
        full_lookup,
        full_gate,
        full_memory,
        full_first,
        full_second,
        full_gain_one,
        full_gain_two,
    ) = (
        lax.all_gather(query_weight.astype(jnp.bfloat16), "fsdp", axis=1, tiled=True),
        lax.all_gather(key_weight.astype(jnp.bfloat16), "fsdp", axis=1, tiled=True),
        lax.all_gather(value_weight.astype(jnp.bfloat16), "fsdp", axis=1, tiled=True),
        lax.all_gather(attention_weight.astype(jnp.bfloat16), "fsdp", axis=2, tiled=True),
        lax.all_gather(lookup_weight.astype(jnp.bfloat16), "fsdp", axis=1, tiled=True),
        lax.all_gather(gate_weight.astype(jnp.bfloat16), "fsdp", axis=1, tiled=True),
        lax.all_gather(memory_weight.astype(jnp.bfloat16), "fsdp", axis=2, tiled=True),
        lax.all_gather(first_table.astype(jnp.bfloat16), "fsdp", axis=2, tiled=True),
        lax.all_gather(second_table.astype(jnp.bfloat16), "fsdp", axis=2, tiled=True),
        lax.all_gather(attention_gain.astype(jnp.bfloat16), "fsdp", axis=1, tiled=True),
        lax.all_gather(memory_gain.astype(jnp.bfloat16), "fsdp", axis=1, tiled=True),
    )
    key_ids = blocks[0]
    query_ids = lax.dynamic_slice_in_dim(key_ids, lax.axis_index("ctx") * tokens, tokens)
    residual = inputs[0].astype(jnp.float32)
    kept_state = []
    for layer_index in range(layer_count):
        gain_one = full_gain_one[layer_index].astype(jnp.float32)
        factor_one = lax.rsqrt(jnp.mean(residual * residual, axis=1, keepdims=True) + norm_eps)
        normed_one = (residual * factor_one * gain_one).astype(jnp.bfloat16)
        queries = plain_dot(normed_one, full_query[layer_index]).astype(jnp.bfloat16)
        key_part = plain_dot(normed_one, full_key[layer_index]).astype(jnp.bfloat16)
        value_part = plain_dot(normed_one, full_value[layer_index]).astype(jnp.bfloat16)
        key_rows, value_rows = (
            lax.all_gather(key_part, "ctx", axis=0, tiled=True),
            lax.all_gather(value_part, "ctx", axis=0, tiled=True),
        )
        attended, log_total = attention_forward(
            queries, key_rows, value_rows, query_ids, key_ids, head_count, block_rows
        )
        middle = residual + tensor_total(plain_dot(attended, full_attention[layer_index]))
        gain_two = full_gain_two[layer_index].astype(jnp.float32)
        factor_two = lax.rsqrt(jnp.mean(middle * middle, axis=1, keepdims=True) + norm_eps)
        normed_two = (middle * factor_two * gain_two).astype(jnp.bfloat16)
        lookups = plain_dot(normed_two, full_lookup[layer_index]).astype(jnp.bfloat16)
        half_width = lookups.shape[1] // 2
        score_first = dot_last(lookups[:, :half_width], full_first[layer_index][0])
        score_second = dot_last(lookups[:, half_width:], full_second[layer_index][0])
        first_ids = first_picks[layer_index, 0, 0]
        second_ids = second_picks[layer_index, 0, 0]
        pick_count = first_ids.shape[1]
        inner_count = second_ids.shape[2]
        picked_first = jnp.take_along_axis(score_first, first_ids, axis=1)
        picked_second = jnp.take_along_axis(
            score_second, second_ids.reshape(tokens, pick_count * inner_count), axis=1
        )
        logits = picked_first[:, :, None] + picked_second.reshape(tokens, pick_count, inner_count)
        weights = jax.nn.softmax(logits.reshape(tokens, -1), axis=1).reshape(
            tokens, pick_count, inner_count
        )
        rounded = weights.astype(jnp.bfloat16).astype(jnp.float32)
        spread = jnp.sum(
            jnp.where(second_ids[..., None] == sub_index, rounded[..., None], 0.0), axis=2
        ).astype(jnp.bfloat16)
        first_flat = first_ids.reshape(-1)
        slot_rank = slot_ranks(first_flat, NSUB)
        outbox = (
            jnp.zeros((NSUB, CAP, NSUB), jnp.bfloat16)
            .at[first_flat, slot_rank]
            .set(spread.reshape(-1, NSUB))
        )
        incoming = lax.all_to_all(
            lax.all_to_all(
                outbox.reshape(fsdp_ctx, tp_size, groups * CAP, NSUB),
                ("fsdp", "ctx"),
                split_axis=0,
                concat_axis=0,
                tiled=True,
            ),
            "tp",
            split_axis=1,
            concat_axis=1,
            tiled=True,
        ).reshape(devices, groups, CAP, NSUB)
        local_table = memory_values[layer_index].reshape(groups, NSUB, model_width)
        pieces = jnp.einsum(
            "sgck,gkd->sgcd", incoming, local_table, preferred_element_type=jnp.float32
        ).astype(jnp.bfloat16)
        returned = lax.all_to_all(
            lax.all_to_all(
                pieces.reshape(fsdp_ctx, tp_size, groups * CAP, model_width),
                ("fsdp", "ctx"),
                split_axis=0,
                concat_axis=0,
                tiled=True,
            ),
            "tp",
            split_axis=1,
            concat_axis=1,
            tiled=True,
        ).reshape(NSUB, CAP, model_width)
        fetched = returned[first_flat, slot_rank].reshape(tokens, pick_count, model_width)
        head_memory = jnp.sum(fetched, axis=1, dtype=jnp.float32)
        memory_cols = lax.psum_scatter(
            head_memory.astype(jnp.bfloat16), "tp", scatter_dimension=1, tiled=True
        ).astype(jnp.float32)
        gate_values = plain_dot(normed_two, full_gate[layer_index])
        gated_rows = (memory_cols * jax.nn.silu(gate_values)).astype(jnp.bfloat16)
        branch = tensor_total(plain_dot(gated_rows, full_memory[layer_index]))
        kept_state.append(
            (
                residual,
                factor_one,
                normed_one,
                queries,
                key_rows,
                value_rows,
                attended,
                log_total,
                middle,
                factor_two,
                normed_two,
                lookups,
                weights,
                first_ids,
                second_ids,
                first_flat,
                slot_rank,
                incoming,
                local_table,
                memory_cols,
                gate_values,
                gated_rows,
            )
        )
        residual = middle + branch
    output = residual.astype(jnp.bfloat16)[None]
    upstream = cotangent[0].astype(jnp.float32)
    pending = []
    table_changes = []
    for layer_index in reversed(range(layer_count)):
        (
            residual,
            factor_one,
            normed_one,
            queries,
            key_rows,
            value_rows,
            attended,
            log_total,
            middle,
            factor_two,
            normed_two,
            lookups,
            weights,
            first_ids,
            second_ids,
            first_flat,
            slot_rank,
            incoming,
            local_table,
            memory_cols,
            gate_values,
            gated_rows,
        ) = kept_state[layer_index]
        out_adjoint = upstream.astype(jnp.bfloat16)
        memory_change = dot_first(gated_rows, out_adjoint)
        gated_adjoint = dot_last(out_adjoint, full_memory[layer_index])
        cols_adjoint = (gated_adjoint * jax.nn.silu(gate_values)).astype(jnp.bfloat16)
        gate_adjoint = (gated_adjoint * memory_cols * silu_slope(gate_values)).astype(jnp.bfloat16)
        gate_change = dot_first(normed_two, gate_adjoint)
        memory_adjoint = lax.all_gather(cols_adjoint, "tp", axis=1, tiled=True)
        pick_count = first_ids.shape[1]
        outbox = (
            jnp.zeros((NSUB, CAP, model_width), jnp.bfloat16)
            .at[first_flat, slot_rank]
            .set(jnp.repeat(memory_adjoint, pick_count, axis=0))
        )
        adjoint_inbox = lax.all_to_all(
            lax.all_to_all(
                outbox.reshape(fsdp_ctx, tp_size, groups * CAP, model_width),
                ("fsdp", "ctx"),
                split_axis=0,
                concat_axis=0,
                tiled=True,
            ),
            "tp",
            split_axis=1,
            concat_axis=1,
            tiled=True,
        ).reshape(devices, groups, CAP, model_width)
        table_changes.insert(
            0,
            jnp.einsum(
                "sgck,sgcd->gkd", incoming, adjoint_inbox, preferred_element_type=jnp.float32
            ).reshape(rows_dev, model_width),
        )
        spread_adjoint = jnp.einsum(
            "sgcd,gkd->sgck", adjoint_inbox, local_table, preferred_element_type=jnp.float32
        )
        returned = (
            lax.all_to_all(
                lax.all_to_all(
                    spread_adjoint.reshape(fsdp_ctx, tp_size, groups * CAP, NSUB).astype(
                        jnp.bfloat16
                    ),
                    ("fsdp", "ctx"),
                    split_axis=0,
                    concat_axis=0,
                    tiled=True,
                ),
                "tp",
                split_axis=1,
                concat_axis=1,
                tiled=True,
            )
            .astype(jnp.float32)
            .reshape(NSUB, CAP, NSUB)
        )
        rows_adjoint = returned[first_flat, slot_rank].reshape(tokens, pick_count, NSUB)
        weight_adjoint = jnp.take_along_axis(rows_adjoint, second_ids, axis=2)
        logit_adjoint = weights * (
            weight_adjoint - jnp.sum(weights * weight_adjoint, axis=(1, 2), keepdims=True)
        )
        first_adjoint = jnp.sum(
            jnp.where(
                first_ids[..., None] == sub_index, jnp.sum(logit_adjoint, axis=2)[..., None], 0.0
            ),
            axis=1,
        ).astype(jnp.bfloat16)
        second_adjoint = jnp.sum(
            jnp.where(second_ids[..., None] == sub_index, logit_adjoint[..., None], 0.0),
            axis=(1, 2),
        ).astype(jnp.bfloat16)
        half_width = lookups.shape[1] // 2
        lookup_adjoint = jnp.concatenate(
            [
                plain_dot(first_adjoint, full_first[layer_index][0]),
                plain_dot(second_adjoint, full_second[layer_index][0]),
            ],
            axis=1,
        ).astype(jnp.bfloat16)
        first_change = dot_first(first_adjoint, lookups[:, :half_width])[None]
        second_change = dot_first(second_adjoint, lookups[:, half_width:])[None]
        lookup_change = dot_first(normed_two, lookup_adjoint)
        normed_two_adjoint = tensor_total(
            dot_last(gate_adjoint, full_gate[layer_index])
            + dot_last(lookup_adjoint, full_lookup[layer_index])
        )
        gain_two = full_gain_two[layer_index].astype(jnp.float32)
        gain_two_change = jnp.sum(normed_two_adjoint * middle * factor_two, axis=0)
        middle_adjoint = upstream + norm_back(middle, factor_two, gain_two, normed_two_adjoint)
        middle_rounded = middle_adjoint.astype(jnp.bfloat16)
        attention_change = dot_first(attended, middle_rounded)
        attended_adjoint = dot_last(middle_rounded, full_attention[layer_index]).astype(
            jnp.bfloat16
        )
        query_adjoint, key_adjoint, value_adjoint = attention_backward(
            queries,
            key_rows,
            value_rows,
            attended_adjoint,
            log_total,
            query_ids,
            key_ids,
            head_count,
            block_rows,
        )
        key_adjoint, value_adjoint = (
            lax.psum_scatter(
                key_adjoint.astype(jnp.bfloat16), "ctx", scatter_dimension=0, tiled=True
            ).astype(jnp.float32),
            lax.psum_scatter(
                value_adjoint.astype(jnp.bfloat16), "ctx", scatter_dimension=0, tiled=True
            ).astype(jnp.float32),
        )
        query_adjoint = query_adjoint.astype(jnp.bfloat16)
        key_adjoint = key_adjoint.astype(jnp.bfloat16)
        value_adjoint = value_adjoint.astype(jnp.bfloat16)
        query_change = dot_first(normed_one, query_adjoint)
        key_change = dot_first(normed_one, key_adjoint)
        value_change = dot_first(normed_one, value_adjoint)
        normed_one_adjoint = tensor_total(
            dot_last(query_adjoint, full_query[layer_index])
            + dot_last(key_adjoint, full_key[layer_index])
            + dot_last(value_adjoint, full_value[layer_index])
        )
        gain_one = full_gain_one[layer_index].astype(jnp.float32)
        gain_one_change = jnp.sum(normed_one_adjoint * residual * factor_one, axis=0)
        upstream = middle_adjoint + norm_back(residual, factor_one, gain_one, normed_one_adjoint)
        layer_parts = (
            query_change[None],
            key_change[None],
            value_change[None],
            attention_change[None],
            lookup_change[None],
            gate_change[None],
            memory_change[None],
            first_change[None],
            second_change[None],
            gain_one_change[None],
            gain_two_change[None],
        )
        pending.insert(0, layer_parts)
    finals = reduce_parts(
        *[
            jnp.concatenate([element[position] for element in pending], axis=0)
            for position in range(11)
        ]
    )
    return (
        output,
        upstream[None],
        finals[0],
        finals[1],
        finals[2],
        finals[3],
        finals[4],
        finals[5],
        finals[6],
        finals[7],
        finals[8],
        finals[9],
        finals[10],
        jnp.stack(table_changes),
    )


def solution(mesh):
    placed = (
        P("fsdp", "ctx", None),
        P(None, "fsdp", "tp"),
        P(None, "fsdp", "tp"),
        P(None, "fsdp", "tp"),
        P(None, "tp", "fsdp"),
        P(None, "fsdp", "tp"),
        P(None, "fsdp", "tp"),
        P(None, "tp", "fsdp"),
        P(None, "tp", "fsdp", None),
        P(None, "tp", "fsdp", None),
        P(None, "fsdp"),
        P(None, "fsdp"),
        P(None, ("fsdp", "ctx", "tp"), None),
        P("fsdp", None),
        P(None, "fsdp", "tp", "ctx", None),
        P(None, "fsdp", "tp", "ctx", None, None),
        P("fsdp", "ctx", None),
    )
    return jax.shard_map(
        body,
        mesh=mesh,
        in_specs=placed,
        out_specs=(
            P("fsdp", "ctx", None),
            P("fsdp", "ctx", None),
            P(None, "fsdp", "tp"),
            P(None, "fsdp", "tp"),
            P(None, "fsdp", "tp"),
            P(None, "tp", "fsdp"),
            P(None, "fsdp", "tp"),
            P(None, "fsdp", "tp"),
            P(None, "tp", "fsdp"),
            P(None, "tp", "fsdp", None),
            P(None, "tp", "fsdp", None),
            P(None, "fsdp"),
            P(None, "fsdp"),
            P(None, ("fsdp", "ctx", "tp"), None),
        ),
        check_vma=False,
    )
```

profile of v0, /device:TPU:0, one launch (start us, length us, event | category | flops | bytes accessed | tf_op | source)
XLA Modules:
  0.0 2155.5 jit_solution(5398438136521241005)
XLA Ops:
  86.1 38.5 %all-reduce.13.cloned.1.call-done = bf16[256,1024]{1,0:T(8,128)(2,1)} async-done(((bf16[256,1024]{1,0:T(8,128)(2,1)}), bf16[256,1024]{1,0:T(8,128)(2,1)}) %all-reduce.13.cloned.1.call-update) | async-done | bytes 524304 | tf_op jit(solution)/shard_map/psum | solution.py:42
  128.3 65.0 %gather_fusion.6 = f32[8192]{0:T(1024)S(1)} fusion(f32[256,256]{1,0:T(8,128)S(1)} %fusion.161, s32[8192]{0:T(1024)S(1)} %reshape.842), kind=kCustom, calls=%fused_computation.2.clone | custom fusion | bytes 131072 | tf_op jit(solution)/shard_map/jit(take_along_axis)/gather | solution.py:325
  271.6 51.2 %all_to_all.81 = bf16[8,4,64,1024]{3,2,1,0:T(8,128)(2,1)S(1)} all-to-all(bf16[8,4,64,1024]{3,2,1,0:T(8,128)(2,1)S(1)} %bitcast.564), channel_id=1, replica_groups=mesh['fsdp'=2,'ctx'=4,'tp'=4] {'fsdp','ctx'}, dimensions={0} | all-to-all | bytes 8388608 | tf_op jit(solution)/shard_map/all_to_all | solution.py:361
  334.5 89.5 %all-to-all-done.3 = bf16[8,4,64,1024]{3,2,0,1:T(8,128)(2,1)} async-done(((bf16[8,4,64,1024]{3,2,0,1:T(8,128)(2,1)}), bf16[8,4,64,1024]{3,2,0,1:T(8,128)(2,1)}, u32[]{:S(2)}, u32[]{:S(2)}) %all-to-all-start.3) | async-done | bytes 4194336 | tf_op jit(solution)/shard_map/all_to_all | solution.py:360
  479.9 37.2 %all-reduce.15.cloned.1.call-done = bf16[256,1024]{1,0:T(8,128)(2,1)} async-done(((bf16[256,1024]{1,0:T(8,128)(2,1)}), bf16[256,1024]{1,0:T(8,128)(2,1)}) %all-reduce.15.cloned.1.call-update) | async-done | bytes 524304 | tf_op jit(solution)/shard_map/psum | solution.py:42
  552.5 37.5 %all-reduce.17.cloned.1.call-done = bf16[256,1024]{1,0:T(8,128)(2,1)} async-done(((bf16[256,1024]{1,0:T(8,128)(2,1)}), bf16[256,1024]{1,0:T(8,128)(2,1)}) %all-reduce.17.cloned.1.call-update) | async-done | bytes 524304 | tf_op jit(solution)/shard_map/psum | solution.py:42
  623.7 52.3 %all_to_all.82 = bf16[8,4,64,1024]{3,2,1,0:T(8,128)(2,1)S(1)} all-to-all(bf16[8,4,64,1024]{3,2,1,0:T(8,128)(2,1)} %bitcast.565), channel_id=1, replica_groups=mesh['fsdp'=2,'ctx'=4,'tp'=4] {'fsdp','ctx'}, dimensions={0} | all-to-all | bytes 8388608 | tf_op jit(solution)/shard_map/all_to_all | solution.py:451
  676.7 97.2 %all_to_all.83 = bf16[8,4,64,1024]{3,2,0,1:T(8,128)(2,1)S(1)} all-to-all(bf16[8,4,64,1024]{3,2,0,1:T(8,128)(2,1)S(1)} %copy.252), channel_id=1, replica_groups=mesh['fsdp'=2,'ctx'=4,'tp'=4] {'tp'}, dimensions={1} | all-to-all | bytes 8388608 | tf_op jit(solution)/shard_map/all_to_all | solution.py:450
  807.1 65.0 %gather_fusion.9 = f32[8192]{0:T(1024)S(1)} fusion(f32[256,256]{1,0:T(8,128)S(1)} %fusion.163, s32[8192]{0:T(1024)S(1)} %reshape.858), kind=kCustom, calls=%fused_computation.6.clone | custom fusion | bytes 131072 | tf_op jit(solution)/shard_map/jit(take_along_axis)/gather | solution.py:325
  889.8 80.1 %gather_fusion.10 = f32[8192]{0:T(1024)S(1)} fusion(f32[256,4,256]{2,1,0:T(4,128)S(1)} %reshape.658, s32[8192]{0:T(1024)S(1)} %reshape.863), kind=kCustom, calls=%fused_computation.3.clone | custom fusion | bytes 163840 | tf_op jit(solution)/shard_map/jit(take_along_axis)/gather | solution.py:492
  1000.0 31.3 %all_to_all.85 = bf16[8,4,64,256]{3,2,0,1:T(8,128)(2,1)S(1)} all-to-all(bf16[8,4,64,256]{3,2,0,1:T(8,128)(2,1)S(1)} %copy.245), channel_id=1, replica_groups=mesh['fsdp'=2,'ctx'=4,'tp'=4] {'tp'}, dimensions={1} | all-to-all | bytes 2097152 | tf_op jit(solution)/shard_map/all_to_all | solution.py:343
  1034.3 51.2 %all_to_all.86 = bf16[8,4,64,1024]{3,2,1,0:T(8,128)(2,1)S(1)} all-to-all(bf16[8,4,64,1024]{3,2,1,0:T(8,128)(2,1)S(1)} %bitcast.566), channel_id=1, replica_groups=mesh['fsdp'=2,'ctx'=4,'tp'=4] {'fsdp','ctx'}, dimensions={0} | all-to-all | bytes 8388608 | tf_op jit(solution)/shard_map/all_to_all | solution.py:361
  1086.2 96.3 %all_to_all.87 = bf16[8,4,64,1024]{3,2,0,1:T(8,128)(2,1)S(1)} all-to-all(bf16[8,4,64,1024]{3,2,0,1:T(8,128)(2,1)S(1)} %copy.249), channel_id=1, replica_groups=mesh['fsdp'=2,'ctx'=4,'tp'=4] {'tp'}, dimensions={1} | all-to-all | bytes 8388608 | tf_op jit(solution)/shard_map/all_to_all | solution.py:360
  1232.2 36.0 %all-reduce.19.cloned.1.call-done = bf16[256,1024]{1,0:T(8,128)(2,1)} async-done(((bf16[256,1024]{1,0:T(8,128)(2,1)}), bf16[256,1024]{1,0:T(8,128)(2,1)}) %all-reduce.19.cloned.1.call-update) | async-done | bytes 524304 | tf_op jit(solution)/shard_map/psum | solution.py:42
  1304.3 26.5 %reduce-scatter.32.cloned.1.call-done = bf16[256,256]{0,1:T(8,128)(2,1)} async-done(((bf16[1024,256]{0,1:T(8,128)(2,1)}), bf16[256,256]{0,1:T(8,128)(2,1)}) %reduce-scatter.32.cloned.1.call-update) | async-done | bytes 131088 | tf_op jit(solution)/shard_map/reduce_scatter | solution.py:544
  1333.0 38.8 %all-reduce.21.cloned.1.call-done = bf16[256,1024]{1,0:T(8,128)(2,1)} async-done(((bf16[256,1024]{1,0:T(8,128)(2,1)}), bf16[256,1024]{1,0:T(8,128)(2,1)}) %all-reduce.21.cloned.1.call-update) | async-done | bytes 524304 | tf_op jit(solution)/shard_map/psum | solution.py:42
  1404.6 52.3 %all_to_all.88 = bf16[8,4,64,1024]{3,2,1,0:T(8,128)(2,1)S(1)} all-to-all(bf16[8,4,64,1024]{3,2,1,0:T(8,128)(2,1)} %bitcast.563), channel_id=1, replica_groups=mesh['fsdp'=2,'ctx'=4,'tp'=4] {'fsdp','ctx'}, dimensions={0} | all-to-all | bytes 8388608 | tf_op jit(solution)/shard_map/all_to_all | solution.py:451
  1457.6 97.0 %all_to_all.89 = bf16[8,4,64,1024]{3,2,0,1:T(8,128)(2,1)S(1)} all-to-all(bf16[8,4,64,1024]{3,2,0,1:T(8,128)(2,1)S(1)} %copy.262), channel_id=1, replica_groups=mesh['fsdp'=2,'ctx'=4,'tp'=4] {'tp'}, dimensions={1} | all-to-all | bytes 8388608 | tf_op jit(solution)/shard_map/all_to_all | solution.py:450
  1613.7 80.1 %gather_fusion.11 = f32[8192]{0:T(1024)S(1)} fusion(f32[256,4,256]{2,1,0:T(4,128)S(1)} %reshape.665, s32[8192]{0:T(1024)S(1)} %reshape.868), kind=kCustom, calls=%fused_computation.7.clone | custom fusion | bytes 163840 | tf_op jit(solution)/shard_map/jit(take_along_axis)/gather | solution.py:492
  1708.6 35.2 %all-reduce.23.cloned.1.call-done = bf16[256,1024]{1,0:T(8,128)(2,1)} async-done(((bf16[256,1024]{1,0:T(8,128)(2,1)}), bf16[256,1024]{1,0:T(8,128)(2,1)}) %all-reduce.23.cloned.1.call-update) | async-done | bytes 524304 | tf_op jit(solution)/shard_map/psum | solution.py:42
  1780.0 26.5 %reduce-scatter.36.cloned.1.call-done = bf16[256,256]{0,1:T(8,128)(2,1)} async-done(((bf16[1024,256]{0,1:T(8,128)(2,1)}), bf16[256,256]{0,1:T(8,128)(2,1)}) %reduce-scatter.36.cloned.1.call-update) | async-done | bytes 131088 | tf_op jit(solution)/shard_map/reduce_scatter | solution.py:544
  1820.0 41.7 %all-reduce.25.cloned.1.call-done = (bf16[256,1024]{1,0:T(8,128)(2,1)}, bf16[256,1024]{1,0:T(8,128)(2,1)}) async-done(((bf16[256,1024]{1,0:T(8,128)(2,1)}, bf16[256,1024]{1,0:T(8,128)(2,1)}), (bf16[256,1024]{1,0:T(8,128)(2,1)}, bf16[256,1024]{1,0:T(8,128)(2,1)})) %all-reduce.25.cloned.1.call-update) | async-done | bytes 1048592 | tf_op jit(solution)/shard_map/psum | solution.py:42
  2006.3 32.7 %all-reduce.27.cloned.1.call-done = (bf16[2,1,128,64]{2,3,1,0:T(8,128)(2,1)}, bf16[2,1,128,64]{2,3,1,0:T(8,128)(2,1)}, bf16[2,512]{1,0:T(2,128)(2,1)}, bf16[2,512]{1,0:T(2,128)(2,1)}) async-done(((bf16[2,1,128,64]{2,3,1,0:T(8,128)(2,1)}, bf16[2,1,128,64]{2,3,1,0:T(8,128)(2,1)}, bf16[2,512]{1,0:T(2,128)(2,1)}, bf16[2,512]{1,0:T(2,128)(2,1)}), (bf16[2,1,128,64]{2,3,1,0:T(8,128)(2,1)}, ...) | async-done | bytes 69648 | tf_op jit(solution)/shard_map/psum | solution.py:232
  2044.3 93.7 %all-reduce.29.cloned.1.call-done = (bf16[2,512,256]{2,1,0:T(8,128)(2,1)}, bf16[2,512,256]{2,1,0:T(8,128)(2,1)}, bf16[2,512,256]{2,1,0:T(8,128)(2,1)}, bf16[2,25...) async-done(((bf16[2,512,256]{2,1,0:T(8,128)(2,1)}, bf16[2,512,256]{2,1,0:T(8,128)(2,1)}, ...) | async-done | bytes 3407888 | tf_op jit(solution)/shard_map/psum | solution.py:225
  (756 shorter events, 785.3 us)
Async XLA Ops:
  12.6 71.2 %all-gather.13.cloned.1.call-start = ((), (), s32[]{:S(2)}) async-start(), calls=%async_computation.36 | async-start | bytes 1572864 | tf_op jit(solution)/shard_map/all_gather | solution.py:285
  13.5 111.1 %all-reduce.13.cloned.1.call-start = ((), (), s32[]{:S(2)}) async-start(), calls=%async_computation.37 | async-start | bytes 1048576 | tf_op jit(solution)/shard_map/psum | solution.py:42
  325.3 98.7 %all-to-all-start.3 = ((bf16[8,4,64,1024]{3,2,0,1:T(8,128)(2,1)}), bf16[8,4,64,1024]{3,2,0,1:T(8,128)(2,1)}, u32[]{:S(2)}, u32[]{:S(2)}) async-start(bf16[8,4,64,1024]{3,2,0,1:T(8,128)(2,1)} %copy.232), calls=%async_computation.3 | async-start | bytes 8388608 | tf_op jit(solution)/shard_map/all_to_all | solution.py:360
  330.1 128.3 %all-gather.15.cloned.1.call-start = ((), (), s32[]{:S(2)}) async-start(), calls=%async_computation.39 | async-start | bytes 1572864 | tf_op jit(solution)/shard_map/all_gather | solution.py:287
  332.2 127.5 %all-gather.17.cloned.1.call-start = ((), (), s32[]{:S(2)}) async-start(), calls=%async_computation.40 | async-start | bytes 1572864 | tf_op jit(solution)/shard_map/all_gather | solution.py:288
  334.4 143.1 %reduce-scatter.26.cloned.1.call-start = ((), (), s32[]{:S(2)}) async-start(), calls=%async_computation.38 | async-start | bytes 655360 | tf_op jit(solution)/shard_map/reduce_scatter | solution.py:375
  479.8 110.3 %all-reduce.17.cloned.1.call-start = ((), (), s32[]{:S(2)}) async-start(), calls=%async_computation.42 | async-start | bytes 1048576 | tf_op jit(solution)/shard_map/psum | solution.py:42
  799.5 83.5 %all-to-all-start.11 = ((bf16[8,4,64,256]{3,2,0,1:T(8,128)(2,1)}), bf16[8,4,64,256]{3,2,0,1:T(8,128)(2,1)}, u32[]{:S(2)}, u32[]{:S(2)}) async-start(bf16[8,4,64,256]{3,2,0,1:T(8,128)(2,1)} %copy.256), calls=%async_computation.13 | async-start | bytes 2097152 | tf_op jit(solution)/shard_map/all_to_all | solution.py:473
  803.8 423.4 %reduce-scatter.28.cloned.1.call-start = ((), (), s32[]{:S(2)}) async-start(), calls=%async_computation.43 | async-start | bytes 655360 | tf_op jit(solution)/shard_map/reduce_scatter | solution.py:375
  1231.5 71.0 %reduce-scatter.30.cloned.1.call-start = ((), (), s32[]{:S(2)}) async-start(), calls=%async_computation.45 | async-start | bytes 655360 | tf_op jit(solution)/shard_map/reduce_scatter | solution.py:541
  1281.8 90.0 %all-reduce.21.cloned.1.call-start = ((), (), s32[]{:S(2)}) async-start(), calls=%async_computation.47 | async-start | bytes 1048576 | tf_op jit(solution)/shard_map/psum | solution.py:42
  1581.9 161.9 %all-reduce.23.cloned.1.call-start = ((), (), s32[]{:S(2)}) async-start(), calls=%async_computation.48 | async-start | bytes 1048576 | tf_op jit(solution)/shard_map/psum | solution.py:42
  1757.5 104.2 %all-reduce.25.cloned.1.call-start = ((), (), s32[]{:S(2)}) async-start(), calls=%async_computation.62 | async-start | bytes 2097152 | tf_op jit(solution)/shard_map/psum | solution.py:42
  1808.7 74.0 %reduce-scatter.52.cloned.1.call-start = ((), (), s32[]{:S(2)}) async-start(), calls=%async_computation.58 | async-start | bytes 98304
  1813.8 70.5 %reduce-scatter.54.cloned.1.call-start = ((), (), s32[]{:S(2)}) async-start(), calls=%async_computation.59 | async-start | bytes 98304
  1815.5 78.9 %reduce-scatter.58.cloned.1.call-start = ((), (), s32[]{:S(2)}) async-start(), calls=%async_computation.61 | async-start | bytes 393216
  1819.9 86.2 %reduce-scatter.56.cloned.1.call-start = ((), (), s32[]{:S(2)}) async-start(), calls=%async_computation.60 | async-start | bytes 393216
  1870.7 72.3 %reduce-scatter.46.cloned.1.call-start = ((), (), s32[]{:S(2)}) async-start(), calls=%async_computation.55 | async-start | bytes 786432 | tf_op jit(solution)/shard_map/reduce_scatter | solution.py:202
  1874.0 81.5 %reduce-scatter.38.cloned.1.call-start = ((), (), s32[]{:S(2)}) async-start(), calls=%async_computation.51 | async-start | bytes 1572864 | tf_op jit(solution)/shard_map/reduce_scatter | solution.py:190
  1876.9 91.2 %reduce-scatter.44.cloned.1.call-start = ((), (), s32[]{:S(2)}) async-start(), calls=%async_computation.54 | async-start | bytes 1572864 | tf_op jit(solution)/shard_map/reduce_scatter | solution.py:199
  1878.7 102.0 %reduce-scatter.40.cloned.1.call-start = ((), (), s32[]{:S(2)}) async-start(), calls=%async_computation.52 | async-start | bytes 1572864 | tf_op jit(solution)/shard_map/reduce_scatter | solution.py:193
  1880.7 112.5 %reduce-scatter.42.cloned.1.call-start = ((), (), s32[]{:S(2)}) async-start(), calls=%async_computation.53 | async-start | bytes 1572864 | tf_op jit(solution)/shard_map/reduce_scatter | solution.py:196
  1882.6 156.4 %all-reduce.27.cloned.1.call-start = ((), (), s32[]{:S(2)}) async-start(), calls=%async_computation.63 | async-start | bytes 139264 | tf_op jit(solution)/shard_map/psum | solution.py:232
  1907.7 230.3 %all-reduce.29.cloned.1.call-start = ((), (), s32[]{:S(2)}) async-start(), calls=%async_computation.64 | async-start | bytes 6815744 | tf_op jit(solution)/shard_map/psum | solution.py:225
  (189 other events, 10867.7 us)
Sparse Core Ops, SparseCore 0:
  10.2 11.7 all-gather.6
  24.1 10.1 all-gather.10
  36.4 10.5 all-gather.8
  49.0 9.8 all-gather.12
  86.1 38.4 all-reduce.12
  343.8 10.1 all-gather.16
  458.4 19.0 reduce-scatter.25
  480.5 36.5 all-reduce.14
  552.6 37.3 all-reduce.16
  1208.0 19.0 reduce-scatter.27
  1231.6 36.5 all-reduce.18
  1277.6 24.7 reduce-scatter.29
  1305.9 24.7 reduce-scatter.31
  1333.5 38.2 all-reduce.20
  1708.0 35.7 all-reduce.22
  1753.3 24.7 reduce-scatter.33
  1781.6 24.7 reduce-scatter.35
  1809.4 52.1 all-reduce.24
  1921.4 9.6 reduce-scatter.49
  1945.7 9.6 reduce-scatter.37
  1958.4 9.6 reduce-scatter.43
  1970.9 9.6 reduce-scatter.39
  1996.9 42.0 all-reduce.26
  2043.4 94.5 all-reduce.28
  (8 shorter events, 70.0 us)
where the time goes:
time: 2170 us; the launch traced here: 2160 us
  waiting for transfers between devices  757 us (35%)
  blocking collectives  669 us (31%)
  local copies, waits for them, and re-layouts  486 us (22%)
  other arithmetic  104 us (5%)
  matrix products  98.5 us (5%)
  starting transfers between devices  23.2 us (1%)
    psum x7, waiting for transfers between devices, tensor_total(): return lax.psum(partial_sum.astype(jnp.bfloat16), 'tp').astype(jnp.float32)  265 us
    all_to_all x3, blocking collectives, body(): lax.all_to_all(lax.all_to_all(outbox.reshape(fsdp_ctx, tp_size, groups *...  225 us
    gather x10, local copies, waits for them, and re-layouts, body(): weight_adjoint = jnp.take_along_axis(rows_adjoint, second_ids, axis=2)  163 us
    gather x10, local copies, waits for them, and re-layouts, body(): jnp.take_along_axis(score_second, second_ids.reshape(tokens, pick_count *...  131 us
    all_to_all x2, blocking collectives, body(): lax.all_to_all(outbox.reshape(fsdp_ctx, tp_size, groups * CAP, model_widt...  105 us
    all_to_all x2, blocking collectives, body(): lax.all_to_all(pieces.reshape(fsdp_ctx, tp_size, groups * CAP, model_widt...  102 us
    all_to_all x1, blocking collectives, body(): lax.all_to_all(lax.all_to_all(pieces.reshape(fsdp_ctx, tp_size, groups *...  96.3 us
    psum x1, waiting for transfers between devices, reduce_parts(): lax.psum(query_share.astype(jnp.bfloat16), 'ctx').astype(jnp.float32)  93.7 us
  transfers between devices with their start and end apart: 37, of which 28 were waited for; matrix products, arithmetic and copies ran while one was open for 12% of the time, Pallas kernels for 0%

commit v1 on v0

v1 whole, which is shorter than its diff:
```python
import functools

import jax
import jax.numpy as jnp
from jax import lax
from jax.experimental import pallas as pl
from jax.experimental.pallas import tpu as pltpu
from jax.sharding import PartitionSpec as P

HD = 64
NSUB = 256
CAP = 8
EPS = 1e-05
NEG = -1e30
f32 = jnp.float32
bf16 = jnp.bfloat16
MIB = 1 << 20


def dot(a, b):
    return jnp.dot(a, b, preferred_element_type=f32)


def dot_nt(a, b):
    return lax.dot_general(a, b, (((1,), (1,)), ((), ())), preferred_element_type=f32)


def dot_tn(a, b):
    return lax.dot_general(a, b, (((0,), (0,)), ((), ())), preferred_element_type=f32)


def swap(x, axis, step):
    size = lax.axis_size(axis)
    return lax.ppermute(x, axis, [(i, i ^ step) for i in range(size)])


def swaps(xs, axis):
    return [xs[0]] + [swap(xs[d], axis, d) for d in range(1, len(xs))]


def spread(x, axis):
    return [x] + [swap(x, axis, d) for d in range(1, lax.axis_size(axis))]


def shape(dims, dtype):
    return jax.ShapeDtypeStruct(dims, dtype)


def kernel_call(body, name, outs, idx, args, scratch=(), limit=32, flops=0):
    in_specs = [pl.BlockSpec(memory_space=pltpu.SMEM)]
    in_specs += [pl.BlockSpec(memory_space=pltpu.VMEM) for _ in args]
    moved = sum(a.size * a.dtype.itemsize for a in args)
    moved += sum(o.size * o.dtype.itemsize for o in outs)
    return pl.pallas_call(
        body,
        out_shape=outs,
        in_specs=in_specs,
        out_specs=[pl.BlockSpec(memory_space=pltpu.VMEM) for _ in outs],
        scratch_shapes=list(scratch),
        compiler_params=pltpu.CompilerParams(vmem_limit_bytes=limit * MIB),
        cost_estimate=pl.CostEstimate(flops=flops, bytes_accessed=moved, transcendentals=0),
        name=name,
    )(idx, *args)


def rows_at(index, count):
    return pl.ds(pl.multiple_of(index * count, count), count)


def rms(x, gain):
    factor = lax.rsqrt(jnp.mean(x * x, axis=1, keepdims=True) + EPS)
    return factor, x * factor * gain


def rms_back(x, factor, gain, upstream):
    scaled = upstream * gain
    return factor * scaled - x * factor**3 * jnp.mean(scaled * x, axis=1, keepdims=True)


def total4(refs):
    return (refs[0][...].astype(f32) + refs[1][...].astype(f32)) + (
        refs[2][...].astype(f32) + refs[3][...].astype(f32)
    )


def fold(x):
    half = x.shape[0] // 2
    return jnp.concatenate([x[:half], x[half:]], axis=1)


def unfold(x):
    half = x.shape[1] // 2
    return jnp.concatenate([x[:, :half], x[:, half:]], axis=0)


class Plan:
    def __init__(self, SA, TA):
        self.SA, self.TA = SA, TA
        self.si = 1 if SA == "ctx" else 2
        self.ti = 1 if TA == "ctx" else 2

    def src(self, sa, ta):
        return sa * 4 + ta if self.SA == "ctx" else ta * 4 + sa

    def rel(self, ds, dt):
        return (ds, dt) if self.SA == "ctx" else (dt, ds)


PLAN = Plan("ctx", "tp")


def slots_kernel(idx, first_ref, second_ref, slot_ref, out_ref, gbits, dbits):
    tokens = first_ref.shape[1]
    picks = first_ref.shape[0]
    lanes = out_ref.shape[0] * out_ref.shape[2]
    iota = lax.broadcasted_iota(jnp.int32, (NSUB, tokens), 0)
    onehot = jnp.zeros((NSUB, tokens), f32)
    for i in range(picks):
        onehot = jnp.where(iota == first_ref[i : i + 1, :], 1.0, onehot)
    before = lax.broadcasted_iota(jnp.int32, (tokens, tokens), 0) < lax.broadcasted_iota(
        jnp.int32, (tokens, tokens), 1
    )
    counts = dot(onehot.astype(bf16), jnp.where(before, 1.0, 0.0).astype(bf16))
    row = lax.broadcasted_iota(jnp.int32, (lanes, tokens), 0)
    token_row = (lax.broadcasted_iota(jnp.int32, (8, tokens), 1) + 1).astype(f32)
    token_row = jnp.where(
        lax.broadcasted_iota(jnp.int32, (8, tokens), 0) == 0, token_row, 0.0
    )
    total = jnp.zeros((16, lanes), f32)
    for i in range(picks):
        first = first_ref[i : i + 1, :]
        rank = jnp.sum(jnp.where(iota == first, counts, 0.0), axis=0, keepdims=True)
        shard = lax.shift_right_logical(first, gbits)
        group = lax.shift_right_logical(shard, dbits) * (1 << gbits) + (first & ((1 << gbits) - 1))
        slot = (shard & ((1 << dbits) - 1)) * out_ref.shape[2] + group * CAP + rank.astype(jnp.int32)
        slot_ref[i : i + 1, :] = slot
        names = jnp.concatenate([second_ref[8 * i : 8 * i + 8, :].astype(f32), token_row], axis=0)
        hit = jnp.where(row == slot, 1.0, 0.0).astype(bf16)
        total = total + dot_nt(names.astype(bf16), hit)
    for d in range(out_ref.shape[0]):
        out_ref[d] = total[:, d * out_ref.shape[2] : (d + 1) * out_ref.shape[2]].astype(bf16)


def emit_heads(h, w_ref, pack, outs, s):
    width = w_ref.shape[1] // 3
    qkv = dot(h, w_ref[...]).astype(bf16)
    for j in range(4):
        q = qkv[:, HD * j : HD * (j + 1)]
        k = qkv[:, width + HD * j : width + HD * (j + 1)]
        v = qkv[:, 2 * width + HD * j : 2 * width + HD * (j + 1)]
        pack[j] = jnp.concatenate([jnp.concatenate([q, k], axis=1), fold(v)], axis=0)
    for d in range(4):
        outs[d][...] = pack[s ^ d]


def qkv_first_kernel(idx, x_ref, gain_ref, w_ref, h_ref, e0, e1, e2, e3, pack, plan, row):
    _, normed = rms(x_ref[...].astype(f32), gain_ref[row : row + 1, :])
    h = normed.astype(bf16)
    h_ref[...] = h
    emit_heads(h, w_ref, pack, (e0, e1, e2, e3), idx[plan.si])


def place_chunks(refs, full, t):
    count = refs[0].shape[0]
    for d in range(4):
        full[rows_at(t ^ d, count), :] = refs[d][...]


def qkv_kernel(idx, h0, h1, h2, h3, w_ref, h_ref, e0, e1, e2, e3, pack, plan):
    place_chunks((h0, h1, h2, h3), h_ref, idx[plan.ti])
    emit_heads(h_ref[...], w_ref, pack, (e0, e1, e2, e3), idx[plan.si])


def load_heads(es, kk, vv):
    for d in range(4):
        rows = es[d].shape[0] * 2 // 3
        kk[rows * d : rows * (d + 1), :] = es[d][0:rows, HD : 2 * HD]
        vv[rows * d : rows * (d + 1), :] = unfold(es[d][rows:, :])


def load_ids(col_ref, ids_col, s):
    count = col_ref.shape[0] // 4
    for d in range(4):
        ids_col[count * d : count * (d + 1), :] = col_ref[rows_at(s ^ d, count), :]


def probabilities(kk, q, key_ids, query_ids):
    scores = dot_nt(kk, q) * (HD ** (-0.5))
    scores = jnp.where(key_ids <= query_ids, scores, NEG)
    top = jnp.max(scores, axis=0, keepdims=True)
    exponent = jnp.exp(scores - top)
    return exponent * (1.0 / jnp.sum(exponent, axis=0, keepdims=True))


def attend_kernel(idx, e0, e1, e2, e3, row_ref, col_ref, a0, a1, a2, a3, kk, vv, ids_col, plan):
    es, outs = (e0, e1, e2, e3), (a0, a1, a2, a3)
    s = idx[plan.si]
    load_heads(es, kk, vv)
    load_ids(col_ref, ids_col, s)
    count = kk.shape[0] // 4
    for d in range(4):
        query_ids = row_ref[:, rows_at(s ^ d, count)]
        p = probabilities(kk[...], es[d][0:count, 0:HD], ids_col[...], query_ids)
        blended = dot_tn(vv[...], p.astype(bf16))
        outs[d][...] = fold(blended.T.astype(bf16))


def attend_back_kernel(
    idx, e0, e1, e2, e3, u0, u1, u2, u3, row_ref, col_ref, g0, g1, g2, g3, kk, vv, ids_col, gk, gv, plan
):
    es, us, outs = (e0, e1, e2, e3), (u0, u1, u2, u3), (g0, g1, g2, g3)
    s = idx[plan.si]
    load_heads(es, kk, vv)
    load_ids(col_ref, ids_col, s)
    count = kk.shape[0] // 4
    scale = HD ** (-0.5)
    for d in range(4):
        query_ids = row_ref[:, rows_at(s ^ d, count)]
        q = es[d][0:count, 0:HD]
        up = unfold(us[d][...])
        p = probabilities(kk[...], q, ids_col[...], query_ids)
        gp = dot_nt(vv[...], up)
        centre = jnp.sum(p * gp, axis=0, keepdims=True)
        gs = (p * (gp - centre)).astype(bf16)
        gq = (dot_tn(kk[...], gs) * scale).T.astype(bf16)
        outs[d][0:count, 0:HD] = gq
        key_term = dot(gs, q)
        value_term = dot(p.astype(bf16), up)
        if d == 0:
            gk[...] = key_term
            gv[...] = value_term
        else:
            gk[...] += key_term
            gv[...] += value_term
    for d in range(4):
        outs[d][0:count, HD : 2 * HD] = (gk[count * d : count * (d + 1), :] * scale).astype(bf16)
        outs[d][count:, :] = fold(gv[count * d : count * (d + 1), :].astype(bf16))


def out_kernel(idx, a0, a1, a2, a3, w_ref, a_ref, p0, p1, p2, p3, heads, part, plan):
    s, t = idx[plan.si], idx[plan.ti]
    for d, a in enumerate((a0, a1, a2, a3)):
        heads[s ^ d] = unfold(a[...])
    a_ref[...] = jnp.concatenate([heads[j] for j in range(4)], axis=1)
    part[...] = dot(a_ref[...], w_ref[...]).astype(bf16)
    emit_chunks(part, (p0, p1, p2, p3), t)


def emit_chunks(part, outs, t):
    count = outs[0].shape[0]
    for d in range(4):
        outs[d][...] = part[rows_at(t ^ d, count), :]


def own_rows(ref, idx, plan, count):
    if ref.shape[0] == count:
        return ref[...].astype(f32)
    return ref[rows_at(idx[plan.ti], count), :].astype(f32)


def norm_kernel(idx, x_ref, p0, r1, r2, r3, gain_ref, x_out, h_out, plan, row):
    x = own_rows(x_ref, idx, plan, p0.shape[0]) + total4((p0, r1, r2, r3))
    x_out[...] = x
    _, normed = rms(x, gain_ref[row : row + 1, :])
    h_out[...] = normed.astype(bf16)


def last_kernel(idx, x_ref, p0, r1, r2, r3, out_ref, plan):
    x = own_rows(x_ref, idx, plan, p0.shape[0]) + total4((p0, r1, r2, r3))
    out_ref[...] = x.astype(bf16)


def norm_back_kernel(idx, p0, r1, r2, r3, x_ref, g_ref, gain_ref, gx_ref, round_ref, dgain_ref, plan, row):
    count = p0.shape[0]
    upstream = total4((p0, r1, r2, r3))
    x = own_rows(x_ref, idx, plan, count)
    gain = gain_ref[row : row + 1, :]
    factor, _ = rms(x, gain)
    dgain_ref[...] = jnp.sum(upstream * x * factor, axis=0, keepdims=True)
    gx = own_rows(g_ref, idx, plan, count) + rms_back(x, factor, gain, upstream)
    gx_ref[...] = gx
    round_ref[...] = gx.astype(bf16)


def lookup_kernel(
    idx, h0, h1, h2, h3, wm_ref, ka_ref, kb_ref, first_ref, second_ref, slot_ref, h_ref, u_ref, w_ref, out_ref, plan
):
    place_chunks((h0, h1, h2, h3), h_ref, idx[plan.ti])
    u = dot(h_ref[...], wm_ref[...]).astype(bf16)
    u_ref[...] = u
    half = u.shape[1] // 2
    c1 = dot_nt(ka_ref[...], u[:, :half])
    c2 = dot_nt(kb_ref[...], u[:, half:])
    tokens = u.shape[0]
    picks = first_ref.shape[0]
    inner = second_ref.shape[0] // picks
    iota = lax.broadcasted_iota(jnp.int32, (NSUB, tokens), 0)
    for i in range(picks):
        base = jnp.sum(jnp.where(iota == first_ref[i : i + 1, :], c1, 0.0), axis=0, keepdims=True)
        for b in range(inner):
            r = i * inner + b
            picked = jnp.sum(
                jnp.where(iota == second_ref[r : r + 1, :], c2, 0.0), axis=0, keepdims=True
            )
            w_ref[r : r + 1, :] = base + picked
    logits = w_ref[...]
    exponent = jnp.exp(logits - jnp.max(logits, axis=0, keepdims=True))
    w = exponent * (1.0 / jnp.sum(exponent, axis=0, keepdims=True))
    w_ref[...] = w
    lanes = out_ref.shape[0] * out_ref.shape[2]
    row = lax.broadcasted_iota(jnp.int32, (lanes, tokens), 0)
    total = jnp.zeros((inner, lanes), f32)
    for i in range(picks):
        hit = jnp.where(row == slot_ref[i : i + 1, :], 1.0, 0.0).astype(bf16)
        total = total + dot_nt(w[inner * i : inner * (i + 1), :].astype(bf16), hit)
    for d in range(out_ref.shape[0]):
        out_ref[d] = total[:, d * out_ref.shape[2] : (d + 1) * out_ref.shape[2]]


def gate_kernel(idx, m0, m1, m2, m3, z1, z2, z3, gate_ref, w_ref, mem_ref, z_ref, p0, p1, p2, p3, part, plan):
    mem = total4((m0, m1, m2, m3)) + z1[...].astype(f32) + z2[...].astype(f32) + z3[...].astype(f32)
    mem_ref[...] = mem
    gate = gate_ref[...]
    z = (mem * (gate * jax.nn.sigmoid(gate))).astype(bf16)
    z_ref[...] = z
    part[...] = dot(z, w_ref[...]).astype(bf16)
    emit_chunks(part, (p0, p1, p2, p3), idx[plan.ti])


def gate_back(gy, w_ref, gate_ref, mem_ref, gn_ref, gg_ref):
    gz = dot_nt(gy, w_ref[...])
    gate = gate_ref[...]
    sigmoid = jax.nn.sigmoid(gate)
    gn_ref[...] = (gz * (gate * sigmoid)).astype(bf16)
    gg_ref[...] = (gz * mem_ref[...] * (sigmoid * (1.0 + gate * (1.0 - sigmoid)))).astype(bf16)


def gate_back_full_kernel(idx, gy_ref, w_ref, gate_ref, mem_ref, gn_ref, gg_ref):
    gate_back(gy_ref[...], w_ref, gate_ref, mem_ref, gn_ref, gg_ref)


def gate_back_kernel(idx, g0, g1, g2, g3, w_ref, gate_ref, mem_ref, gy_ref, gn_ref, gg_ref, plan):
    place_chunks((g0, g1, g2, g3), gy_ref, idx[plan.ti])
    gate_back(gy_ref[...], w_ref, gate_ref, mem_ref, gn_ref, gg_ref)


def lookup_back_kernel(
    idx, gw_ref, slot_ref, w_ref, first_ref, second_ref, ka_ref, kb_ref, u_ref, gg_ref, wg_ref, wm_ref,
    p0, p1, p2, p3, gu_ref, dka_ref, dkb_ref, gl, part, plan,
):
    tokens = u_ref.shape[0]
    picks = first_ref.shape[0]
    inner = second_ref.shape[0] // picks
    owners, _, width = gw_ref.shape
    row = lax.broadcasted_iota(jnp.int32, (owners * width, tokens), 0)
    arrived = jnp.concatenate([gw_ref[d] for d in range(owners)], axis=1).astype(bf16)
    for i in range(picks):
        hit = jnp.where(row == slot_ref[i : i + 1, :], 1.0, 0.0).astype(bf16)
        gl[inner * i : inner * (i + 1), :] = dot(arrived, hit)
    w = w_ref[...]
    gw = gl[...]
    gl[...] = w * (gw - jnp.sum(w * gw, axis=0, keepdims=True))
    iota = lax.broadcasted_iota(jnp.int32, (NSUB, tokens), 0)
    gc1 = jnp.zeros((NSUB, tokens), f32)
    gc2 = jnp.zeros((NSUB, tokens), f32)
    for i in range(picks):
        both = jnp.sum(gl[inner * i : inner * (i + 1), :], axis=0, keepdims=True)
        gc1 = jnp.where(iota == first_ref[i : i + 1, :], both, gc1)
        for b in range(inner):
            r = i * inner + b
            gc2 = gc2 + jnp.where(iota == second_ref[r : r + 1, :], gl[r : r + 1, :], 0.0)
    gc1 = gc1.astype(bf16)
    gc2 = gc2.astype(bf16)
    half = u_ref.shape[1] // 2
    gu = jnp.concatenate([dot_tn(gc1, ka_ref[...]), dot_tn(gc2, kb_ref[...])], axis=1).astype(bf16)
    gu_ref[...] = gu
    dka_ref[...] = dot(gc1, u_ref[:, :half]).astype(bf16)
    dkb_ref[...] = dot(gc2, u_ref[:, half:]).astype(bf16)
    part[...] = (dot_nt(gg_ref[...], wg_ref[...]) + dot_nt(gu, wm_ref[...])).astype(bf16)
    emit_chunks(part, (p0, p1, p2, p3), idx[plan.ti])


def read_kernel(idx, w_ref, names_ref, v_ref, o0, o1, o2, o3, s_ref, pieces, rows, plan):
    step = pl.program_id(0)
    sources, _, width = w_ref.shape

    @pl.when(step == 0)
    def _():
        iota = lax.broadcasted_iota(jnp.int32, (NSUB, width), 0).astype(f32)

        def build(src, carry):
            names = names_ref[src].astype(f32)
            weights = w_ref[src]
            dense = jnp.zeros((NSUB, width), f32)
            for b in range(8):
                dense = jnp.where(iota == names[b : b + 1, :], weights[b : b + 1, :], dense)
            s_ref[src] = dense.T
            return carry

        lax.fori_loop(0, sources, build, 0)

    at = rows_at(step, CAP)
    left = s_ref[:, at, :].reshape(sources * CAP, NSUB).astype(bf16)
    pieces[:, at, :] = dot(left, v_ref[...]).reshape(sources, CAP, v_ref.shape[1])

    @pl.when(step == pl.num_programs(0) - 1)
    def _():
        s, t = idx[plan.si], idx[plan.ti]
        tokens = rows.shape[0]
        quarter = o0.shape[1]
        outs = (o0, o1, o2, o3)
        iota = (lax.broadcasted_iota(jnp.int32, (tokens, width), 0) + 1).astype(f32)
        for ds in range(4):
            hits, parts = [], []
            for ta in range(4):
                src = plan.src(s ^ ds, ta)
                token = names_ref[src].astype(f32)[8:9, :]
                hits.append(jnp.where(iota == token, 1.0, 0.0).astype(bf16))
                parts.append(pieces[src].astype(bf16))
            rows[...] = dot(
                jnp.concatenate(hits, axis=1), jnp.concatenate(parts, axis=0)
            ).astype(bf16)
            for dt in range(4):
                dp, dz = plan.rel(ds, dt)
                outs[dp][tokens * dz : tokens * (dz + 1), :] = rows[:, rows_at(t ^ dt, quarter)]


def read_call(idx, weights, names, layer, values, plan, tokens):
    sources, inner, width = weights.shape
    steps = width // CAP
    d_model = values.shape[2]
    quarter = d_model // 4
    out = shape((4 * tokens, quarter), bf16)
    return pl.pallas_call(
        functools.partial(read_kernel, plan=plan),
        grid=(steps,),
        out_shape=[out, out, out, out, shape((sources, width, NSUB), f32)],
        in_specs=[
            pl.BlockSpec(memory_space=pltpu.SMEM),
            pl.BlockSpec((sources, inner, width), lambda g: (0, 0, 0)),
            pl.BlockSpec((sources, 16, width), lambda g: (0, layer, 0)),
            pl.BlockSpec((None, NSUB, d_model), lambda g: (layer, g, 0)),
        ],
        out_specs=[pl.BlockSpec((4 * tokens, quarter), lambda g: (0, 0)) for _ in range(4)]
        + [pl.BlockSpec((sources, width, NSUB), lambda g: (0, 0, 0))],
        scratch_shapes=[
            pltpu.VMEM((sources, width, d_model), f32),
            pltpu.VMEM((tokens, d_model), bf16),
        ],
        compiler_params=pltpu.CompilerParams(vmem_limit_bytes=48 * MIB),
        cost_estimate=pl.CostEstimate(
            flops=4 * sources * width * NSUB * d_model, bytes_accessed=20 * MIB, transcendentals=0
        ),
        name="memory_read",
    )(idx, weights, names, values)


def write_kernel(
    idx, g0, g1, g2, g3, names_ref, s_ref, v_ref, dv_ref, gw_ref, grads, pieces, cross, plan
):
    step = pl.program_id(0)
    sources, width, _ = s_ref.shape
    d_model = v_ref.shape[1]

    @pl.when(step == 0)
    def _():
        s, t = idx[plan.si], idx[plan.ti]
        tokens = grads.shape[1]
        quarter = g0.shape[1]
        for dp, g in enumerate((g0, g1, g2, g3)):
            for dz in range(4):
                ds, dt = plan.rel(dp, dz)
                grads[s ^ ds, :, rows_at(t ^ dt, quarter)] = g[tokens * dz : tokens * (dz + 1), :]
        iota = (lax.broadcasted_iota(jnp.int32, (tokens, width), 0) + 1).astype(f32)
        for sa in range(4):
            for ta in range(4):
                src = plan.src(sa, ta)
                token = names_ref[src].astype(f32)[8:9, :]
                hit = jnp.where(iota == token, 1.0, 0.0).astype(bf16)
                pieces[src] = dot_tn(hit, grads[sa])

    at = rows_at(step, CAP)
    inbox = pieces[:, at, :].reshape(sources * CAP, d_model).astype(bf16)
    left = s_ref[:, at, :].reshape(sources * CAP, NSUB).astype(bf16)
    dv_ref[...] = dot_tn(left, inbox).astype(bf16)
    cross[:, at, :] = dot_nt(inbox, v_ref[...]).reshape(sources, CAP, NSUB)

    @pl.when(step == pl.num_programs(0) - 1)
    def _():
        iota = lax.broadcasted_iota(jnp.int32, (NSUB, width), 0).astype(f32)

        def select(src, carry):
            turned = cross[src].T
            names = names_ref[src].astype(f32)
            picked = [
                jnp.sum(jnp.where(iota == names[b : b + 1, :], turned, 0.0), axis=0, keepdims=True)
                for b in range(8)
            ]
            gw_ref[src] = jnp.concatenate(picked, axis=0)
            return carry

        lax.fori_loop(0, sources, select, 0)


def write_call(idx, grads, names, layer, dense, values, plan, tokens):
    sources, width, _ = dense.shape
    steps = width // CAP
    d_model = values.shape[2]
    quarter = d_model // 4
    return pl.pallas_call(
        functools.partial(write_kernel, plan=plan),
        grid=(steps,),
        out_shape=[shape((values.shape[1], d_model), bf16), shape((sources, 8, width), f32)],
        in_specs=[pl.BlockSpec(memory_space=pltpu.SMEM)]
        + [pl.BlockSpec((4 * tokens, quarter), lambda g: (0, 0)) for _ in range(4)]
        + [
            pl.BlockSpec((sources, 16, width), lambda g: (0, layer, 0)),
            pl.BlockSpec((sources, width, NSUB), lambda g: (0, 0, 0)),
            pl.BlockSpec((None, NSUB, d_model), lambda g: (layer, g, 0)),
        ],
        out_specs=[
            pl.BlockSpec((NSUB, d_model), lambda g: (g, 0)),
            pl.BlockSpec((sources, 8, width), lambda g: (0, 0, 0)),
        ],
        scratch_shapes=[
            pltpu.VMEM((4, tokens, d_model), bf16),
            pltpu.VMEM((sources, width, d_model), f32),
            pltpu.VMEM((sources, width, NSUB), f32),
        ],
        compiler_params=pltpu.CompilerParams(vmem_limit_bytes=48 * MIB),
        cost_estimate=pl.CostEstimate(
            flops=6 * sources * width * NSUB * d_model, bytes_accessed=28 * MIB, transcendentals=0
        ),
        name="memory_write",
    )(idx, *grads, names, dense, values)


def sum_kernel(idx, m0, r1, r2, r3, o0, o1, o2, o3):
    count = o0.shape[0]
    for dz, out in enumerate((o0, o1, o2, o3)):
        at = slice(count * dz, count * (dz + 1))
        out[...] = (
            (m0[at, :].astype(f32) + r1[at, :].astype(f32))
            + (r2[at, :].astype(f32) + r3[at, :].astype(f32))
        ).astype(bf16)


def gather_shards(x, axis):
    if lax.axis_size("fsdp") != 2:
        return lax.all_gather(x, "fsdp", axis=axis, tiled=True)
    other = swap(x, "fsdp", 1)
    mine = lax.axis_index("fsdp") == 0
    return jnp.where(
        mine, jnp.concatenate([x, other], axis=axis), jnp.concatenate([other, x], axis=axis)
    )


def body(
    inputs,
    query_weight,
    key_weight,
    value_weight,
    attention_weight,
    lookup_weight,
    gate_weight,
    memory_weight,
    first_table,
    second_table,
    attention_gain,
    memory_gain,
    memory_values,
    blocks,
    first_picks,
    second_picks,
    cotangent,
):
    plan = PLAN
    SA, TA = plan.SA, plan.TA
    layers = query_weight.shape[0]
    tokens = inputs.shape[1]
    d_model = inputs.shape[2]
    chunk = tokens // 4
    width = query_weight.shape[2]
    shards = lax.axis_size("fsdp")
    owners = lax.axis_size("ctx") * lax.axis_size("tp")
    groups = memory_values.shape[1] // NSUB
    lanes = shards * groups * CAP
    gbits = groups.bit_length() - 1
    dbits = owners.bit_length() - 1
    idx = jnp.stack(
        [lax.axis_index("fsdp"), lax.axis_index("ctx"), lax.axis_index("tp"), 0]
    ).astype(jnp.int32)

    gains = gather_shards(jnp.concatenate([attention_gain, memory_gain], axis=0).astype(bf16), 1)
    gains = gains.astype(f32)
    w_qkv, w_o, w_gate, w_look, w_mem, tab_a, tab_b = [], [], [], [], [], [], []
    for l in range(layers):
        w_qkv.append(
            gather_shards(
                jnp.concatenate([query_weight[l], key_weight[l], value_weight[l]], axis=1).astype(bf16), 0
            )
        )
        w_o.append(gather_shards(attention_weight[l].astype(bf16), 1))
        w_look.append(gather_shards(lookup_weight[l].astype(bf16), 0))
        tables = gather_shards(
            jnp.concatenate([first_table[l, 0], second_table[l, 0]], axis=1).astype(bf16), 0
        )
        tab_a.append(tables[:, :HD])
        tab_b.append(tables[:, HD:])
        w_gate.append(gather_shards(gate_weight[l].astype(bf16), 0))
        w_mem.append(gather_shards(memory_weight[l].astype(bf16), 1))
    values = lax.all_gather(memory_values, "fsdp", axis=1, tiled=True)

    ids_row = blocks
    ids_col = blocks.reshape(-1, 1)
    firsts = [first_picks[l, 0, 0].T for l in range(layers)]
    seconds = [second_picks[l, 0, 0].reshape(tokens, -1).T for l in range(layers)]
    picks = first_picks.shape[4]
    slots, names = [], []
    for l in range(layers):
        slot, name = kernel_call(
            functools.partial(slots_kernel, gbits=gbits, dbits=dbits),
            "pick_slots",
            [shape((picks, tokens), jnp.int32), shape((owners, 16, lanes), bf16)],
            idx,
            [firsts[l], seconds[l]],
        )
        slots.append(slot)
        names.append(name)
    names = lax.all_to_all(jnp.concatenate(names, axis=1), ("ctx", "tp"), 0, 0, tiled=True)

    heads_shape = shape((tokens * 3 // 2, 2 * HD), bf16)
    folded = shape((tokens // 2, 2 * HD), bf16)
    part_shape = shape((chunk, d_model), bf16)
    chunk_shape = shape((chunk, d_model), f32)
    full_shape = shape((tokens, d_model), bf16)
    pack_scratch = pltpu.VMEM((4, tokens * 3 // 2, 2 * HD), bf16)
    part_scratch = pltpu.VMEM((tokens, d_model), bf16)
    kv_scratch = [
        pltpu.VMEM((4 * tokens, HD), bf16),
        pltpu.VMEM((4 * tokens, HD), bf16),
        pltpu.VMEM((4 * tokens, 1), jnp.int32),
    ]
    x = inputs[0]
    h_chunk = None
    kept = []
    for l in range(layers):
        if l == 0:
            h1, *es = kernel_call(
                functools.partial(qkv_first_kernel, plan=plan, row=l),
                "qkv_first",
                [full_shape] + [heads_shape] * 4,
                idx,
                [x, gains, w_qkv[l]],
                [pack_scratch],
            )
        else:
            h1, *es = kernel_call(
                functools.partial(qkv_kernel, plan=plan),
                "qkv",
                [full_shape] + [heads_shape] * 4,
                idx,
                [*spread(h_chunk, TA), w_qkv[l]],
                [pack_scratch],
            )
        es = swaps(es, SA)
        heads = kernel_call(
            functools.partial(attend_kernel, plan=plan),
            "attend",
            [folded] * 4,
            idx,
            [*es, ids_row, ids_col],
            kv_scratch,
        )
        attended, *parts = kernel_call(
            functools.partial(out_kernel, plan=plan),
            "attend_out",
            [shape((tokens, width), bf16)] + [part_shape] * 4,
            idx,
            [*swaps(heads, SA), w_o[l]],
            [pltpu.VMEM((4, tokens, HD), bf16), part_scratch],
        )
        middle, h_chunk = kernel_call(
            functools.partial(norm_kernel, plan=plan, row=layers + l),
            "norm_mid",
            [chunk_shape, part_shape],
            idx,
            [x, *swaps(parts, TA), gains],
        )
        h2, u, w, outbox = kernel_call(
            functools.partial(lookup_kernel, plan=plan),
            "lookup",
            [
                full_shape,
                shape((tokens, w_look[l].shape[1]), bf16),
                shape(seconds[l].shape, f32),
                shape((owners, 8, lanes), f32),
            ],
            idx,
            [*spread(h_chunk, TA), w_look[l], tab_a[l], tab_b[l], firsts[l], seconds[l], slots[l]],
        )
        weights = lax.all_to_all(outbox, ("ctx", "tp"), 0, 0, tiled=True)
        gate = dot(h2, w_gate[l])
        *reads, dense = read_call(idx, weights, names, l, values, plan, tokens)
        sums = kernel_call(
            sum_kernel,
            "memory_sum",
            [shape((tokens, width), bf16)] * 4,
            idx,
            swaps(reads, "ctx"),
        )
        first_sum, *rest = swaps(sums, "tp")
        mem, z, *parts = kernel_call(
            functools.partial(gate_sum_kernel, plan=plan),
            "gate",
            [shape((tokens, width), f32), shape((tokens, width), bf16)] + [part_shape] * 4,
            idx,
            [first_sum, *rest, gate, w_mem[l]],
            [part_scratch],
        )
        kept.append((x, h1, es, attended, middle, h2, u, w, gate, dense, mem, z))
        if l + 1 < layers:
            x, h_chunk = kernel_call(
                functools.partial(norm_kernel, plan=plan, row=l + 1),
                "norm_next",
                [chunk_shape, part_shape],
                idx,
                [middle, *swaps(parts, TA), gains],
            )
        else:
            (out_chunk,) = kernel_call(
                functools.partial(last_kernel, plan=plan),
                "last",
                [part_shape],
                idx,
                [middle, *swaps(parts, TA)],
            )
    output = lax.all_gather(out_chunk, TA, axis=0, tiled=True)[None]

    g = cotangent[0]
    gy_chunk = None
    grads = []
    table_grads = []
    fence = None
    for l in reversed(range(layers)):
        x, h1, es, attended, middle, h2, u, w, gate, dense, mem, z = kept[l]
        pair = [shape((tokens, width), bf16)] * 2
        if l == layers - 1:
            gy = g
            gn, gg = kernel_call(
                gate_back_full_kernel, "gate_back_first", pair, idx, [gy, w_mem[l], gate, mem]
            )
        else:
            gy, gn, gg = kernel_call(
                functools.partial(gate_back_kernel, plan=plan),
                "gate_back",
                [full_shape] + pair,
                idx,
                [*spread(gy_chunk, TA), w_mem[l], gate, mem],
            )
        d_mem = dot_tn(z, gy).astype(bf16)
        d_gate = dot_tn(h2, gg).astype(bf16)
        line = jnp.concatenate(spread(gn, "tp"), axis=0)
        dv, gw = write_call(idx, spread(line, "ctx"), names, l, dense, values, plan, tokens)
        table_grads.insert(0, lax.psum_scatter(dv, "fsdp", scatter_dimension=0, tiled=True))
        gw = lax.all_to_all(gw, ("ctx", "tp"), 0, 0, tiled=True)
        *parts, gu, d_first, d_second = kernel_call(
            functools.partial(lookup_back_kernel, plan=plan),
            "lookup_back",
            [part_shape] * 4
            + [shape(u.shape, bf16), shape((NSUB, HD), bf16), shape((NSUB, HD), bf16)],
            idx,
            [gw, slots[l], w, firsts[l], seconds[l], tab_a[l], tab_b[l], u, gg, w_gate[l], w_look[l]],
            [pltpu.VMEM(w.shape, f32), part_scratch],
        )
        d_look = dot_tn(h2, gu).astype(bf16)
        g_mid, go_chunk, d_gain_two = kernel_call(
            functools.partial(norm_back_kernel, plan=plan, row=layers + l),
            "norm_mid_back",
            [chunk_shape, part_shape, shape((1, d_model), f32)],
            idx,
            [*swaps(parts, TA), middle, g, gains],
        )
        go, *ups = kernel_call(
            functools.partial(out_back_kernel, plan=plan),
            "attend_out_back",
            [full_shape] + [folded] * 4,
            idx,
            [*spread(go_chunk, TA), w_o[l]],
            [pltpu.VMEM((4, tokens // 2, 2 * HD), bf16)],
        )
        d_out = dot_tn(attended, go).astype(bf16)
        head_grads = kernel_call(
            functools.partial(attend_back_kernel, plan=plan),
            "attend_back",
            [heads_shape] * 4,
            idx,
            [*es, *swaps(ups, SA), ids_row, ids_col],
            kv_scratch + [pltpu.VMEM((4 * tokens, HD), f32)] * 2,
        )
        g_qkv, *parts = kernel_call(
            functools.partial(qkv_back_kernel, plan=plan),
            "qkv_back",
            [shape((tokens, 3 * width), bf16)] + [part_shape] * 4,
            idx,
            [*swaps(head_grads, SA), w_qkv[l]],
            [pack_scratch, part_scratch],
        )
        d_qkv = dot_tn(h1, g_qkv).astype(bf16)
        g, gy_chunk, d_gain_one = kernel_call(
            functools.partial(norm_back_kernel, plan=plan, row=l),
            "norm_back",
            [chunk_shape, part_shape, shape((1, d_model), f32)],
            idx,
            [*swaps(parts, TA), x, g_mid, gains],
        )
        gain_rows = jnp.concatenate([d_gain_one, d_gain_two], axis=0)
        gain_rows = sum(spread(gain_rows, "tp")[1:], gain_rows)
        if lax.axis_size("tp") != 4:
            raise ValueError("tp")
        pieces = [
            (jnp.concatenate([d_qkv, d_gate, d_look], axis=1), 0),
            (jnp.concatenate([d_out, d_mem], axis=0), 1),
            (jnp.concatenate([d_first, d_second], axis=1), 0),
            (gain_rows.astype(bf16), 1),
        ]
        if fence is not None:
            fenced = lax.optimization_barrier(tuple(p for p, _ in pieces) + tuple(fence))
            pieces = [(q, axis) for q, (_, axis) in zip(fenced, pieces)]
            grads[0] = fenced[len(pieces) :]
        reduced = [
            lax.psum(lax.psum_scatter(p, "fsdp", scatter_dimension=axis, tiled=True), "ctx")
            for p, axis in pieces
        ]
        fence = reduced
        grads.insert(0, reduced)
    input_gradient = lax.all_gather(gy_chunk, TA, axis=0, tiled=True).astype(f32)[None]

    def stacked(pick):
        return jnp.stack([pick(*grads[l]).astype(f32) for l in range(layers)])

    return (
        output,
        input_gradient,
        stacked(lambda a, b, c, d: a[:, :width]),
        stacked(lambda a, b, c, d: a[:, width : 2 * width]),
        stacked(lambda a, b, c, d: a[:, 2 * width : 3 * width]),
        stacked(lambda a, b, c, d: b[:width]),
        stacked(lambda a, b, c, d: a[:, 4 * width :]),
        stacked(lambda a, b, c, d: a[:, 3 * width : 4 * width]),
        stacked(lambda a, b, c, d: b[width:]),
        stacked(lambda a, b, c, d: c[None, :, :HD]),
        stacked(lambda a, b, c, d: c[None, :, HD:]),
        stacked(lambda a, b, c, d: d[0]),
        stacked(lambda a, b, c, d: d[1]),
        jnp.stack([t.astype(f32) for t in table_grads]),
    )


def gate_sum_kernel(idx, m0, m1, m2, m3, gate_ref, w_ref, mem_ref, z_ref, p0, p1, p2, p3, part, plan):
    mem = total4((m0, m1, m2, m3))
    mem_ref[...] = mem
    gate = gate_ref[...]
    z = (mem * (gate * jax.nn.sigmoid(gate))).astype(bf16)
    z_ref[...] = z
    part[...] = dot(z, w_ref[...]).astype(bf16)
    emit_chunks(part, (p0, p1, p2, p3), idx[plan.ti])


def out_back_kernel(idx, g0, g1, g2, g3, w_ref, go_ref, u0, u1, u2, u3, pack, plan):
    place_chunks((g0, g1, g2, g3), go_ref, idx[plan.ti])
    up = dot_nt(go_ref[...], w_ref[...]).astype(bf16)
    for j in range(4):
        pack[j] = fold(up[:, HD * j : HD * (j + 1)])
    for d, u in enumerate((u0, u1, u2, u3)):
        u[...] = pack[idx[plan.si] ^ d]


def qkv_back_kernel(idx, g0, g1, g2, g3, w_ref, g_ref, p0, p1, p2, p3, pack, part, plan):
    for d, g in enumerate((g0, g1, g2, g3)):
        pack[idx[plan.si] ^ d] = g[...]
    rows = g_ref.shape[0]
    columns = [pack[j, 0:rows, 0:HD] for j in range(4)]
    columns += [pack[j, 0:rows, HD : 2 * HD] for j in range(4)]
    columns += [unfold(pack[j, rows:, :]) for j in range(4)]
    g_ref[...] = jnp.concatenate(columns, axis=1)
    part[...] = dot_nt(g_ref[...], w_ref[...]).astype(bf16)
    emit_chunks(part, (p0, p1, p2, p3), idx[plan.ti])


def solution(mesh):
    placed = (
        P("fsdp", "ctx", None),
        P(None, "fsdp", "tp"),
        P(None, "fsdp", "tp"),
        P(None, "fsdp", "tp"),
        P(None, "tp", "fsdp"),
        P(None, "fsdp", "tp"),
        P(None, "fsdp", "tp"),
        P(None, "tp", "fsdp"),
        P(None, "tp", "fsdp", None),
        P(None, "tp", "fsdp", None),
        P(None, "fsdp"),
        P(None, "fsdp"),
        P(None, ("fsdp", "ctx", "tp"), None),
        P("fsdp", None),
        P(None, "fsdp", "tp", "ctx", None),
        P(None, "fsdp", "tp", "ctx", None, None),
        P("fsdp", "ctx", None),
    )
    return jax.shard_map(
        body,
        mesh=mesh,
        in_specs=placed,
        out_specs=(
            P("fsdp", "ctx", None),
            P("fsdp", "ctx", None),
            P(None, "fsdp", "tp"),
            P(None, "fsdp", "tp"),
            P(None, "fsdp", "tp"),
            P(None, "tp", "fsdp"),
            P(None, "fsdp", "tp"),
            P(None, "fsdp", "tp"),
            P(None, "tp", "fsdp"),
            P(None, "tp", "fsdp", None),
            P(None, "tp", "fsdp", None),
            P(None, "fsdp"),
            P(None, "fsdp"),
            P(None, ("fsdp", "ctx", "tp"), None),
        ),
        check_vma=False,
    )
```

time: 2170 us -> 801 us (0.37)
  blocking collectives: 669 us -> 93 us
  waiting for transfers between devices: 757 us -> 273 us
  local copies, waits for them, and re-layouts: 486 us -> 55.1 us
  Pallas kernels: 0 us -> 130 us
  starting transfers between devices: 23.2 us -> 151 us
  matrix products: 98.5 us -> 15.7 us
  other arithmetic: 104 us -> 58 us
    all_to_all x11 -> x2, blocking collectives: 583 us -> 23.4 us  [the longest x1 12.1 us: body(): weights = lax.all_to_all(outbox, ('ctx', 'tp'), 0, 0, tiled=True)]
    gather x32 -> x0, local copies, waits for them, and re-layouts: 375 us -> none  [the longest x10 163 us: body(): weight_adjoint = jnp.take_along_axis(rows_adjoint, second_ids, axis=2)]
    psum x9 -> x2, waiting for transfers between devices: 391 us -> 21.2 us  [body(): lax.psum(lax.psum_scatter(p, 'fsdp', scatter_dimension=axis, tiled=True),...]
    ppermute x0 -> x109, waiting for transfers between devices: none -> 187 us  [swap(): return lax.ppermute(x, axis, [(i, i ^ step) for i in range(size)])]
    reduce_scatter x13 -> x8, waiting for transfers between devices: 198 us -> 50.9 us  [the longest x2 28.4 us: body(): lax.psum_scatter(dv, 'fsdp', scatter_dimension=0, tiled=True)]
    all_to_all x5 -> x3, waiting for transfers between devices: 149 us -> 10.6 us  [the longest x1 7.23 us: body(): gw = lax.all_to_all(gw, ('ctx', 'tp'), 0, 0, tiled=True)]
    ppermute x0 -> x109, starting transfers between devices: none -> 134 us  [swap(): return lax.ppermute(x, axis, [(i, i ^ step) for i in range(size)])]
    pallas_call x0 -> x36, Pallas kernels: none -> 130 us  [the longest x32 60.8 us: kernel_call(): pl.pallas_call(body, out_shape=outs, in_specs=in_specs, out_specs=[pl.Blo...]
  transfers between devices with their start and end apart: 37 -> 125, of which waited for: 28 -> 74; matrix products, arithmetic and copies ran while one was open for 12% -> 10% of each run, Pallas kernels for 0% -> 10%
where the time goes in v1:
time: 801 us; the launch traced here: 791 us
  waiting for transfers between devices  273 us (34%)
  starting transfers between devices  151 us (19%)
  Pallas kernels  130 us (16%)
  blocking collectives  93 us (12%)
  other arithmetic  58 us (7%)
  local copies, waits for them, and re-layouts  55.1 us (7%)
  between operations  16 us (2%)
  matrix products  15.7 us (2%)
    ppermute x109, waiting for transfers between devices, swap(): return lax.ppermute(x, axis, [(i, i ^ step) for i in range(size)])  187 us
    ppermute x109, starting transfers between devices, swap(): return lax.ppermute(x, axis, [(i, i ^ step) for i in range(size)])  134 us
    pallas_call x32, Pallas kernels, kernel_call(): pl.pallas_call(body, out_shape=outs, in_specs=in_specs, out_specs=[pl.Blo...  60.8 us
    unnamed x304, local copies, waits for them, and re-layouts  47 us
    pallas_call x2, Pallas kernels, write_call(): pl.pallas_call(functools.partial(write_kernel, plan=plan), grid=(steps,),...  39.5 us
    psum x2, blocking collectives, body(): lax.psum(lax.psum_scatter(p, 'fsdp', scatter_dimension=axis, tiled=True),...  36.9 us
    pallas_call x2, Pallas kernels, read_call(): pl.pallas_call(functools.partial(read_kernel, plan=plan), grid=(steps,),...  29.7 us
    reduce_scatter x2, waiting for transfers between devices, body(): lax.psum_scatter(dv, 'fsdp', scatter_dimension=0, tiled=True)  28.4 us
  transfers between devices with their start and end apart: 125, of which 74 were waited for; matrix products, arithmetic and copies ran while one was open for 10% of the time, Pallas kernels for 10%

profile of v1, /device:TPU:0, one launch (start us, length us, event | category | flops | bytes accessed | tf_op | source)
XLA Modules:
  0.0 791.4 jit_solution(11704818715781563439)
XLA Ops:
  20.1 7.9 all-to-all-start.1
  30.4 8.8 %maximum_select_fusion.w_ref = bf16[1024,768]{1,0:T(8,128)(2,1)S(1)} fusion(bf16[512,768]{1,0:T(8,128)(2,1)} %collective-permute-done.1, bf16[512,256]{1,0:T(8,128)(2,1)S(1)} %get-tuple-element.379, bf16[512,256]{1,0:T(8,128)(2,1)S(1)} %get-tuple-element.402, bf16[512,256]{1,0:T(8,128)(2,1)S(1)} %get-tuple-element.375, pred[]{:T(512)S(6)} %eq.2), kind=kLoop, calls=%fused_computation.5 | loop fusion | flops 13369344 | bytes 3145729 | tf_op jit(solution)/shard_map/jit(_where)/select_n | solution.py:553
  106.7 14.9 %memory_read.2 = (bf16[1024,256]{1,0:T(8,128)(2,1)S(1)}, bf16[1024,256]{1,0:T(8,128)(2,1)S(1)}, bf16[1024,256]{1,0:T(8,128)(2,1)S(1)}, bf16[1024,256]{1,0:T(8,128)(2,1)S(1)}, f32[16,128,256]{2,1,0:T(8,128)S(1)}) custom-call(s32[4]{0:T(128)S(1)} %pad_add_fusion.idx, f32[16,8,128]{2,1,0:T(8,128)S(1)} %all-to-all-done.w_ref, ...), custom_call_target="tpu_custom_call" | custom-call | flops 2147483648 | bytes 20971520 | tf_op jit(solution)/shard_map/memory_read/pallas_call | solution.py:434
  127.0 9.6 %collective-permute-done.17.r1 = bf16[1024,256]{1,0:T(8,128)(2,1)S(1)} collective-permute-done((bf16[1024,256]{1,0:T(8,128)(2,1)S(1)}, bf16[1024,256]{1,0:T(8,128)(2,1)S(1)}, u32[]{:S(2)}, u32[]{:S(2)}) %collective-permute-start.17) | collective-permute-done | bytes 524320 | tf_op jit(solution)/shard_map/ppermute | solution.py:34
  136.6 9.0 %collective-permute-done.18.r2 = bf16[1024,256]{1,0:T(8,128)(2,1)S(1)} collective-permute-done((bf16[1024,256]{1,0:T(8,128)(2,1)S(1)}, bf16[1024,256]{1,0:T(8,128)(2,1)S(1)}, u32[]{:S(2)}, u32[]{:S(2)}) %collective-permute-start.18) | collective-permute-done | bytes 524320 | tf_op jit(solution)/shard_map/ppermute | solution.py:34
  167.9 7.5 collective-permute-done.26.r2
  181.4 8.5 %maximum_select_fusion.1.w_ref = bf16[1024,768]{1,0:T(8,128)(2,1)S(1)} fusion(bf16[512,768]{1,0:T(8,128)(2,1)} %collective-permute-done.31, bf16[512,256]{1,0:T(8,128)(2,1)S(1)} %copy-done.106, bf16[512,256]{1,0:T(8,128)(2,1)S(1)} %copy-done.107, bf16[512,256]{1,0:T(8,128)(2,1)S(1)} %copy-done.105, pred[]{:T(512)S(6)} %eq.2), kind=kLoop, calls=%fused_computation.6 | loop fusion | flops 13369344 | bytes 3145729 | tf_op jit(solution)/shard_map/jit(_where)/select_n | solution.py:553
  217.9 8.0 %collective-permute-done.40.r2 = bf16[64,1024]{1,0:T(8,128)(2,1)S(1)} collective-permute-done((bf16[64,1024]{1,0:T(8,128)(2,1)S(1)}, bf16[64,1024]{1,0:T(8,128)(2,1)S(1)}, u32[]{:S(2)}, u32[]{:S(2)}) %collective-permute-start.40) | collective-permute-done | bytes 131104 | tf_op jit(solution)/shard_map/ppermute | solution.py:34
  241.2 12.1 %all_to_all.25.w_ref = f32[16,8,128]{2,1,0:T(8,128)S(1)} all-to-all(f32[16,8,128]{2,1,0:T(8,128)S(1)} %get-tuple-element.208), channel_id=1, replica_groups=mesh['fsdp'=2,'ctx'=4,'tp'=4] {'ctx','tp'}, dimensions={0} | all-to-all | bytes 131072 | tf_op jit(solution)/shard_map/all_to_all | solution.py:702
  253.3 14.8 %memory_read.3 = (bf16[1024,256]{1,0:T(8,128)(2,1)S(1)}, bf16[1024,256]{1,0:T(8,128)(2,1)S(1)}, bf16[1024,256]{1,0:T(8,128)(2,1)S(1)}, bf16[1024,256]{1,0:T(8,128)(2,1)S(1)}, f32[16,128,256]{2,1,0:T(8,128)S(1)}) custom-call(s32[4]{0:T(128)S(1)} %copy-done.22, f32[16,8,128]{2,1,0:T(8,128)S(1)} %all_to_all.25.w_ref, ...), custom_call_target="tpu_custom_call" | custom-call | flops 2147483648 | bytes 20971520 | tf_op jit(solution)/shard_map/memory_read/pallas_call | solution.py:434
  328.1 19.4 %memory_write.2 = (bf16[4096,1024]{1,0:T(8,128)(2,1)}, f32[16,8,128]{2,1,0:T(8,128)S(1)}) custom-call(s32[4]{0:T(128)S(1)} %copy-done.22, bf16[1024,256]{1,0:T(8,128)(2,1)S(1)} %constant_dynamic-update-slice_fusion.g0, bf16[1024,256]{1,0:T(8,128)(2,1)S(1)} %collective-permute-done.61.g1, bf16[1024,256]{1,0:T(8,128)(2,1)S(1)} %collective-permute-done.62.g2, ...), custom_call_target="tpu_custom_call" | custom-call | flops 3221225472 | bytes 29360128 | tf_op jit(solution)/shard_map/memory_write/pallas_call | solution.py:510
  347.5 11.3 %all_to_all.26.gw_ref = f32[16,8,128]{2,1,0:T(8,128)S(1)} all-to-all(f32[16,8,128]{2,1,0:T(8,128)S(1)} %get-tuple-element.225), channel_id=1, replica_groups=mesh['fsdp'=2,'ctx'=4,'tp'=4] {'ctx','tp'}, dimensions={0} | all-to-all | bytes 131072 | tf_op jit(solution)/shard_map/all_to_all | solution.py:766
  469.5 19.4 %all-reduce.1 = (bf16[128,128]{1,0:T(8,128)(2,1)}, bf16[2,512]{1,0:T(2,128)(2,1)}) all-reduce(bf16[128,128]{1,0:T(8,128)(2,1)} %reduce-scatter.19.cloned.1.call-done, bf16[2,512]{1,0:T(2,128)(2,1)} %copy.67), channel_id=1, replica_groups=mesh['fsdp'=2,'ctx'=4,'tp'=4] {'ctx'}, use_global_device_ids=true, to_apply=%region_5.6 | all-reduce | flops 17408 | bytes 69632 | tf_op jit(solution)/shard_map/psum | solution.py:832
  492.3 20.0 %memory_write.3 = (bf16[4096,1024]{1,0:T(8,128)(2,1)}, f32[16,8,128]{2,1,0:T(8,128)S(1)}) custom-call(s32[4]{0:T(128)S(1)} %copy-done.24, bf16[1024,256]{1,0:T(8,128)(2,1)S(1)} %copy-done.20, bf16[1024,256]{1,0:T(8,128)(2,1)} %collective-permute-done.85.g1, bf16[1024,256]{1,0:T(8,128)(2,1)} %collective-permute-done.86.g2, ...), custom_call_target="tpu_custom_call" | custom-call | flops 3221225472 | bytes 29360128 | tf_op jit(solution)/shard_map/memory_write/pallas_call | solution.py:510
  557.4 7.8 collective-permute-done.92.g2
  619.3 9.1 %reduce-scatter.23.cloned.1.call-done = bf16[512,512]{1,0:T(8,128)(2,1)} async-done(((bf16[512,1024]{1,0:T(8,128)(2,1)}), bf16[512,512]{1,0:T(8,128)(2,1)}) %reduce-scatter.23.cloned.1.call-update) | async-done | bytes 524304 | tf_op jit(solution)/shard_map/reduce_scatter | solution.py:832
  628.5 13.3 %reduce-scatter.21.cloned.1.call-done = bf16[512,1152]{0,1:T(8,128)(2,1)} async-done(((bf16[1024,1152]{0,1:T(8,128)(2,1)}), bf16[512,1152]{0,1:T(8,128)(2,1)}) %reduce-scatter.21.cloned.1.call-update) | async-done | bytes 1179664 | tf_op jit(solution)/shard_map/reduce_scatter | solution.py:832
  658.6 17.2 %all_gather.10 = bf16[256,1024]{1,0:T(8,128)(2,1)S(1)} all-gather(bf16[64,1024]{1,0:T(8,128)(2,1)S(1)} %last.1), channel_id=1, replica_groups=mesh['fsdp'=2,'ctx'=4,'tp'=4] {'tp'}, dimensions={0}, use_global_device_ids=true | all-gather | bytes 655360 | tf_op jit(solution)/shard_map/all_gather | solution.py:738
  675.9 15.4 %all_gather.11 = bf16[256,1024]{1,0:T(8,128)(2,1)S(1)} all-gather(bf16[64,1024]{1,0:T(8,128)(2,1)S(1)} %get-tuple-element.274), channel_id=1, replica_groups=mesh['fsdp'=2,'ctx'=4,'tp'=4] {'tp'}, dimensions={0}, use_global_device_ids=true | all-gather | bytes 655360 | tf_op jit(solution)/shard_map/all_gather | solution.py:837
  694.4 17.5 %all-reduce = (bf16[128,128]{1,0:T(8,128)(2,1)S(1)}, bf16[2,512]{1,0:T(2,128)(2,1)S(1)}) all-reduce(bf16[128,128]{1,0:T(8,128)(2,1)} %reduce-scatter.25.cloned.1.call-done, bf16[2,512]{1,0:T(2,128)(2,1)S(1)} %copy.69), channel_id=1, replica_groups=mesh['fsdp'=2,'ctx'=4,'tp'=4] {'ctx'}, use_global_device_ids=true, to_apply=%region_13.14 | all-reduce | flops 17408 | bytes 69632 | tf_op jit(solution)/shard_map/psum | solution.py:832
  714.7 18.4 %all-reduce.7.cloned.1.call-done = (bf16[512,1152]{0,1:T(8,128)(2,1)}, bf16[512,512]{1,0:T(8,128)(2,1)}) async-done(((bf16[512,1152]{0,1:T(8,128)(2,1)}, bf16[512,512]{1,0:T(8,128)(2,1)}), (bf16[512,1152]{0,1:T(8,128)(2,1)}, bf16[512,512]{1,0:T(8,128)(2,1)})) %all-reduce.7.cloned.1.call-update) | async-done | bytes 1703952 | tf_op jit(solution)/shard_map/psum | solution.py:832
  744.7 7.9 %reduce-scatter.29.cloned.1.call-done = bf16[2048,1024]{1,0:T(8,128)(2,1)} async-done(((bf16[4096,1024]{1,0:T(8,128)(2,1)}), bf16[2048,1024]{1,0:T(8,128)(2,1)}) %reduce-scatter.29.cloned.1.call-update) | async-done | bytes 4194320 | tf_op jit(solution)/shard_map/reduce_scatter | solution.py:765
  752.6 20.5 %reduce-scatter.27.cloned.1.call-done = bf16[2048,1024]{1,0:T(8,128)(2,1)} async-done(((bf16[4096,1024]{1,0:T(8,128)(2,1)}), bf16[2048,1024]{1,0:T(8,128)(2,1)}) %reduce-scatter.27.cloned.1.call-update) | async-done | bytes 4194320 | tf_op jit(solution)/shard_map/reduce_scatter | solution.py:765
  773.1 10.7 %maximum_convert_fusion = f32[2,2048,1024]{2,1,0:T(8,128)} fusion(bf16[1,2048,1024]{2,1,0:T(8,128)(2,1)} %bitcast.135, bf16[1,2048,1024]{2,1,0:T(8,128)(2,1)} %bitcast.136), kind=kLoop, calls=%fused_computation | loop fusion | flops 8388608 | bytes 25165824 | tf_op jit(solution)/shard_map/stack | solution.py:856
  (673 shorter events, 466.5 us)
Async XLA Ops:
  7.2 99.5 %all-gather.2.cloned.1.call-start = ((), (), s32[]{:S(2)}) async-start(), calls=%async_computation.15 | async-start | bytes 25165824 | tf_op jit(solution)/shard_map/all_gather | solution.py:612
  10.1 57.9 %collective-permute-start.16 = (bf16[128,128]{1,0:T(8,128)(2,1)}, bf16[128,128]{1,0:T(8,128)(2,1)}, u32[]{:S(2)}, u32[]{:S(2)}) collective-permute-start(bf16[128,128]{1,0:T(8,128)(2,1)} %pad_maximum_fusion.9), channel_id=1, source_target_pairs={{0,16},{16,0},{1,17},{17,1},{2,18},{18,2},{3,19},{19,3},{4,20},{20... | collective-permute-start | bytes 98312 | tf_op jit(solution)/shard_map/ppermute | solution.py:34
  20.1 74.6 %all-to-all-start.1 = ((bf16[16,32,128]{2,1,0:T(8,128)(2,1)}), bf16[16,32,128]{2,1,0:T(8,128)(2,1)S(1)}, u32[]{:S(2)}, u32[]{:S(2)}) async-start(bf16[16,32,128]{2,1,0:T(8,128)(2,1)} %pad_maximum_fusion.6), calls=%async_computation.1 | async-start | bytes 262144 | tf_op jit(solution)/shard_map/all_to_all | solution.py:630
  28.9 27.2 %collective-permute-start.8 = (bf16[256,512]{1,0:T(8,128)(2,1)}, bf16[256,512]{1,0:T(8,128)(2,1)}, u32[]{:S(2)}, u32[]{:S(2)}) collective-permute-start(bf16[256,512]{1,0:T(8,128)(2,1)} %get-tuple-element.373), channel_id=1, source_target_pairs={{0,16},{16,0},{1,17},{17,1},{2,18},{18,2},{3,19},{19,3},{4,20},{20... | collective-permute-start | bytes 786440 | tf_op jit(solution)/shard_map/ppermute | solution.py:34
  47.0 34.4 %collective-permute-start.15 = (bf16[512,128]{1,0:T(8,128)(2,1)}, bf16[512,128]{1,0:T(8,128)(2,1)S(1)}, u32[]{:S(2)}, u32[]{:S(2)}) collective-permute-start(bf16[512,128]{1,0:T(8,128)(2,1)} %get-tuple-element.381), channel_id=1, source_target_pairs={{0,16},{16,0},{1,17},{17,1},{2,18},{18,2},{3,19},{19,3},{4,20},{20... | collective-permute-start | bytes 393224 | tf_op jit(solution)/shard_map/ppermute | solution.py:34
  68.0 57.2 %collective-permute-start.23 = (bf16[512,256]{1,0:T(8,128)(2,1)}, bf16[512,256]{1,0:T(8,128)(2,1)}, u32[]{:S(2)}, u32[]{:S(2)}) collective-permute-start(bf16[512,256]{1,0:T(8,128)(2,1)} %get-tuple-element.371), channel_id=1, source_target_pairs={{0,16},{16,0},{1,17},{17,1},{2,18},{18,2},{3,19},{19,3},{4,20},{20... | collective-permute-start | bytes 786440 | tf_op jit(solution)/shard_map/ppermute | solution.py:34
  99.3 368.7 %reduce-scatter.31.cloned.1.call-start = ((), (), s32[]{:S(2)}) async-start(), calls=%async_computation.24 | async-start | bytes 393216
  101.3 80.0 %collective-permute-start.31 = (bf16[512,768]{1,0:T(8,128)(2,1)}, bf16[512,768]{1,0:T(8,128)(2,1)}, u32[]{:S(2)}, u32[]{:S(2)}) collective-permute-start(bf16[512,768]{1,0:T(8,128)(2,1)} %pad_maximum_fusion.5), channel_id=1, source_target_pairs={{0,16},{16,0},{1,17},{17,1},{2,18},{18,2},{3,19},{19,3},{4,20},{20... | collective-permute-start | bytes 2359304 | tf_op jit(solution)/shard_map/ppermute | solution.py:34
  122.5 23.2 %collective-permute-start.18 = (bf16[1024,256]{1,0:T(8,128)(2,1)S(1)}, bf16[1024,256]{1,0:T(8,128)(2,1)S(1)}, u32[]{:S(2)}, u32[]{:S(2)}) collective-permute-start(bf16[1024,256]{1,0:T(8,128)(2,1)S(1)} %get-tuple-element.180), channel_id=1, source_target_pairs={{0,8},{4,12},{8,0},{12,4},{1,9},{5,13},{9,1},{13,5},{2,10},{6,14},... | collective-permute-start | bytes 1572872 | tf_op jit(solution)/shard_map/ppermute | solution.py:34
  166.4 40.8 %collective-permute-start.38 = (bf16[256,512]{1,0:T(8,128)(2,1)S(1)}, bf16[256,512]{1,0:T(8,128)(2,1)S(1)}, u32[]{:S(2)}, u32[]{:S(2)}) collective-permute-start(bf16[256,512]{1,0:T(8,128)(2,1)S(1)} %copy-done.118), channel_id=1, source_target_pairs={{0,16},{16,0},{1,17},{17,1},{2,18},{18,2},{3,19},{19,3},{4,20},{20... | collective-permute-start | bytes 786440 | tf_op jit(solution)/shard_map/ppermute | solution.py:34
  427.1 42.5 %reduce-scatter.19.cloned.1.call-start = ((), (), s32[]{:S(2)}) async-start(), calls=%async_computation.18 | async-start | bytes 98304 | tf_op jit(solution)/shard_map/reduce_scatter | solution.py:832
  428.7 125.6 %reduce-scatter.17.cloned.1.call-start = ((), (), s32[]{:S(2)}) async-start(), calls=%async_computation.17 | async-start | bytes 1572864 | tf_op jit(solution)/shard_map/reduce_scatter | solution.py:832
  432.3 122.0 %reduce-scatter.15.cloned.1.call-start = ((), (), s32[]{:S(2)}) async-start(), calls=%async_computation.16 | async-start | bytes 3538944 | tf_op jit(solution)/shard_map/reduce_scatter | solution.py:832
  463.6 25.4 %collective-permute-start.87 = (bf16[1024,256]{1,0:T(8,128)(2,1)S(1)}, bf16[1024,256]{1,0:T(8,128)(2,1)}, u32[]{:S(2)}, u32[]{:S(2)}) collective-permute-start(bf16[1024,256]{1,0:T(8,128)(2,1)S(1)} %constant_dynamic-update-slice_fusion.4.g0), channel_id=1, source_target_pairs={{0,12},{4,8},{8,4},{12,0},{1,13},{5,9},{9,5},{13,1},{2,14},{6,10},... | collective-permute-start | bytes 1572872 | tf_op jit(solution)/shard_map/ppermute | solution.py:34
  463.9 25.0 %collective-permute-start.86 = (bf16[1024,256]{1,0:T(8,128)(2,1)S(1)}, bf16[1024,256]{1,0:T(8,128)(2,1)}, u32[]{:S(2)}, u32[]{:S(2)}) collective-permute-start(bf16[1024,256]{1,0:T(8,128)(2,1)S(1)} %constant_dynamic-update-slice_fusion.4.g0), channel_id=1, source_target_pairs={{0,8},{4,12},{8,0},{12,4},{1,9},{5,13},{9,1},{13,5},{2,10},{6,14},... | collective-permute-start | bytes 1572872 | tf_op jit(solution)/shard_map/ppermute | solution.py:34
  465.7 23.2 %collective-permute-start.85 = (bf16[1024,256]{1,0:T(8,128)(2,1)S(1)}, bf16[1024,256]{1,0:T(8,128)(2,1)}, u32[]{:S(2)}, u32[]{:S(2)}) collective-permute-start(bf16[1024,256]{1,0:T(8,128)(2,1)S(1)} %constant_dynamic-update-slice_fusion.4.g0), channel_id=1, source_target_pairs={{0,4},{4,0},{8,12},{12,8},{1,5},{5,1},{9,13},{13,9},{2,6},{6,2},{1... | collective-permute-start | bytes 1572872 | tf_op jit(solution)/shard_map/ppermute | solution.py:34
  516.9 100.1 %all-reduce.9.cloned.1.call-start = ((), (), s32[]{:S(2)}) async-start(), calls=%async_computation.27 | async-start | bytes 3407872 | tf_op jit(solution)/shard_map/psum | solution.py:832
  554.4 74.1 %reduce-scatter.23.cloned.1.call-start = ((), (), s32[]{:S(2)}) async-start(), calls=%async_computation.20 | async-start | bytes 1572864 | tf_op jit(solution)/shard_map/reduce_scatter | solution.py:832
  617.0 24.8 %reduce-scatter.21.cloned.1.call-start = ((), (), s32[]{:S(2)}) async-start(), calls=%async_computation.19 | async-start | bytes 3538944 | tf_op jit(solution)/shard_map/reduce_scatter | solution.py:832
  617.8 75.7 %reduce-scatter.33.cloned.1.call-start = ((), (), s32[]{:S(2)}) async-start(), calls=%async_computation.25 | async-start | bytes 393216
  618.7 75.7 %reduce-scatter.25.cloned.1.call-start = ((), (), s32[]{:S(2)}) async-start(), calls=%async_computation.21 | async-start | bytes 98304 | tf_op jit(solution)/shard_map/reduce_scatter | solution.py:832
  619.3 113.8 %all-reduce.7.cloned.1.call-start = ((), (), s32[]{:S(2)}) async-start(), calls=%async_computation.26 | async-start | bytes 3407872 | tf_op jit(solution)/shard_map/psum | solution.py:832
  641.8 110.8 %reduce-scatter.29.cloned.1.call-start = ((), (), s32[]{:S(2)}) async-start(), calls=%async_computation.23 | async-start | bytes 12582912 | tf_op jit(solution)/shard_map/reduce_scatter | solution.py:765
  642.4 130.7 %reduce-scatter.27.cloned.1.call-start = ((), (), s32[]{:S(2)}) async-start(), calls=%async_computation.22 | async-start | bytes 12582912 | tf_op jit(solution)/shard_map/reduce_scatter | solution.py:765
  (243 other events, 3120.5 us)
Sparse Core Ops, SparseCore 0:
  9.6 32.7 all-gather.1
  427.2 5.2 reduce-scatter.30
  434.7 8.5 reduce-scatter.18
  446.1 9.6 reduce-scatter.16
  457.9 11.0 reduce-scatter.14
  554.5 62.4 all-reduce.8
  619.9 8.5 reduce-scatter.22
  630.7 11.0 reduce-scatter.20
  644.7 8.8 reduce-scatter.32
  656.2 8.5 reduce-scatter.24
  668.0 65.0 all-reduce.6
  735.8 16.8 reduce-scatter.28
  755.0 18.0 reduce-scatter.26

commit v2 on v1

v2 whole, which is shorter than its diff:
```python
import functools

import jax
import jax.numpy as jnp
from jax import lax
from jax.experimental import pallas as pl
from jax.experimental.pallas import tpu as pltpu
from jax.sharding import PartitionSpec as P

HD = 64
NSUB = 256
CAP = 8
EPS = 1e-05
NEG = -1e30
f32 = jnp.float32
bf16 = jnp.bfloat16
MIB = 1 << 20


def dot(a, b):
    return jnp.dot(a, b, preferred_element_type=f32)


def dot_nt(a, b):
    return lax.dot_general(a, b, (((1,), (1,)), ((), ())), preferred_element_type=f32)


def dot_tn(a, b):
    return lax.dot_general(a, b, (((0,), (0,)), ((), ())), preferred_element_type=f32)


def swap(x, axis, step):
    size = lax.axis_size(axis)
    return lax.ppermute(x, axis, [(i, i ^ step) for i in range(size)])


def swaps(xs, axis):
    return [xs[0]] + [swap(xs[d], axis, d) for d in range(1, len(xs))]


def spread(x, axis):
    return [x] + [swap(x, axis, d) for d in range(1, lax.axis_size(axis))]


def shape(dims, dtype):
    return jax.ShapeDtypeStruct(dims, dtype)


def kernel_call(body, name, outs, idx, args, scratch=(), limit=32, flops=0):
    in_specs = [pl.BlockSpec(memory_space=pltpu.SMEM)]
    in_specs += [pl.BlockSpec(memory_space=pltpu.VMEM) for _ in args]
    moved = sum(a.size * a.dtype.itemsize for a in args)
    moved += sum(o.size * o.dtype.itemsize for o in outs)
    return pl.pallas_call(
        body,
        out_shape=outs,
        in_specs=in_specs,
        out_specs=[pl.BlockSpec(memory_space=pltpu.VMEM) for _ in outs],
        scratch_shapes=list(scratch),
        compiler_params=pltpu.CompilerParams(vmem_limit_bytes=limit * MIB),
        cost_estimate=pl.CostEstimate(flops=flops, bytes_accessed=moved, transcendentals=0),
        name=name,
    )(idx, *args)


def rows_at(index, count):
    return pl.ds(pl.multiple_of(index * count, count), count)


def rms(x, gain):
    factor = lax.rsqrt(jnp.mean(x * x, axis=1, keepdims=True) + EPS)
    return factor, x * factor * gain


def rms_back(x, factor, gain, upstream):
    scaled = upstream * gain
    return factor * scaled - x * factor**3 * jnp.mean(scaled * x, axis=1, keepdims=True)


def total4(refs):
    return (refs[0][...].astype(f32) + refs[1][...].astype(f32)) + (
        refs[2][...].astype(f32) + refs[3][...].astype(f32)
    )


def fold(x):
    half = x.shape[0] // 2
    return jnp.concatenate([x[:half], x[half:]], axis=1)


def unfold(x):
    half = x.shape[1] // 2
    return jnp.concatenate([x[:, :half], x[:, half:]], axis=0)


class Plan:
    def __init__(self, SA, TA):
        self.SA, self.TA = SA, TA
        self.si = 1 if SA == "ctx" else 2
        self.ti = 1 if TA == "ctx" else 2

    def src(self, sa, ta):
        return sa * 4 + ta if self.SA == "ctx" else ta * 4 + sa

    def rel(self, ds, dt):
        return (ds, dt) if self.SA == "ctx" else (dt, ds)


PLAN = Plan("ctx", "tp")


def slots_kernel(idx, first_ref, second_ref, out_ref, t0, t1, t2, t3, table, plan, gbits, dbits):
    layers, picks, tokens = first_ref.shape
    inner = second_ref.shape[1]
    owners, _, width = out_ref.shape
    lanes = owners * width
    chunk = tokens // 4
    iota = lax.broadcasted_iota(jnp.int32, (NSUB, tokens), 0)
    before = lax.broadcasted_iota(jnp.int32, (tokens, tokens), 0) < lax.broadcasted_iota(
        jnp.int32, (tokens, tokens), 1
    )
    before = jnp.where(before, 1.0, 0.0).astype(bf16)
    row = lax.broadcasted_iota(jnp.int32, (lanes, tokens), 0)
    token_row = (lax.broadcasted_iota(jnp.int32, (8, tokens), 1) + 1).astype(f32)
    token_row = jnp.where(
        lax.broadcasted_iota(jnp.int32, (8, tokens), 0) == 0, token_row, 0.0
    )
    for l in range(layers):
        onehot = jnp.zeros((NSUB, tokens), f32)
        for i in range(picks):
            onehot = jnp.where(iota == first_ref[l, i : i + 1, :], 1.0, onehot)
        counts = dot(onehot.astype(bf16), before)
        total = jnp.zeros((16, lanes), f32)
        slots = []
        for i in range(picks):
            first = first_ref[l, i : i + 1, :]
            rank = jnp.sum(jnp.where(iota == first, counts, 0.0), axis=0, keepdims=True)
            shard = lax.shift_right_logical(first, gbits)
            group = lax.shift_right_logical(shard, dbits) * (1 << gbits) + (first & ((1 << gbits) - 1))
            slot = (shard & ((1 << dbits) - 1)) * width + group * CAP + rank.astype(jnp.int32)
            slots.append(slot)
            names = jnp.concatenate(
                [second_ref[l, 8 * i : 8 * i + 8, :].astype(f32), token_row], axis=0
            )
            hit = jnp.where(row == slot, 1.0, 0.0).astype(bf16)
            total = total + dot_nt(names.astype(bf16), hit)
        for d in range(owners):
            out_ref[d, 16 * l : 16 * l + 16, :] = total[:, d * width : (d + 1) * width].astype(bf16)
        both = jnp.concatenate([first_ref[l], jnp.concatenate(slots, axis=0)], axis=0)
        for n in range(4):
            cut = slice(n * chunk, (n + 1) * chunk)
            at = l * (8 + inner)
            table[n, at : at + 8, :] = both[:, cut]
            table[n, at + 8 : at + 8 + inner, :] = second_ref[l, :, cut]
    for d, out in enumerate((t0, t1, t2, t3)):
        out[...] = table[idx[plan.ti] ^ d]


def pick_table_kernel(idx, t0, t1, t2, t3, out_ref, table, plan):
    for d, t in enumerate((t0, t1, t2, t3)):
        table[idx[plan.ti] ^ d] = t[...]
    rows = out_ref.shape[1]
    for l in range(out_ref.shape[0]):
        out_ref[l] = jnp.concatenate([table[n, rows * l : rows * (l + 1), :] for n in range(4)], axis=1)


def head_mask(shape_, lanes_each):
    return lax.broadcasted_iota(jnp.int32, shape_, 1) // lanes_each


def place_chunks(refs, full, t):
    count = refs[0].shape[0]
    for d in range(4):
        full[rows_at(t ^ d, count), :] = refs[d][...]


def emit_chunks(part, outs, t):
    count = outs[0].shape[0]
    for d in range(4):
        outs[d][...] = part[rows_at(t ^ d, count), :]


def piece_at(f, j, pieces, size):
    return rows_at(f ^ j, size) if len(pieces) > 1 else slice(0, size)


def emit_heads(h_ref, pieces, pack, outs, idx, plan):
    width = pieces[0].shape[1] // 3
    size = pieces[0].shape[0]
    qkv = sum(
        dot(h_ref[:, piece_at(idx[0], j, pieces, size)], w[...]) for j, w in enumerate(pieces)
    ).astype(bf16)
    for j in range(4):
        q = qkv[:, HD * j : HD * (j + 1)]
        k = qkv[:, width + HD * j : width + HD * (j + 1)]
        v = qkv[:, 2 * width + HD * j : 2 * width + HD * (j + 1)]
        pack[j] = jnp.concatenate([jnp.concatenate([q, k], axis=1), fold(v)], axis=0)
    for d in range(4):
        outs[d][...] = pack[idx[plan.si] ^ d]


def qkv_first_kernel(idx, x_ref, gain_ref, *refs, plan, row):
    *pieces, h_ref, e0, e1, e2, e3, pack = refs
    _, normed = rms(x_ref[...].astype(f32), gain_ref[row : row + 1, :])
    h_ref[...] = normed.astype(bf16)
    emit_heads(h_ref, pieces, pack, (e0, e1, e2, e3), idx, plan)


def qkv_kernel(idx, h0, h1, h2, h3, *refs, plan):
    *pieces, h_ref, e0, e1, e2, e3, pack = refs
    place_chunks((h0, h1, h2, h3), h_ref, idx[plan.ti])
    emit_heads(h_ref, pieces, pack, (e0, e1, e2, e3), idx, plan)


def load_heads(es, kk, vv):
    for d in range(4):
        rows = es[d].shape[0] * 2 // 3
        kk[rows * d : rows * (d + 1), :] = es[d][0:rows, HD : 2 * HD]
        vv[rows * d : rows * (d + 1), :] = unfold(es[d][rows:, :])


def load_ids(col_ref, ids_col, s):
    count = col_ref.shape[0] // 4
    for d in range(4):
        ids_col[count * d : count * (d + 1), :] = col_ref[rows_at(s ^ d, count), :]


def probabilities(kk, q, key_ids, query_ids):
    scores = dot_nt(kk, q) * (HD ** (-0.5))
    scores = jnp.where(key_ids <= query_ids, scores, NEG)
    top = jnp.max(scores, axis=0, keepdims=True)
    exponent = jnp.exp(scores - top)
    return exponent * (1.0 / jnp.sum(exponent, axis=0, keepdims=True))


def attend_kernel(idx, e0, e1, e2, e3, row_ref, col_ref, a0, a1, a2, a3, kk, vv, ids_col, plan):
    es, outs = (e0, e1, e2, e3), (a0, a1, a2, a3)
    s = idx[plan.si]
    load_heads(es, kk, vv)
    load_ids(col_ref, ids_col, s)
    count = kk.shape[0] // 4
    for d in range(4):
        query_ids = row_ref[:, rows_at(s ^ d, count)]
        p = probabilities(kk[...], es[d][0:count, 0:HD], ids_col[...], query_ids)
        blended = dot_tn(vv[...], p.astype(bf16))
        outs[d][...] = fold(blended.T.astype(bf16))


def attend_back_kernel(
    idx, e0, e1, e2, e3, u0, u1, u2, u3, row_ref, col_ref, g0, g1, g2, g3, kk, vv, ids_col, gk, gv, plan
):
    es, us, outs = (e0, e1, e2, e3), (u0, u1, u2, u3), (g0, g1, g2, g3)
    s = idx[plan.si]
    load_heads(es, kk, vv)
    load_ids(col_ref, ids_col, s)
    count = kk.shape[0] // 4
    scale = HD ** (-0.5)
    for d in range(4):
        query_ids = row_ref[:, rows_at(s ^ d, count)]
        q = es[d][0:count, 0:HD]
        up = unfold(us[d][...])
        p = probabilities(kk[...], q, ids_col[...], query_ids)
        gp = dot_nt(vv[...], up)
        centre = jnp.sum(p * gp, axis=0, keepdims=True)
        gs = (p * (gp - centre)).astype(bf16)
        gq = (dot_tn(kk[...], gs) * scale).T.astype(bf16)
        outs[d][0:count, 0:HD] = gq
        key_term = dot(gs, q)
        value_term = dot(p.astype(bf16), up)
        if d == 0:
            gk[...] = key_term
            gv[...] = value_term
        else:
            gk[...] += key_term
            gv[...] += value_term
    for d in range(4):
        outs[d][0:count, HD : 2 * HD] = (gk[count * d : count * (d + 1), :] * scale).astype(bf16)
        outs[d][count:, :] = fold(gv[count * d : count * (d + 1), :].astype(bf16))


def out_kernel(idx, a0, a1, a2, a3, *refs, plan):
    *pieces, a_ref, p0, p1, p2, p3, heads, part = refs
    for d, a in enumerate((a0, a1, a2, a3)):
        heads[idx[plan.si] ^ d] = unfold(a[...])
    a_ref[...] = jnp.concatenate([heads[j] for j in range(4)], axis=1)
    size = pieces[0].shape[1]
    for j, w in enumerate(pieces):
        part[:, piece_at(idx[0], j, pieces, size)] = dot(a_ref[...], w[...]).astype(bf16)
    emit_chunks(part, (p0, p1, p2, p3), idx[plan.ti])


def out_back_kernel(idx, g0, g1, g2, g3, *refs, plan):
    *pieces, go_ref, u0, u1, u2, u3, pack = refs
    place_chunks((g0, g1, g2, g3), go_ref, idx[plan.ti])
    size = pieces[0].shape[1]
    up = sum(
        dot_nt(go_ref[:, piece_at(idx[0], j, pieces, size)], w[...]) for j, w in enumerate(pieces)
    ).astype(bf16)
    for j in range(4):
        pack[j] = fold(up[:, HD * j : HD * (j + 1)])
    for d, u in enumerate((u0, u1, u2, u3)):
        u[...] = pack[idx[plan.si] ^ d]


def qkv_back_kernel(idx, g0, g1, g2, g3, *refs, plan):
    *pieces, g_ref, p0, p1, p2, p3, pack, part = refs
    for d, g in enumerate((g0, g1, g2, g3)):
        pack[idx[plan.si] ^ d] = g[...]
    rows = g_ref.shape[0]
    columns = [pack[j, 0:rows, 0:HD] for j in range(4)]
    columns += [pack[j, 0:rows, HD : 2 * HD] for j in range(4)]
    columns += [unfold(pack[j, rows:, :]) for j in range(4)]
    g_ref[...] = jnp.concatenate(columns, axis=1)
    size = pieces[0].shape[0]
    for j, w in enumerate(pieces):
        part[:, piece_at(idx[0], j, pieces, size)] = dot_nt(g_ref[...], w[...]).astype(bf16)
    emit_chunks(part, (p0, p1, p2, p3), idx[plan.ti])


def to_pack(x):
    rows, width = x.shape
    if width >= 256:
        return jnp.concatenate([x[:, 256 * i : 256 * (i + 1)] for i in range(width // 256)], axis=0)
    fold_by = 256 // width
    rows = rows // fold_by
    return jnp.concatenate([x[rows * i : rows * (i + 1)] for i in range(fold_by)], axis=1)


def from_pack(p, rows, width):
    if width >= 256:
        return jnp.concatenate([p[rows * i : rows * (i + 1)] for i in range(width // 256)], axis=1)
    return jnp.concatenate([p[:, width * i : width * (i + 1)] for i in range(256 // width)], axis=0)


def shard_rows(x, f, shards):
    size = x.shape[0] // shards
    return x[size * f : size * (f + 1)]


def shard_columns(x, f, shards):
    size = x.shape[1] // shards
    return x[:, size * f : size * (f + 1)]


def out_grad_kernel(idx, a_ref, go_ref, pack_ref):
    shards = pack_ref.shape[0]
    change = dot_tn(a_ref[...], go_ref[...])
    for f in range(shards):
        pack_ref[f] = to_pack(shard_columns(change, f, shards)).astype(bf16)


def qkv_grad_kernel(idx, h_ref, g_ref, pack_ref):
    shards = pack_ref.shape[0]
    change = dot_tn(h_ref[...], g_ref[...])
    for f in range(shards):
        pack_ref[f] = to_pack(shard_rows(change, f, shards)).astype(bf16)


def qkv_grad_split_kernel(idx, h_ref, g_ref, mine_ref, other_ref, change):
    change[...] = dot_tn(h_ref[...], g_ref[...])
    size = change.shape[0] // 2
    for j, out in enumerate((mine_ref, other_ref)):
        out[...] = to_pack(change[rows_at(idx[0] ^ j, size), :]).astype(bf16)


def memory_grad_kernel(idx, *refs, plan, has_full):
    forward, back = refs[0:4], refs[4:8]
    full = refs[8] if has_full else None
    pack_ref, h, z, gg, gu, gy = refs[-6:]
    chunk = forward[0].shape[0]
    d_model = h.shape[1]
    quarter = z.shape[1]
    shards = pack_ref.shape[0]
    tables = jnp.zeros((NSUB, 2 * HD), f32)
    for d in range(4):
        at = slice(chunk * d, chunk * (d + 1))
        h[at, :] = forward[d][:, 0:d_model]
        z[at, :] = forward[d][:, d_model:]
        gg[at, :] = back[d][:, 0:quarter]
        gu[at, :] = back[d][:, quarter : quarter + 2 * HD]
        folded = back[d][:, quarter + 2 * HD : quarter + 10 * HD].astype(f32)
        tables = tables + jnp.concatenate(
            [folded[:, 2 * HD * i : 2 * HD * (i + 1)] for i in range(4)], axis=0
        )
        if has_full:
            gy[at, :] = full[rows_at(idx[plan.ti] ^ d, chunk), :]
        else:
            gy[at, :] = back[d][:, quarter + 10 * HD :]
    gate_change = dot_tn(h[...], gg[...])
    look_change = dot_tn(h[...], gu[...])
    mem_change = dot_tn(z[...], gy[...])
    for f in range(shards):
        pack_ref[f] = jnp.concatenate(
            [
                to_pack(shard_rows(gate_change, f, shards)),
                to_pack(shard_columns(mem_change, f, shards)),
                to_pack(shard_rows(look_change, f, shards)),
                to_pack(shard_rows(tables, f, shards)),
            ],
            axis=0,
        ).astype(bf16)


def finalize_kernel(idx, *refs, layers, late):
    count = 3 * layers - 1 + (4 if late else 1)
    packs = refs[:count]
    q_ref, k_ref, v_ref, o_ref, look_ref, gate_ref, mem_ref, first_ref, second_ref, merged = refs[count:]
    part = q_ref.shape[1]
    for l in range(layers):
        if l == 0:
            memory, out = packs[0], packs[1]
            if late:
                chunk = packs[2].shape[0]
                for d in range(4):
                    merged[rows_at(idx[1] ^ d, chunk), :] = packs[2 + d][...]
            else:
                merged[...] = packs[2][...]
            qkv = merged
        else:
            memory, out, qkv = packs[count - 3 * (layers - l) : count - 3 * (layers - l) + 3]
        for n, ref in enumerate((q_ref, k_ref, v_ref)):
            ref[l] = qkv[part * n : part * (n + 1), :].astype(f32)
        o_ref[l] = from_pack(out[...], o_ref.shape[1], o_ref.shape[2]).astype(f32)
        gate_ref[l] = memory[0:part, :].astype(f32)
        mem_ref[l] = from_pack(memory[part : 2 * part, :], mem_ref.shape[1], mem_ref.shape[2]).astype(f32)
        look_ref[l] = from_pack(
            memory[2 * part : 2 * part + part // 2, :].astype(f32), part, look_ref.shape[2]
        )
        tables = from_pack(
            memory[2 * part + part // 2 :, :].astype(f32), first_ref.shape[2], 2 * HD
        )
        first_ref[l, 0] = tables[:, :HD]
        second_ref[l, 0] = tables[:, HD:]


def add_four_kernel(idx, a, b, c, d, out):
    out[...] = total4((a, b, c, d)).astype(out.dtype)


def add_two_kernel(idx, a, b, o0, o1, o2, o3):
    chunk = o0.shape[0]
    for d, out in enumerate((o0, o1, o2, o3)):
        at = rows_at(idx[1] ^ d, chunk)
        out[...] = (a[at, :].astype(f32) + b[at, :].astype(f32)).astype(bf16)


def place_kernel(idx, c0, c1, c2, c3, out_ref, plan):
    chunk = c0.shape[0]
    for d, c in enumerate((c0, c1, c2, c3)):
        out_ref[rows_at(idx[plan.ti] ^ d, chunk), :] = c[...].astype(out_ref.dtype)


def own_rows(ref, idx, plan, count):
    if ref.shape[0] == count:
        return ref[...].astype(f32)
    return ref[rows_at(idx[plan.ti], count), :].astype(f32)


def table_of(a_ref, m, shards):
    size = a_ref.shape[1] * 4 // 5
    both = [a_ref[f * 4 + m, size:, :] for f in range(shards)]
    both = both[0] if shards == 1 else jnp.concatenate(both, axis=0)
    return both[:, :HD], both[:, HD:]


def only_head(x, m, chunk):
    lane = lax.broadcasted_iota(jnp.int32, x.shape, 1)
    return jnp.where((lane >= m * chunk) & (lane < (m + 1) * chunk), x, 0.0)


def lookup_kernel(
    idx, x_ref, p0, r1, r2, r3, gain_ref, a_ref, pick_ref, x_out, h_ref, u_ref, w_ref, out_ref, plan, row, layer, shards
):
    chunk = p0.shape[0]
    x = own_rows(x_ref, idx, plan, chunk) + total4((p0, r1, r2, r3))
    x_out[...] = x
    _, normed = rms(x, gain_ref[row : row + 1, :])
    h_ref[...] = normed.astype(bf16)
    size = a_ref.shape[1] * 4 // 5
    c1, c2 = [], []
    for m in range(4):
        u = sum(
            dot(h_ref[:, size * f : size * (f + 1)], a_ref[f * 4 + m, 0:size, :]) for f in range(shards)
        ).astype(bf16)
        u_ref[:, 2 * HD * m : 2 * HD * (m + 1)] = u
        ka, kb = table_of(a_ref, m, shards)
        c1.append(dot_nt(ka, u[:, :HD]))
        c2.append(dot_nt(kb, u[:, HD:]))
    c1 = jnp.concatenate(c1, axis=1)
    c2 = jnp.concatenate(c2, axis=1)
    lanes = c1.shape[1]
    iota = lax.broadcasted_iota(jnp.int32, (NSUB, lanes), 0)
    for i in range(4):
        first = pick_ref[layer, i : i + 1, :]
        base = jnp.sum(jnp.where(iota == first, c1, 0.0), axis=0, keepdims=True)
        for b in range(8):
            r = i * 8 + b
            second = pick_ref[layer, 8 + r : 9 + r, :]
            picked = jnp.sum(jnp.where(iota == second, c2, 0.0), axis=0, keepdims=True)
            w_ref[r : r + 1, :] = base + picked
    logits = w_ref[...]
    exponent = jnp.exp(logits - jnp.max(logits, axis=0, keepdims=True))
    w = exponent * (1.0 / jnp.sum(exponent, axis=0, keepdims=True))
    w_ref[...] = w
    owners, _, width = out_ref.shape
    slots = lax.broadcasted_iota(jnp.int32, (owners * width, lanes), 0)
    total = jnp.zeros((32, owners * width), f32)
    for i in range(4):
        hit = jnp.where(slots == pick_ref[layer, 4 + i : 5 + i, :], 1.0, 0.0).astype(bf16)
        mine = w[8 * i : 8 * (i + 1), :]
        split = jnp.concatenate([only_head(mine, m, chunk) for m in range(4)], axis=0)
        total = total + dot_nt(split.astype(bf16), hit)
    for d in range(owners):
        out_ref[d] = total[:, d * width : (d + 1) * width].astype(bf16)


def gate_values_kernel(idx, h_ref, wg_ref, gate_ref, shards):
    size = wg_ref.shape[1]
    quarter = wg_ref.shape[2]
    for t in range(4):
        gate_ref[:, quarter * t : quarter * (t + 1)] = sum(
            dot(h_ref[:, size * f : size * (f + 1)], wg_ref[f * 4 + t]) for f in range(shards)
        )


def gate_kernel(
    idx, s0, s1, s2, s3, gate_ref, wp_ref, x_ref, h_ref, gain_ref,
    mem_ref, z_ref, x_out, h_out, f0, f1, f2, f3, plan, row, shards,
):
    mem = total4((s0, s1, s2, s3))
    mem_ref[...] = mem
    gate = gate_ref[...]
    z_ref[...] = (mem * (gate * jax.nn.sigmoid(gate))).astype(bf16)
    quarter, size = wp_ref.shape[1], wp_ref.shape[2]
    for f in range(shards):
        at = slice(size * f, size * (f + 1))
        x_out[:, at] = x_ref[:, at] + sum(
            dot(z_ref[:, quarter * t : quarter * (t + 1)], wp_ref[f * 4 + t]) for t in range(4)
        )
    x = x_out[...]
    if row is None:
        h_out[...] = x.astype(bf16)
    else:
        h_out[...] = rms(x, gain_ref[row : row + 1, :])[1].astype(bf16)
    d_model = x.shape[1]
    for d, f in enumerate((f0, f1, f2, f3)):
        f[:, 0:d_model] = h_ref[...]
        f[:, d_model:] = z_ref[:, rows_at(idx[plan.ti] ^ d, quarter)]


def gate_back(gy_ref, wp_ref, gate_ref, mem_ref, gn_ref, gg_ref, shards):
    quarter, size = wp_ref.shape[1], wp_ref.shape[2]
    for t in range(4):
        at = slice(quarter * t, quarter * (t + 1))
        gz = sum(dot_nt(gy_ref[:, size * f : size * (f + 1)], wp_ref[f * 4 + t]) for f in range(shards))
        gate = gate_ref[:, at]
        sigmoid = jax.nn.sigmoid(gate)
        gn_ref[:, at] = (gz * (gate * sigmoid)).astype(bf16)
        slope = sigmoid * (1.0 + gate * (1.0 - sigmoid))
        gg_ref[:, at] = (gz * mem_ref[:, at] * slope).astype(bf16)


def start_back_kernel(idx, g_ref, wp_ref, gate_ref, mem_ref, gy_ref, gn_ref, gg_ref, plan, shards):
    gy_ref[...] = g_ref[rows_at(idx[plan.ti], gy_ref.shape[0]), :]
    gate_back(gy_ref, wp_ref, gate_ref, mem_ref, gn_ref, gg_ref, shards)


def norm_back(idx, parts, x_ref, g_ref, gain_ref, dgain_ref, plan, row):
    count = parts[0].shape[0]
    upstream = total4(parts)
    x = own_rows(x_ref, idx, plan, count)
    gain = gain_ref[row : row + 1, :]
    factor, _ = rms(x, gain)
    dgain_ref[...] = jnp.sum(upstream * x * factor, axis=0, keepdims=True)
    return g_ref[...] + rms_back(x, factor, gain, upstream)


def norm_back_kernel(
    idx, p0, r1, r2, r3, x_ref, g_ref, gain_ref, wp_ref, gate_ref, mem_ref,
    gx_ref, gy_ref, dgain_ref, gn_ref, gg_ref, plan, row, shards,
):
    gx = norm_back(idx, (p0, r1, r2, r3), x_ref, g_ref, gain_ref, dgain_ref, plan, row)
    gx_ref[...] = gx
    gy_ref[...] = gx.astype(bf16)
    gate_back(gy_ref, wp_ref, gate_ref, mem_ref, gn_ref, gg_ref, shards)


def norm_back_last_kernel(idx, p0, r1, r2, r3, x_ref, g_ref, gain_ref, gx_ref, dgain_ref, plan, row):
    gx = norm_back(idx, (p0, r1, r2, r3), x_ref, g_ref, gain_ref, dgain_ref, plan, row)
    gx_ref[...] = gx.astype(bf16)


def lookup_back_kernel(
    idx, gw_ref, pick_ref, w_ref, a_ref, u_ref, gg_ref, gy_ref, wg_ref, x_ref, g_ref, gain_ref,
    gx_ref, go_ref, dgain_ref, b0, b1, b2, b3, gl, gu_all, tables, gh, plan, row, layer, shards,
):
    chunk = u_ref.shape[0]
    owners, _, width = gw_ref.shape
    lanes = w_ref.shape[1]
    slots = lax.broadcasted_iota(jnp.int32, (owners * width, lanes), 0)
    arrived = jnp.concatenate([gw_ref[d] for d in range(owners)], axis=1)
    for i in range(4):
        hit = jnp.where(slots == pick_ref[layer, 4 + i : 5 + i, :], 1.0, 0.0).astype(bf16)
        mixed = dot(arrived, hit)
        gl[8 * i : 8 * (i + 1), :] = sum(
            only_head(mixed[8 * m : 8 * (m + 1), :], m, chunk) for m in range(4)
        )
    w = w_ref[...]
    gw = gl[...]
    gl[...] = w * (gw - jnp.sum(w * gw, axis=0, keepdims=True))
    iota = lax.broadcasted_iota(jnp.int32, (NSUB, lanes), 0)
    gc1 = jnp.zeros((NSUB, lanes), f32)
    gc2 = jnp.zeros((NSUB, lanes), f32)
    for i in range(4):
        both = jnp.sum(gl[8 * i : 8 * (i + 1), :], axis=0, keepdims=True)
        gc1 = jnp.where(iota == pick_ref[layer, i : i + 1, :], both, gc1)
        for b in range(8):
            r = i * 8 + b
            gc2 = gc2 + jnp.where(iota == pick_ref[layer, 8 + r : 9 + r, :], gl[r : r + 1, :], 0.0)
    gc1 = gc1.astype(bf16)
    gc2 = gc2.astype(bf16)
    for m in range(4):
        ka, kb = table_of(a_ref, m, shards)
        one = gc1[:, chunk * m : chunk * (m + 1)]
        two = gc2[:, chunk * m : chunk * (m + 1)]
        gu_all[:, 2 * HD * m : 2 * HD * (m + 1)] = jnp.concatenate(
            [dot_tn(one, ka), dot_tn(two, kb)], axis=1
        ).astype(bf16)
        change = jnp.concatenate(
            [
                dot(one, u_ref[:, 2 * HD * m : 2 * HD * m + HD]),
                dot(two, u_ref[:, 2 * HD * m + HD : 2 * HD * (m + 1)]),
            ],
            axis=1,
        ).astype(bf16)
        tables[m] = jnp.concatenate(
            [change[NSUB // 4 * n : NSUB // 4 * (n + 1), :] for n in range(4)], axis=1
        )
    size, quarter = wg_ref.shape[1], wg_ref.shape[2]
    for f in range(shards):
        gh[:, size * f : size * (f + 1)] = sum(
            dot_nt(gg_ref[:, quarter * t : quarter * (t + 1)], wg_ref[f * 4 + t])
            + dot_nt(gu_all[:, 2 * HD * t : 2 * HD * (t + 1)], a_ref[f * 4 + t, 0:size, :])
            for t in range(4)
        )
    upstream = gh[...]
    x = x_ref[...]
    gain = gain_ref[row : row + 1, :]
    factor, _ = rms(x, gain)
    dgain_ref[...] = jnp.sum(upstream * x * factor, axis=0, keepdims=True)
    gx = own_rows(g_ref, idx, plan, chunk) + rms_back(x, factor, gain, upstream)
    gx_ref[...] = gx
    go_ref[...] = gx.astype(bf16)
    for d, b in enumerate((b0, b1, b2, b3)):
        n = idx[plan.ti] ^ d
        b[:, 0:quarter] = gg_ref[:, rows_at(n, quarter)]
        b[:, quarter : quarter + 2 * HD] = gu_all[:, rows_at(n, 2 * HD)]
        b[:, quarter + 2 * HD : quarter + 10 * HD] = tables[n]
        if b.shape[1] > quarter + 10 * HD:
            b[:, quarter + 10 * HD :] = gy_ref[...]


STEP_GROUPS = 4


def step_base(idx, step, pieces, per_piece):
    if pieces == 1:
        return step * STEP_GROUPS
    piece = step // per_piece
    return ((idx[0] ^ piece) * per_piece + step % per_piece) * STEP_GROUPS


def read_kernel(idx, w_ref, names_ref, *refs, plan, pieces, per_piece):
    vs = refs[:pieces]
    o0, o1, o2, o3, s_ref, partial, rows = refs[pieces:]
    step = pl.program_id(0)
    sources, _, width = w_ref.shape

    @pl.when(step == 0)
    def _():
        iota = lax.broadcasted_iota(jnp.int32, (NSUB, width), 0).astype(f32)

        def build(sa, carry):
            weights = sum(w_ref[plan.src(sa, ta)].astype(f32) for ta in range(4))
            for m in range(4):
                src = plan.src(sa, m)
                names = names_ref[src].astype(f32)
                dense = jnp.zeros((NSUB, width), f32)
                for b in range(8):
                    r = 8 * m + b
                    dense = jnp.where(iota == names[b : b + 1, :], weights[r : r + 1, :], dense)
                s_ref[src] = dense.T
            return carry

        lax.fori_loop(0, 4, build, 0)

    base = step_base(idx, step, pieces, per_piece)

    def multiply(v_ref):
        for k in range(STEP_GROUPS):
            at = rows_at(base + k, CAP)
            left = s_ref[:, at, :].reshape(sources * CAP, NSUB).astype(bf16)
            got = dot(left, v_ref[NSUB * k : NSUB * (k + 1), :])
            partial[:, at, :] = got.reshape(sources, CAP, v_ref.shape[1])

    for n in range(pieces):
        pl.when(step // per_piece == n)(functools.partial(multiply, vs[n]))

    @pl.when(step == pl.num_programs(0) - 1)
    def _():
        s, t = idx[plan.si], idx[plan.ti]
        tokens = rows.shape[0]
        chunk = tokens // 4
        outs = (o0, o1, o2, o3)
        iota = (lax.broadcasted_iota(jnp.int32, (tokens, width), 0) + 1).astype(f32)
        for ds in range(4):
            hits, parts = [], []
            for m in range(4):
                src = plan.src(s ^ ds, m)
                token = names_ref[src].astype(f32)[8:9, :]
                hits.append(jnp.where(iota == token, 1.0, 0.0).astype(bf16))
                parts.append(partial[src].astype(bf16))
            rows[...] = dot(
                jnp.concatenate(hits, axis=1), jnp.concatenate(parts, axis=0)
            ).astype(bf16)
            for dt in range(4):
                dp, dz = plan.rel(ds, dt)
                outs[dp][chunk * dz : chunk * (dz + 1), :] = rows[rows_at(t ^ dt, chunk), :]


def value_specs(values, layer):
    d_model = values[0].shape[2]
    per_piece = values[0].shape[1] // (STEP_GROUPS * NSUB)
    specs = []
    for n in range(len(values)):
        def index(g, n=n):
            return (layer, jnp.clip(g - n * per_piece, 0, per_piece - 1), 0)

        specs.append(pl.BlockSpec((None, STEP_GROUPS * NSUB, d_model), index))
    return specs, per_piece


def read_call(idx, weights, names, layer, values, plan, tokens):
    sources, inner, width = weights.shape
    specs, per_piece = value_specs(values, layer)
    d_model = values[0].shape[2]
    out = shape((tokens, d_model), bf16)
    return pl.pallas_call(
        functools.partial(read_kernel, plan=plan, pieces=len(values), per_piece=per_piece),
        grid=(per_piece * len(values),),
        out_shape=[out, out, out, out, shape((sources, width, NSUB), f32)],
        in_specs=[
            pl.BlockSpec(memory_space=pltpu.SMEM),
            pl.BlockSpec((sources, inner, width), lambda g: (0, 0, 0)),
            pl.BlockSpec((sources, 16, width), lambda g: (0, layer, 0)),
        ]
        + specs,
        out_specs=[pl.BlockSpec((tokens, d_model), lambda g: (0, 0)) for _ in range(4)]
        + [pl.BlockSpec((sources, width, NSUB), lambda g: (0, 0, 0))],
        scratch_shapes=[
            pltpu.VMEM((sources, width, d_model), f32),
            pltpu.VMEM((tokens, d_model), bf16),
        ],
        compiler_params=pltpu.CompilerParams(vmem_limit_bytes=50 * MIB),
        cost_estimate=pl.CostEstimate(
            flops=4 * sources * width * NSUB * d_model, bytes_accessed=20 * MIB, transcendentals=0
        ),
        name="memory_read",
    )(idx, weights, names, *values)


def write_kernel(idx, g0, g1, g2, g3, names_ref, s_ref, *refs, plan, pieces, per_piece):
    vs, dvs = refs[:pieces], refs[pieces : 2 * pieces]
    gw_ref, grads, partial, cross = refs[2 * pieces :]
    step = pl.program_id(0)
    sources, width, _ = s_ref.shape
    d_model = vs[0].shape[1]

    @pl.when(step == 0)
    def _():
        s, t = idx[plan.si], idx[plan.ti]
        tokens = grads.shape[1]
        chunk = tokens // 4
        for dp, g in enumerate((g0, g1, g2, g3)):
            for dz in range(4):
                ds, dt = plan.rel(dp, dz)
                grads[s ^ ds, rows_at(t ^ dt, chunk), :] = g[chunk * dz : chunk * (dz + 1), :]
        iota = (lax.broadcasted_iota(jnp.int32, (tokens, width), 0) + 1).astype(f32)
        for sa in range(4):
            for m in range(4):
                src = plan.src(sa, m)
                token = names_ref[src].astype(f32)[8:9, :]
                hit = jnp.where(iota == token, 1.0, 0.0).astype(bf16)
                partial[src] = dot_tn(hit, grads[sa])

    base = step_base(idx, step, pieces, per_piece)

    def multiply(v_ref, dv_ref):
        for k in range(STEP_GROUPS):
            at = rows_at(base + k, CAP)
            cut = slice(NSUB * k, NSUB * (k + 1))
            inbox = partial[:, at, :].reshape(sources * CAP, d_model).astype(bf16)
            left = s_ref[:, at, :].reshape(sources * CAP, NSUB).astype(bf16)
            dv_ref[cut, :] = dot_tn(left, inbox).astype(bf16)
            cross[:, at, :] = dot_nt(inbox, v_ref[cut, :]).reshape(sources, CAP, NSUB)

    for n in range(pieces):
        pl.when(step // per_piece == n)(functools.partial(multiply, vs[n], dvs[n]))

    @pl.when(step == pl.num_programs(0) - 1)
    def _():
        iota = lax.broadcasted_iota(jnp.int32, (NSUB, width), 0).astype(f32)

        def select(sa, carry):
            picked = []
            for m in range(4):
                src = plan.src(sa, m)
                turned = cross[src].T
                names = names_ref[src].astype(f32)
                picked += [
                    jnp.sum(jnp.where(iota == names[b : b + 1, :], turned, 0.0), axis=0, keepdims=True)
                    for b in range(8)
                ]
            picked = jnp.concatenate(picked, axis=0).astype(bf16)
            for ta in range(4):
                gw_ref[plan.src(sa, ta)] = picked
            return carry

        lax.fori_loop(0, 4, select, 0)


def write_call(idx, grads, names, layer, dense, values, plan, tokens):
    sources, width, _ = dense.shape
    specs, per_piece = value_specs(values, layer)
    d_model = values[0].shape[2]
    pieces = len(values)

    def dv_spec(n):
        return pl.BlockSpec(
            (STEP_GROUPS * NSUB, d_model), lambda g: (jnp.clip(g - n * per_piece, 0, per_piece - 1), 0)
        )

    return pl.pallas_call(
        functools.partial(write_kernel, plan=plan, pieces=pieces, per_piece=per_piece),
        grid=(per_piece * pieces,),
        out_shape=[shape((v.shape[1], d_model), bf16) for v in values]
        + [shape((sources, 32, width), bf16)],
        in_specs=[pl.BlockSpec(memory_space=pltpu.SMEM)]
        + [pl.BlockSpec((tokens, d_model), lambda g: (0, 0)) for _ in range(4)]
        + [
            pl.BlockSpec((sources, 16, width), lambda g: (0, layer, 0)),
            pl.BlockSpec((sources, width, NSUB), lambda g: (0, 0, 0)),
        ]
        + specs,
        out_specs=[dv_spec(n) for n in range(pieces)]
        + [pl.BlockSpec((sources, 32, width), lambda g: (0, 0, 0))],
        scratch_shapes=[
            pltpu.VMEM((4, tokens, d_model), bf16),
            pltpu.VMEM((sources, width, d_model), f32),
            pltpu.VMEM((sources, width, NSUB), f32),
        ],
        compiler_params=pltpu.CompilerParams(vmem_limit_bytes=56 * MIB),
        cost_estimate=pl.CostEstimate(
            flops=6 * sources * width * NSUB * d_model, bytes_accessed=28 * MIB, transcendentals=0
        ),
        name="memory_write",
    )(idx, *grads, names, dense, *values)


def sum_kernel(idx, m0, r1, r2, r3, o0, o1, o2, o3):
    count = o0.shape[0]
    for dz, out in enumerate((o0, o1, o2, o3)):
        at = slice(count * dz, count * (dz + 1))
        out[...] = (
            (m0[at, :].astype(f32) + r1[at, :].astype(f32))
            + (r2[at, :].astype(f32) + r3[at, :].astype(f32))
        ).astype(bf16)


def table_grad_kernel(a_ref, b_ref, *refs):
    refs[-1][...] = a_ref[...].astype(f32) + b_ref[...].astype(f32)


def table_grad_call(mine, arrived, layer, layers, earlier):
    rows, d_model = mine.shape
    block = min(rows, 512)
    specs = [pl.BlockSpec((block, d_model), lambda g: (g, 0))] * 2
    args = [mine, arrived]
    if earlier is not None:
        specs = specs + [pl.BlockSpec(memory_space=pl.ANY)]
        args.append(earlier)
    return pl.pallas_call(
        table_grad_kernel,
        grid=(rows // block,),
        out_shape=shape((layers, rows, d_model), f32),
        in_specs=specs,
        out_specs=pl.BlockSpec((None, block, d_model), lambda g: (layer, g, 0)),
        input_output_aliases={} if earlier is None else {2: 0},
        compiler_params=pltpu.CompilerParams(vmem_limit_bytes=32 * MIB),
        cost_estimate=pl.CostEstimate(flops=0, bytes_accessed=16 * MIB, transcendentals=0),
        name="table_grad",
    )(*args)


def gather_shards(x, axis):
    if lax.axis_size("fsdp") != 2:
        return lax.all_gather(x, "fsdp", axis=axis, tiled=True)
    other = swap(x, "fsdp", 1)
    mine = lax.axis_index("fsdp") == 0
    return jnp.where(
        mine, jnp.concatenate([x, other], axis=axis), jnp.concatenate([other, x], axis=axis)
    )


def shard_pieces(x, axis):
    if lax.axis_size("fsdp") != 2:
        return [lax.all_gather(x, "fsdp", axis=axis, tiled=True)]
    return [x, swap(x, "fsdp", 1)]


def after(xs, *others):
    return lax.optimization_barrier((tuple(xs), tuple(others)))[0]


def body(
    inputs,
    query_weight,
    key_weight,
    value_weight,
    attention_weight,
    lookup_weight,
    gate_weight,
    memory_weight,
    first_table,
    second_table,
    attention_gain,
    memory_gain,
    memory_values,
    blocks,
    first_picks,
    second_picks,
    cotangent,
):
    plan = PLAN
    SA, TA = plan.SA, plan.TA
    layers = query_weight.shape[0]
    tokens = inputs.shape[1]
    d_model = inputs.shape[2]
    chunk = tokens // 4
    width = query_weight.shape[2]
    shards = lax.axis_size("fsdp")
    owners = lax.axis_size("ctx") * lax.axis_size("tp")
    groups = memory_values.shape[1] // NSUB
    lanes = shards * groups * CAP
    gbits = groups.bit_length() - 1
    dbits = owners.bit_length() - 1
    idx = jnp.stack(
        [lax.axis_index("fsdp"), lax.axis_index("ctx"), lax.axis_index("tp"), 0]
    ).astype(jnp.int32)

    w_qkv, w_o, w_look, w_gate, w_mem = [], [], [], [], []
    for l in range(layers):
        w_qkv.append(
            shard_pieces(
                jnp.concatenate([query_weight[l], key_weight[l], value_weight[l]], axis=1).astype(bf16), 0
            )
        )
        if l == 0:
            gains = gather_shards(
                jnp.concatenate([attention_gain, memory_gain], axis=0).astype(bf16), 1
            ).astype(f32)
        w_o.append(shard_pieces(attention_weight[l].astype(bf16), 1))
        look = jnp.concatenate(
            [lookup_weight[l], jnp.concatenate([first_table[l, 0], second_table[l, 0]], axis=1)], axis=0
        ).astype(bf16)
        w_look.append(lax.all_gather(look, ("fsdp", "tp"), axis=0, tiled=False))
        w_gate.append(lax.all_gather(gate_weight[l].astype(bf16), ("fsdp", "tp"), axis=0, tiled=False))
        w_mem.append(lax.all_gather(memory_weight[l].astype(bf16), ("fsdp", "tp"), axis=0, tiled=False))
    values = [memory_values]
    if shards == 2:
        values.append(swap(memory_values, "fsdp", 1))
    else:
        values = [lax.all_gather(memory_values, "fsdp", axis=1, tiled=True)]

    ids_row = blocks
    ids_col = blocks.reshape(-1, 1)
    heads_shape = shape((tokens * 3 // 2, 2 * HD), bf16)
    folded = shape((tokens // 2, 2 * HD), bf16)
    part_shape = shape((chunk, d_model), bf16)
    chunk_shape = shape((chunk, d_model), f32)
    full_shape = shape((tokens, d_model), bf16)
    gain_shape = shape((1, d_model), f32)
    forward_shape = shape((chunk, d_model + width), bf16)
    pack_scratch = pltpu.VMEM((4, tokens * 3 // 2, 2 * HD), bf16)
    part_scratch = pltpu.VMEM((tokens, d_model), bf16)
    kv_scratch = [
        pltpu.VMEM((4 * tokens, HD), bf16),
        pltpu.VMEM((4 * tokens, HD), bf16),
        pltpu.VMEM((4 * tokens, 1), jnp.int32),
    ]
    x = inputs[0]
    h_chunk = None
    names = table = None
    kept = []
    for l in range(layers):
        if l == 0:
            h1, *es = kernel_call(
                functools.partial(qkv_first_kernel, plan=plan, row=l),
                "qkv_first",
                [full_shape] + [heads_shape] * 4,
                idx,
                [x, gains, *w_qkv[l]],
                [pack_scratch],
            )
            firsts, seconds = after((first_picks, second_picks), es[0])
            firsts = jnp.swapaxes(firsts[:, 0, 0], 1, 2)
            seconds = jnp.swapaxes(seconds[:, 0, 0].reshape(layers, tokens, -1), 1, 2)
            height = layers * (8 + seconds.shape[1])
            outbox, *tables = kernel_call(
                functools.partial(slots_kernel, plan=plan, gbits=gbits, dbits=dbits),
                "pick_slots",
                [shape((owners, 16 * layers, lanes), bf16)] + [shape((height, chunk), jnp.int32)] * 4,
                idx,
                [firsts, seconds],
                [pltpu.VMEM((4, height, chunk), jnp.int32)],
            )
            (table,) = kernel_call(
                functools.partial(pick_table_kernel, plan=plan),
                "pick_table",
                [shape((layers, height // layers, tokens), jnp.int32)],
                idx,
                swaps(tables, TA),
                [pltpu.VMEM((4, height, chunk), jnp.int32)],
            )
        else:
            h1, *es = kernel_call(
                functools.partial(qkv_kernel, plan=plan),
                "qkv",
                [full_shape] + [heads_shape] * 4,
                idx,
                [*spread(h_chunk, TA), *w_qkv[l]],
                [pack_scratch],
            )
        es = swaps(es, SA)
        if l > 0:
            tied = after([*es, *kept[-1][-1]])
            es = list(tied[:4])
            kept[-1] = kept[-1][:-1] + (list(tied[4:]),)
        heads = kernel_call(
            functools.partial(attend_kernel, plan=plan),
            "attend",
            [folded] * 4,
            idx,
            [*es, ids_row, ids_col],
            kv_scratch,
        )
        attended, *parts = kernel_call(
            functools.partial(out_kernel, plan=plan),
            "attend_out",
            [shape((tokens, width), bf16)] + [part_shape] * 4,
            idx,
            [*swaps(heads, SA), *w_o[l]],
            [pltpu.VMEM((4, tokens, HD), bf16), part_scratch],
        )
        if l == 0:
            (outbox,) = after((outbox,), parts[0])
            names = lax.all_to_all(outbox, ("ctx", "tp"), 0, 0, tiled=True)
        middle, h2, u, w, outbox = kernel_call(
            functools.partial(lookup_kernel, plan=plan, row=layers + l, layer=l, shards=shards),
            "lookup",
            [
                chunk_shape,
                part_shape,
                shape((chunk, 8 * HD), bf16),
                shape((32, tokens), f32),
                shape((owners, 32, lanes), bf16),
            ],
            idx,
            [x, *swaps(parts, TA), gains, w_look[l], table],
        )
        weights = lax.all_to_all(outbox, ("ctx", "tp"), 0, 0, tiled=True)
        (gate,) = kernel_call(
            functools.partial(gate_values_kernel, shards=shards),
            "gate_values",
            [chunk_shape],
            idx,
            [h2, w_gate[l]],
        )
        *reads, dense = read_call(idx, weights, names, l, values, plan, tokens)
        sums = kernel_call(sum_kernel, "memory_sum", [part_shape] * 4, idx, swaps(reads, "ctx"))
        last = l + 1 == layers
        mem, z, x3, h_chunk, *messages = kernel_call(
            functools.partial(gate_kernel, plan=plan, row=None if last else l + 1, shards=shards),
            "gate",
            [chunk_shape, part_shape, chunk_shape, part_shape] + [forward_shape] * 4,
            idx,
            [*swaps(sums, "tp"), gate, w_mem[l], middle, h2, gains],
        )
        kept.append((x, h1, es, attended, middle, u, w, gate, dense, mem, swaps(messages, TA)))
        x = x3
    out_chunks = spread(h_chunk, TA)

    g = cotangent[0]
    packs = [None] * layers
    gain_rows = [None] * (2 * layers)
    table_grads = None
    table_list = [None] * layers
    gy = gn = gg = None
    output = None
    for l in reversed(range(layers)):
        x, h1, es, attended, middle, u, w, gate, dense, mem, messages = kept[l]
        top = l == layers - 1
        if top:
            gy, gn, gg = kernel_call(
                functools.partial(start_back_kernel, plan=plan, shards=shards),
                "start_back",
                [part_shape] * 3,
                idx,
                [g, w_mem[l], gate, mem],
            )
        line = jnp.concatenate(spread(gn, "tp"), axis=0)
        *dvs, gw = write_call(idx, spread(line, "ctx"), names, l, dense, values, plan, tokens)
        if top:
            gw, *out_chunks = after([gw, *out_chunks])
            (output,) = kernel_call(
                functools.partial(place_kernel, plan=plan), "output", [full_shape], idx, out_chunks
            )
        gw = lax.all_to_all(gw, ("ctx", "tp"), 0, 0, tiled=True)
        back_shape = shape((chunk, width + 10 * HD + (0 if top else d_model)), bf16)
        g_mid, go_chunk, gain_rows[layers + l], *back = kernel_call(
            functools.partial(lookup_back_kernel, plan=plan, row=layers + l, layer=l, shards=shards),
            "lookup_back",
            [chunk_shape, part_shape, gain_shape] + [back_shape] * 4,
            idx,
            [gw, table, w, w_look[l], u, gg, gy, w_gate[l], middle, g, gains],
            [
                pltpu.VMEM(w.shape, f32),
                pltpu.VMEM(u.shape, bf16),
                pltpu.VMEM((4, NSUB // 4, 8 * HD), bf16),
                pltpu.VMEM((chunk, d_model), f32),
            ],
        )
        go, *ups = kernel_call(
            functools.partial(out_back_kernel, plan=plan),
            "attend_out_back",
            [full_shape] + [folded] * 4,
            idx,
            [*spread(go_chunk, TA), *w_o[l]],
            [pltpu.VMEM((4, tokens // 2, 2 * HD), bf16)],
        )
        shard_size = d_model // shards
        (memory_pack,) = kernel_call(
            functools.partial(memory_grad_kernel, plan=plan, has_full=top),
            "memory_grad",
            [shape((shards, shard_size * 5 // 2 + NSUB // shards // 2, 256), bf16)],
            idx,
            [*messages, *swaps(back, TA)] + ([cotangent[0]] if top else []),
            [
                pltpu.VMEM((tokens, d_model), bf16),
                pltpu.VMEM((tokens, width), bf16),
                pltpu.VMEM((tokens, width), bf16),
                pltpu.VMEM((tokens, 2 * HD), bf16),
                pltpu.VMEM((tokens, d_model), bf16),
            ],
        )
        (out_pack,) = kernel_call(
            out_grad_kernel, "out_grad", [shape((shards, shard_size, 256), bf16)], idx, [attended, go]
        )
        head_grads = kernel_call(
            functools.partial(attend_back_kernel, plan=plan),
            "attend_back",
            [heads_shape] * 4,
            idx,
            [*es, *swaps(ups, SA), ids_row, ids_col],
            kv_scratch + [pltpu.VMEM((4 * tokens, HD), f32)] * 2,
        )
        g_qkv, *parts = kernel_call(
            functools.partial(qkv_back_kernel, plan=plan),
            "qkv_back",
            [shape((tokens, 3 * width), bf16)] + [part_shape] * 4,
            idx,
            [*swaps(head_grads, SA), *w_qkv[l]],
            [pack_scratch, part_scratch],
        )
        if l > 0:
            below = kept[l - 1]
            g, gy, gain_rows[l], gn, gg = kernel_call(
                functools.partial(norm_back_kernel, plan=plan, row=l, shards=shards),
                "norm_back",
                [chunk_shape, part_shape, gain_shape, part_shape, part_shape],
                idx,
                [*swaps(parts, TA), x, g_mid, gains, w_mem[l - 1], below[7], below[9]],
            )
        else:
            g, gain_rows[l] = kernel_call(
                functools.partial(norm_back_last_kernel, plan=plan, row=l),
                "norm_back_last",
                [part_shape, gain_shape],
                idx,
                [*swaps(parts, TA), x, g_mid, gains],
            )
        qkv_rows = 3 * shard_size
        if l == 0 and shards == 2:
            mine, other = kernel_call(
                qkv_grad_split_kernel,
                "qkv_grad",
                [shape((qkv_rows, 256), bf16)] * 2,
                idx,
                [h1, g_qkv],
                [pltpu.VMEM((d_model, 3 * width), f32)],
            )
            quarter = shape((qkv_rows // 4, 256), bf16)
            parts = kernel_call(
                add_two_kernel, "qkv_add", [quarter] * 4, idx, [mine, swap(other, "fsdp", 1)]
            )
            (part,) = kernel_call(add_four_kernel, "qkv_sum", [quarter], idx, swaps(parts, "ctx"))
            late = spread(part, "ctx")
            group = (memory_pack, out_pack)
        else:
            (pack,) = kernel_call(
                qkv_grad_kernel, "qkv_grad", [shape((shards, qkv_rows, 256), bf16)], idx, [h1, g_qkv]
            )
            late = []
            group = (memory_pack, out_pack, pack)
        if l + 1 < layers:
            group = after(group, *packs[l + 1])
        scattered = [lax.psum_scatter(p, "fsdp", scatter_dimension=0, tiled=False) for p in group]
        packs[l] = [lax.psum(p, "ctx") for p in scattered] + late
        if shards == 2:
            arrived = swap(dvs[1], "fsdp", 1)
            table_grads = table_grad_call(dvs[0], arrived, l, layers, table_grads)
        else:
            table_list[l] = lax.psum_scatter(dvs[0], "fsdp", scatter_dimension=0, tiled=True).astype(f32)
    (input_gradient,) = kernel_call(
        functools.partial(place_kernel, plan=plan),
        "input_gradient",
        [shape((tokens, d_model), f32)],
        idx,
        spread(g, TA),
    )
    if shards != 2:
        table_grads = jnp.stack(table_list)
    gain_all = jnp.concatenate(gain_rows, axis=0)
    for axis in ("tp", "ctx"):
        arrived = spread(gain_all, axis)
        gain_all = (arrived[0] + arrived[1]) + (arrived[2] + arrived[3])
    gain_all = lax.psum_scatter(gain_all, "fsdp", scatter_dimension=1, tiled=True) if shards != 2 else (
        lax.dynamic_slice_in_dim(gain_all + swap(gain_all, "fsdp", 1), idx[0] * (d_model // 2), d_model // 2, 1)
    )
    shard_size = d_model // shards
    tall = shape((layers, shard_size, width), f32)
    wide = shape((layers, width, shard_size), f32)
    sub = shape((layers, 1, NSUB // shards, HD), f32)
    flat = [p for l in range(layers) for p in packs[l]]
    grads = kernel_call(
        functools.partial(finalize_kernel, layers=layers, late=len(packs[0]) > 3),
        "finalize",
        [tall, tall, tall, wide, shape((layers, shard_size, 2 * HD), f32), tall, wide, sub, sub],
        idx,
        flat,
        [pltpu.VMEM((3 * shard_size, 256), bf16)],
        limit=48,
    )
    return (
        output[None],
        input_gradient[None],
        *grads,
        gain_all[:layers],
        gain_all[layers:],
        table_grads,
    )


def solution(mesh):
    placed = (
        P("fsdp", "ctx", None),
        P(None, "fsdp", "tp"),
        P(None, "fsdp", "tp"),
        P(None, "fsdp", "tp"),
        P(None, "tp", "fsdp"),
        P(None, "fsdp", "tp"),
        P(None, "fsdp", "tp"),
        P(None, "tp", "fsdp"),
        P(None, "tp", "fsdp", None),
        P(None, "tp", "fsdp", None),
        P(None, "fsdp"),
        P(None, "fsdp"),
        P(None, ("fsdp", "ctx", "tp"), None),
        P("fsdp", None),
        P(None, "fsdp", "tp", "ctx", None),
        P(None, "fsdp", "tp", "ctx", None, None),
        P("fsdp", "ctx", None),
    )
    return jax.shard_map(
        body,
        mesh=mesh,
        in_specs=placed,
        out_specs=(
            P("fsdp", "ctx", None),
            P("fsdp", "ctx", None),
            P(None, "fsdp", "tp"),
            P(None, "fsdp", "tp"),
            P(None, "fsdp", "tp"),
            P(None, "tp", "fsdp"),
            P(None, "fsdp", "tp"),
            P(None, "fsdp", "tp"),
            P(None, "tp", "fsdp"),
            P(None, "tp", "fsdp", None),
            P(None, "tp", "fsdp", None),
            P(None, "fsdp"),
            P(None, "fsdp"),
            P(None, ("fsdp", "ctx", "tp"), None),
        ),
        check_vma=False,
    )
```

time: 801 us -> 694 us (0.87)
  blocking collectives: 93 us -> 37.4 us
  other arithmetic: 58 us -> 6.77 us
  waiting for transfers between devices: 273 us -> 239 us
  local copies, waits for them, and re-layouts: 55.1 us -> 84.4 us
  Pallas kernels: 130 us -> 149 us
  matrix products: 15.7 us -> 0 us
    reduce_scatter x8 -> x5, waiting for transfers between devices: 50.9 us -> 0.02 us  [body(): lax.psum_scatter(p, 'fsdp', scatter_dimension=0, tiled=False)]
    ppermute x109 -> x112, waiting for transfers between devices: 187 us -> 225 us  [swap(): return lax.ppermute(x, axis, [(i, i ^ step) for i in range(size)])]
    psum x2 -> x0, blocking collectives: 36.9 us -> none  [body(): lax.psum(lax.psum_scatter(p, 'fsdp', scatter_dimension=axis, tiled=True),...]
    all_gather x2 -> x0, blocking collectives: 32.6 us -> none  [the longest x1 17.2 us: body(): output = lax.all_gather(out_chunk, TA, axis=0, tiled=True)[None]]
    unnamed x304 -> x382, local copies, waits for them, and re-layouts: 47 us -> 79.6 us
    pallas_call x32 -> x38, Pallas kernels: 60.8 us -> 86.6 us  [kernel_call(): pl.pallas_call(body, out_shape=outs, in_specs=in_specs, out_specs=[pl.Blo...]
    select_n x12 -> x0, other arithmetic: 21.8 us -> none  [gather_shards(): jnp.where(mine, jnp.concatenate([x, other], axis=axis), jnp.concatenate([...]
    psum x2, waiting for transfers between devices: 21.2 us -> 3.58 us  [body(): packs[l] = [lax.psum(p, 'ctx') for p in scattered] + late]
  transfers between devices with their start and end apart: 125 -> 127, of which waited for: 74 -> 69; matrix products, arithmetic and copies ran while one was open for 10% -> 2% of each run, Pallas kernels for 10% -> 20%
where the time goes in v2:
time: 694 us; the launch traced here: 684 us
  waiting for transfers between devices  239 us (34%)
  starting transfers between devices  152 us (22%)
  Pallas kernels  149 us (21%)
  local copies, waits for them, and re-layouts  84.4 us (12%)
  blocking collectives  37.4 us (5%)
  between operations  15.9 us (2%)
    ppermute x112, waiting for transfers between devices, swap(): return lax.ppermute(x, axis, [(i, i ^ step) for i in range(size)])  225 us
    ppermute x112, starting transfers between devices, swap(): return lax.ppermute(x, axis, [(i, i ^ step) for i in range(size)])  139 us
    pallas_call x38, Pallas kernels, kernel_call(): pl.pallas_call(body, out_shape=outs, in_specs=in_specs, out_specs=[pl.Blo...  86.6 us
    unnamed x382, local copies, waits for them, and re-layouts  79.6 us
    pallas_call x2, Pallas kernels, write_call(): pl.pallas_call(functools.partial(write_kernel, plan=plan, pieces=pieces,...  30.2 us
    all_to_all x2, blocking collectives, body(): gw = lax.all_to_all(gw, ('ctx', 'tp'), 0, 0, tiled=True)  25.4 us
    pallas_call x2, Pallas kernels, read_call(): pl.pallas_call(functools.partial(read_kernel, plan=plan, pieces=len(value...  19.1 us
  transfers between devices with their start and end apart: 127, of which 69 were waited for; matrix products, arithmetic and copies ran while one was open for 2% of the time, Pallas kernels for 20%

profile of v2, /device:TPU:0, one launch (start us, length us, event | category | flops | bytes accessed | tf_op | source)
XLA Modules:
  0.0 684.3 jit_solution(2334042451842988635)
XLA Ops:
  21.1 6.8 collective-permute-done
  80.8 12.8 %collective-permute-done.13.t2 = s32[80,64]{1,0:T(8,128)S(1)} collective-permute-done((s32[80,64]{1,0:T(8,128)}, s32[80,64]{1,0:T(8,128)S(1)}, u32[]{:S(2)}, u32[]{:S(2)}) %collective-permute-start.13) | collective-permute-done | bytes 20512 | tf_op jit(solution)/shard_map/ppermute | solution.py:34
  115.0 6.3 all-to-all-start
  122.6 9.0 %all-to-all-done.w_ref = bf16[16,32,128]{2,1,0:T(8,128)(2,1)S(1)} async-done(((bf16[16,32,128]{2,1,0:T(8,128)(2,1)}), bf16[16,32,128]{2,1,0:T(8,128)(2,1)S(1)}, u32[]{:S(2)}, u32[]{:S(2)}) %all-to-all-start) | async-done | bytes 131104 | tf_op jit(solution)/shard_map/all_to_all | solution.py:1081
  131.6 9.7 %memory_read.2 = (bf16[256,1024]{1,0:T(8,128)(2,1)S(1)}, bf16[256,1024]{1,0:T(8,128)(2,1)S(1)}, bf16[256,1024]{1,0:T(8,128)(2,1)S(1)}, bf16[256,1024]{1,0:T(8,128)(2,1)S(1)}, f32[16,128,256]{2,1,0:T(8,128)}) custom-call(s32[4]{0:T(128)S(1)} %pad_add_fusion.idx, bf16[16,32,128]{2,1,0:T(8,128)(2,1)S(1)} %all-to-all-done.w_ref, ...), custom_call_target="tpu_custom_call" | custom-call | flops 2147483648 | bytes 20971520 | tf_op jit(solution)/shard_map/memory_read/pallas_call | solution.py:748
  144.8 7.8 %collective-permute-done.16.r1 = bf16[256,1024]{1,0:T(8,128)(2,1)S(1)} collective-permute-done((bf16[256,1024]{1,0:T(8,128)(2,1)S(1)}, bf16[256,1024]{1,0:T(8,128)(2,1)S(1)}, u32[]{:S(2)}, u32[]{:S(2)}) %collective-permute-start.16) | collective-permute-done | bytes 524320 | tf_op jit(solution)/shard_map/ppermute | solution.py:34
  152.6 7.0 %collective-permute-done.17.r2 = bf16[256,1024]{1,0:T(8,128)(2,1)S(1)} collective-permute-done((bf16[256,1024]{1,0:T(8,128)(2,1)S(1)}, bf16[256,1024]{1,0:T(8,128)(2,1)S(1)}, u32[]{:S(2)}, u32[]{:S(2)}) %collective-permute-start.17) | collective-permute-done | bytes 524320 | tf_op jit(solution)/shard_map/ppermute | solution.py:34
  190.6 18.6 %collective-permute-done.23.h2 = bf16[64,1024]{1,0:T(8,128)(2,1)S(1)} collective-permute-done((bf16[64,1024]{1,0:T(8,128)(2,1)S(1)}, bf16[64,1024]{1,0:T(8,128)(2,1)S(1)}, u32[]{:S(2)}, u32[]{:S(2)}) %collective-permute-start.23) | collective-permute-done | bytes 131104 | tf_op jit(solution)/shard_map/ppermute | solution.py:34
  255.2 12.0 %all_to_all.25.w_ref = bf16[16,32,128]{2,1,0:T(8,128)(2,1)S(1)} all-to-all(bf16[16,32,128]{2,1,0:T(8,128)(2,1)S(1)} %get-tuple-element.233), channel_id=1, replica_groups=mesh['fsdp'=2,'ctx'=4,'tp'=4] {'ctx','tp'}, dimensions={0} | all-to-all | bytes 262144 | tf_op jit(solution)/shard_map/all_to_all | solution.py:1081
  267.2 9.4 %memory_read.3 = (bf16[256,1024]{1,0:T(8,128)(2,1)S(1)}, bf16[256,1024]{1,0:T(8,128)(2,1)S(1)}, bf16[256,1024]{1,0:T(8,128)(2,1)S(1)}, bf16[256,1024]{1,0:T(8,128)(2,1)S(1)}, f32[16,128,256]{2,1,0:T(8,128)}) custom-call(s32[4]{0:T(128)S(1)} %copy-done.49, bf16[16,32,128]{2,1,0:T(8,128)(2,1)S(1)} %all_to_all.25.w_ref, ...), custom_call_target="tpu_custom_call" | custom-call | flops 2147483648 | bytes 20971520 | tf_op jit(solution)/shard_map/memory_read/pallas_call | solution.py:748
  280.2 7.5 %collective-permute-done.39.r1 = bf16[256,1024]{1,0:T(8,128)(2,1)S(1)} collective-permute-done((bf16[256,1024]{1,0:T(8,128)(2,1)S(1)}, bf16[256,1024]{1,0:T(8,128)(2,1)S(1)}, u32[]{:S(2)}, u32[]{:S(2)}) %collective-permute-start.39) | collective-permute-done | bytes 524320 | tf_op jit(solution)/shard_map/ppermute | solution.py:34
  287.7 6.2 collective-permute-done.40.r2
  320.1 9.6 %collective-permute-done.46 = bf16[64,1024]{1,0:T(8,128)(2,1)S(1)} collective-permute-done((bf16[64,1024]{1,0:T(8,128)(2,1)S(1)}, bf16[64,1024]{1,0:T(8,128)(2,1)S(1)}, u32[]{:S(2)}, u32[]{:S(2)}) %collective-permute-start.46) | collective-permute-done | bytes 131104 | tf_op jit(solution)/shard_map/ppermute | solution.py:34
  347.2 14.9 %memory_write.2 = (bf16[2048,1024]{1,0:T(8,128)(2,1)}, bf16[2048,1024]{1,0:T(8,128)(2,1)}, bf16[16,32,128]{2,1,0:T(8,128)(2,1)}) custom-call(s32[4]{0:T(128)} %copy-done.46, bf16[256,1024]{1,0:T(8,128)(2,1)} %copy-done.176, bf16[256,1024]{1,0:T(8,128)(2,1)} %copy-done.180, bf16[256,1024]{1,0:T(8,128)(2,1)} %copy-done.179, bf16[256,1024]{1,0:T(8,128)(2,1)} %copy-done.178, ...), custom_call_target="tpu_custom_call" | custom-call | flops 3221225472 | bytes 29360128 | tf_op jit(solution)/shard_map/memory_write/pallas_call | solution.py:843
  362.9 11.9 %all_to_all.26.gw_ref = bf16[16,32,128]{2,1,0:T(8,128)(2,1)S(1)} all-to-all(bf16[16,32,128]{2,1,0:T(8,128)(2,1)} %get-tuple-element.252), channel_id=1, replica_groups=mesh['fsdp'=2,'ctx'=4,'tp'=4] {'ctx','tp'}, dimensions={0} | all-to-all | bytes 262144 | tf_op jit(solution)/shard_map/all_to_all | solution.py:1128
  390.0 6.8 collective-permute-done.55.g2
  477.6 6.6 collective-permute-done.67
  487.8 10.7 %collective-permute-done.71.g3 = bf16[256,1024]{1,0:T(8,128)(2,1)S(1)} collective-permute-done((bf16[256,1024]{1,0:T(8,128)(2,1)S(1)}, bf16[256,1024]{1,0:T(8,128)(2,1)S(1)}, u32[]{:S(2)}, u32[]{:S(2)}) %collective-permute-start.71) | collective-permute-done | bytes 524320 | tf_op jit(solution)/shard_map/ppermute | solution.py:34
  504.7 15.3 %memory_write.3 = (bf16[2048,1024]{1,0:T(8,128)(2,1)}, bf16[2048,1024]{1,0:T(8,128)(2,1)}, bf16[16,32,128]{2,1,0:T(8,128)(2,1)}) custom-call(s32[4]{0:T(128)} %copy-done.46, bf16[256,1024]{1,0:T(8,128)(2,1)} %copy-done.177, bf16[256,1024]{1,0:T(8,128)(2,1)} %copy-done.183, bf16[256,1024]{1,0:T(8,128)(2,1)} %copy-done.182, bf16[256,1024]{1,0:T(8,128)(2,1)} %copy-done.181, ...), custom_call_target="tpu_custom_call" | custom-call | flops 3221225472 | bytes 29360128 | tf_op jit(solution)/shard_map/memory_write/pallas_call | solution.py:843
  519.9 13.4 %all_to_all.27.gw_ref = bf16[16,32,128]{2,1,0:T(8,128)(2,1)S(1)} all-to-all(bf16[16,32,128]{2,1,0:T(8,128)(2,1)} %get-tuple-element.274), channel_id=1, replica_groups=mesh['fsdp'=2,'ctx'=4,'tp'=4] {'ctx','tp'}, dimensions={0} | all-to-all | bytes 262144 | tf_op jit(solution)/shard_map/all_to_all | solution.py:1128
  547.2 11.7 %collective-permute-done.73.g2 = bf16[64,1024]{1,0:T(8,128)(2,1)S(1)} collective-permute-done((bf16[64,1024]{1,0:T(8,128)(2,1)S(1)}, bf16[64,1024]{1,0:T(8,128)(2,1)S(1)}, u32[]{:S(2)}, u32[]{:S(2)}) %collective-permute-start.73) | collective-permute-done | bytes 131104 | tf_op jit(solution)/shard_map/ppermute | solution.py:34
  594.2 8.3 %collective-permute-done.82.r2 = bf16[64,1024]{1,0:T(8,128)(2,1)S(1)} collective-permute-done((bf16[64,1024]{1,0:T(8,128)(2,1)S(1)}, bf16[64,1024]{1,0:T(8,128)(2,1)S(1)}, u32[]{:S(2)}, u32[]{:S(2)}) %collective-permute-start.82) | collective-permute-done | bytes 131104 | tf_op jit(solution)/shard_map/ppermute | solution.py:34
  650.6 6.7 table_grad.2.refs_0_
  657.4 6.4 table_grad.3
  (705 shorter events, 433.0 us)
Async XLA Ops:
  7.2 96.4 %all-gather.9.cloned.1.call-start = ((), (), s32[]{:S(2)}) async-start(), calls=%async_computation.11 | async-start | bytes 1474560 | tf_op jit(solution)/shard_map/all_gather | solution.py:976
  11.2 154.9 %all-gather.11.cloned.1.call-start = ((), (), s32[]{:S(2)}) async-start(), calls=%async_computation.12 | async-start | bytes 2359296 | tf_op jit(solution)/shard_map/all_gather | solution.py:977
  12.1 158.2 %all-gather.13.cloned.1.call-start = ((), (), s32[]{:S(2)}) async-start(), calls=%async_computation.13 | async-start | bytes 2359296 | tf_op jit(solution)/shard_map/all_gather | solution.py:978
  13.1 224.5 %all-gather.15.cloned.1.call-start = ((), (), s32[]{:S(2)}) async-start(), calls=%async_computation.14 | async-start | bytes 1474560 | tf_op jit(solution)/shard_map/all_gather | solution.py:976
  13.2 118.4 %collective-permute-start.15 = (bf16[2,2048,1024]{2,1,0:T(8,128)(2,1)}, bf16[2,2048,1024]{2,1,0:T(8,128)(2,1)}, u32[]{:S(2)}, u32[]{:S(2)}) collective-permute-start(bf16[2,2048,1024]{2,1,0:T(8,128)(2,1)} %refs_0_.7), channel_id=1, source_target_pairs={{0,16},{16,0},{1,17},{17,1},{2,18},{18,2},{3,19},{19,3},{4,20},{20... | collective-permute-start | bytes 25165832 | tf_op jit(solution)/shard_map/ppermute | solution.py:34
  14.5 285.9 %all-gather.17.cloned.1.call-start = ((), (), s32[]{:S(2)}) async-start(), calls=%async_computation.15 | async-start | bytes 2359296 | tf_op jit(solution)/shard_map/all_gather | solution.py:977
  15.1 289.6 %all-gather.7.cloned.1.call-start = ((), (), s32[]{:S(2)}) async-start(), calls=%async_computation.10 | async-start | bytes 2359296 | tf_op jit(solution)/shard_map/all_gather | solution.py:978
  21.0 34.3 %collective-permute-start.8 = (bf16[256,512]{1,0:T(8,128)(2,1)S(1)}, bf16[256,512]{1,0:T(8,128)(2,1)S(1)}, u32[]{:S(2)}, u32[]{:S(2)}) collective-permute-start(bf16[256,512]{1,0:T(8,128)(2,1)S(1)} %get-tuple-element.394.refs_0_), channel_id=1, source_target_pairs={{0,16},{16,0},{1,17},{17,1},{2,18},{18,2},{3,19},{19,3},{4,20},{20... | collective-permute-start | bytes 786440 | tf_op jit(solution)/shard_map/ppermute | solution.py:34
  60.2 54.8 %all-to-all-start.1 = ((bf16[16,32,128]{2,1,0:T(8,128)(2,1)}), bf16[16,32,128]{2,1,0:T(8,128)(2,1)S(1)}, u32[]{:S(2)}, u32[]{:S(2)}) async-start(bf16[16,32,128]{2,1,0:T(8,128)(2,1)} %copy-done.116), calls=%async_computation.1 | async-start | bytes 262144 | tf_op jit(solution)/shard_map/all_to_all | solution.py:1067
  66.0 35.6 %collective-permute-start.9 = (bf16[64,1024]{1,0:T(8,128)(2,1)}, bf16[64,1024]{1,0:T(8,128)(2,1)S(1)}, u32[]{:S(2)}, u32[]{:S(2)}) collective-permute-start(bf16[64,1024]{1,0:T(8,128)(2,1)} %copy-done.157), channel_id=1, source_target_pairs={{0,1},{1,0},{2,3},{3,2},{4,5},{5,4},{6,7},{7,6},{8,9},{9,8},{10,11... | collective-permute-start | bytes 393224 | tf_op jit(solution)/shard_map/ppermute | solution.py:34
  68.1 34.2 %collective-permute-start.10 = (bf16[64,1024]{1,0:T(8,128)(2,1)}, bf16[64,1024]{1,0:T(8,128)(2,1)S(1)}, u32[]{:S(2)}, u32[]{:S(2)}) collective-permute-start(bf16[64,1024]{1,0:T(8,128)(2,1)} %copy-done.156), channel_id=1, source_target_pairs={{0,2},{1,3},{2,0},{3,1},{4,6},{5,7},{6,4},{7,5},{8,10},{9,11},{10,... | collective-permute-start | bytes 393224 | tf_op jit(solution)/shard_map/ppermute | solution.py:34
  70.5 32.5 %collective-permute-start.11 = (bf16[64,1024]{1,0:T(8,128)(2,1)}, bf16[64,1024]{1,0:T(8,128)(2,1)S(1)}, u32[]{:S(2)}, u32[]{:S(2)}) collective-permute-start(bf16[64,1024]{1,0:T(8,128)(2,1)} %copy-done.155), channel_id=1, source_target_pairs={{0,3},{1,2},{2,1},{3,0},{4,7},{5,6},{6,5},{7,4},{8,11},{9,10},{10,... | collective-permute-start | bytes 393224 | tf_op jit(solution)/shard_map/ppermute | solution.py:34
  121.3 354.8 %reduce-scatter.8.cloned.1.call-start = ((), (), s32[]{:S(2)}) async-start(), calls=%async_computation.17 | async-start | bytes 786432 | tf_op jit(solution)/shard_map/reduce_scatter | solution.py:1227
  122.5 63.0 %collective-permute-start.25 = (bf16[512,768]{1,0:T(8,128)(2,1)S(1)}, bf16[512,768]{1,0:T(8,128)(2,1)S(1)}, u32[]{:S(2)}, u32[]{:S(2)}) collective-permute-start(bf16[512,768]{1,0:T(8,128)(2,1)S(1)} %pad_maximum_fusion.1.refs_0_), channel_id=1, source_target_pairs={{0,16},{16,0},{1,17},{17,1},{2,18},{18,2},{3,19},{19,3},{4,20},{20... | collective-permute-start | bytes 2359304 | tf_op jit(solution)/shard_map/ppermute | solution.py:34
  190.6 37.3 %collective-permute-start.35 = (bf16[256,512]{1,0:T(8,128)(2,1)S(1)}, bf16[256,512]{1,0:T(8,128)(2,1)S(1)}, u32[]{:S(2)}, u32[]{:S(2)}) collective-permute-start(bf16[256,512]{1,0:T(8,128)(2,1)S(1)} %copy-done.23), channel_id=1, source_target_pairs={{0,16},{16,0},{1,17},{17,1},{2,18},{18,2},{3,19},{19,3},{4,20},{20... | collective-permute-start | bytes 786440 | tf_op jit(solution)/shard_map/ppermute | solution.py:34
  401.3 74.8 %reduce-scatter.6.cloned.1.call-start = ((), (), s32[]{:S(2)}) async-start(), calls=%async_computation.16 | async-start | bytes 2064384 | tf_op jit(solution)/shard_map/reduce_scatter | solution.py:1227
  421.1 55.0 %reduce-scatter.10.cloned.1.call-start = ((), (), s32[]{:S(2)}) async-start(), calls=%async_computation.18 | async-start | bytes 2359296 | tf_op jit(solution)/shard_map/reduce_scatter | solution.py:1227
  452.6 111.9 %all-reduce.7.cloned.1.call-start = ((), (), s32[]{:S(2)}) async-start(), calls=%async_computation.22 | async-start | bytes 3473408 | tf_op jit(solution)/shard_map/psum | solution.py:1228
  476.2 134.8 %reduce-scatter.14.cloned.1.call-start = ((), (), s32[]{:S(2)}) async-start(), calls=%async_computation.20 | async-start | bytes 786432 | tf_op jit(solution)/shard_map/reduce_scatter | solution.py:1227
  564.5 46.4 %reduce-scatter.12.cloned.1.call-start = ((), (), s32[]{:S(2)}) async-start(), calls=%async_computation.19 | async-start | bytes 2064384 | tf_op jit(solution)/shard_map/reduce_scatter | solution.py:1227
  564.6 83.9 %collective-permute-start.111 = (bf16[2048,1024]{1,0:T(8,128)(2,1)}, bf16[2048,1024]{1,0:T(8,128)(2,1)}, u32[]{:S(2)}, u32[]{:S(2)}) collective-permute-start(bf16[2048,1024]{1,0:T(8,128)(2,1)} %get-tuple-element.343), channel_id=1, source_target_pairs={{0,16},{16,0},{1,17},{17,1},{2,18},{18,2},{3,19},{19,3},{4,20},{20... | collective-permute-start | bytes 12582920 | tf_op jit(solution)/shard_map/ppermute | solution.py:34
  564.7 92.7 %collective-permute-start.110 = (bf16[2048,1024]{1,0:T(8,128)(2,1)}, bf16[2048,1024]{1,0:T(8,128)(2,1)}, u32[]{:S(2)}, u32[]{:S(2)}) collective-permute-start(bf16[2048,1024]{1,0:T(8,128)(2,1)} %get-tuple-element.341), channel_id=1, source_target_pairs={{0,16},{16,0},{1,17},{17,1},{2,18},{18,2},{3,19},{19,3},{4,20},{20... | collective-permute-start | bytes 12582920 | tf_op jit(solution)/shard_map/ppermute | solution.py:34
  565.2 102.1 %all-reduce.5.cloned.1.call-start = ((), (), s32[]{:S(2)}) async-start(), calls=%async_computation.21 | async-start | bytes 1900544 | tf_op jit(solution)/shard_map/psum | solution.py:1228
  589.7 32.0 %collective-permute-start.96 = (bf16[1536,256]{1,0:T(8,128)(2,1)}, bf16[1536,256]{1,0:T(8,128)(2,1)S(1)}, u32[]{:S(2)}, u32[]{:S(2)}) collective-permute-start(bf16[1536,256]{1,0:T(8,128)(2,1)} %get-tuple-element.322), channel_id=1, source_target_pairs={{0,16},{16,0},{1,17},{17,1},{2,18},{18,2},{3,19},{19,3},{4,20},{20... | collective-permute-start | bytes 2359304 | tf_op jit(solution)/shard_map/ppermute | solution.py:34
  (289 other events, 3704.5 us)
Sparse Core Ops, SparseCore 0:
  11.3 26.2 all-gather.8
  39.7 28.4 all-gather.10
  70.4 33.4 all-gather.12
  105.4 25.8 all-gather.14
  133.3 28.2 all-gather.16
  163.6 47.9 all-gather.6
  401.4 5.4 reduce-scatter.7
  421.2 6.6 reduce-scatter.5
  452.7 6.8 reduce-scatter.9
  476.3 71.6 all-reduce.6
  564.7 9.1 reduce-scatter.13
  575.9 12.5 reduce-scatter.11
  611.1 56.1 all-reduce.4

commit v3 on v2

--- a/solution.py
+++ b/solution.py
@@ -46,12 +46,12 @@
     return jax.ShapeDtypeStruct(dims, dtype)
 
 
-def kernel_call(body, name, outs, idx, args, scratch=(), limit=32, flops=0):
+def kernel_call(body, name, outs, idx, args, scratch=(), limit=50, flops=0):
     in_specs = [pl.BlockSpec(memory_space=pltpu.SMEM)]
     in_specs += [pl.BlockSpec(memory_space=pltpu.VMEM) for _ in args]
     moved = sum(a.size * a.dtype.itemsize for a in args)
     moved += sum(o.size * o.dtype.itemsize for o in outs)
-    return pl.pallas_call(
+    out = pl.pallas_call(
         body,
         out_shape=outs,
         in_specs=in_specs,
@@ -61,6 +61,7 @@
         cost_estimate=pl.CostEstimate(flops=flops, bytes_accessed=moved, transcendentals=0),
         name=name,
     )(idx, *args)
+    return list(out)
 
 
 def rows_at(index, count):
@@ -342,99 +343,98 @@
     return x[:, size * f : size * (f + 1)]
 
 
-def out_grad_kernel(idx, a_ref, go_ref, pack_ref):
-    shards = pack_ref.shape[0]
-    change = dot_tn(a_ref[...], go_ref[...])
-    for f in range(shards):
-        pack_ref[f] = to_pack(shard_columns(change, f, shards)).astype(bf16)
-
-
-def qkv_grad_kernel(idx, h_ref, g_ref, pack_ref):
-    shards = pack_ref.shape[0]
+def emit_shards(pack, outs, idx):
+    if len(outs) == 1:
+        outs[0][...] = pack[...]
+    else:
+        outs[0][...] = pack[idx[0]]
+        outs[1][...] = pack[idx[0] ^ 1]
+
+
+def qkv_grad_kernel(idx, h_ref, g_ref, *refs):
+    *outs, pack = refs
+    shards = pack.shape[0]
     change = dot_tn(h_ref[...], g_ref[...])
     for f in range(shards):
-        pack_ref[f] = to_pack(shard_rows(change, f, shards)).astype(bf16)
-
-
-def qkv_grad_split_kernel(idx, h_ref, g_ref, mine_ref, other_ref, change):
-    change[...] = dot_tn(h_ref[...], g_ref[...])
-    size = change.shape[0] // 2
-    for j, out in enumerate((mine_ref, other_ref)):
-        out[...] = to_pack(change[rows_at(idx[0] ^ j, size), :]).astype(bf16)
-
-
-def memory_grad_kernel(idx, *refs, plan, has_full):
-    forward, back = refs[0:4], refs[4:8]
+        pack[f] = to_pack(shard_rows(change, f, shards)).astype(bf16)
+    emit_shards(pack, outs, idx)
+
+
+def weight_grad_kernel(idx, *refs, plan, has_full):
+    forward, back, near, (a_ref, go_ref) = refs[0], refs[1], refs[2:6], refs[6:8]
     full = refs[8] if has_full else None
-    pack_ref, h, z, gg, gu, gy = refs[-6:]
-    chunk = forward[0].shape[0]
+    *outs, pack, h, z, gg, gu, gy = refs[8 + has_full :]
+    chunk = forward.shape[1]
     d_model = h.shape[1]
     quarter = z.shape[1]
-    shards = pack_ref.shape[0]
+    shards = pack.shape[0]
     tables = jnp.zeros((NSUB, 2 * HD), f32)
+    mine = rows_at(idx[plan.ti], quarter)
     for d in range(4):
         at = slice(chunk * d, chunk * (d + 1))
-        h[at, :] = forward[d][:, 0:d_model]
-        z[at, :] = forward[d][:, d_model:]
-        gg[at, :] = back[d][:, 0:quarter]
-        gu[at, :] = back[d][:, quarter : quarter + 2 * HD]
-        folded = back[d][:, quarter + 2 * HD : quarter + 10 * HD].astype(f32)
+        h[at, :] = forward[d, :, 0:d_model]
+        z[at, :] = forward.at[:, :, d_model:][d, :, mine]
+        gg[at, :] = back.at[:, :, 0:d_model][d, :, mine]
+        gu[rows_at(idx[plan.ti] ^ d, chunk), :] = near[d][:, 0 : 2 * HD]
+        folded = near[d][:, 2 * HD :].astype(f32)
         tables = tables + jnp.concatenate(
             [folded[:, 2 * HD * i : 2 * HD * (i + 1)] for i in range(4)], axis=0
         )
-        if has_full:
-            gy[at, :] = full[rows_at(idx[plan.ti] ^ d, chunk), :]
-        else:
-            gy[at, :] = back[d][:, quarter + 10 * HD :]
+        gy[at, :] = full[at, :] if has_full else back[d, :, d_model:]
     gate_change = dot_tn(h[...], gg[...])
     look_change = dot_tn(h[...], gu[...])
     mem_change = dot_tn(z[...], gy[...])
+    out_change = dot_tn(a_ref[...], go_ref[...])
     for f in range(shards):
-        pack_ref[f] = jnp.concatenate(
+        pack[f] = jnp.concatenate(
             [
                 to_pack(shard_rows(gate_change, f, shards)),
                 to_pack(shard_columns(mem_change, f, shards)),
                 to_pack(shard_rows(look_change, f, shards)),
                 to_pack(shard_rows(tables, f, shards)),
+                to_pack(shard_columns(out_change, f, shards)),
             ],
             axis=0,
         ).astype(bf16)
+    emit_shards(pack, outs, idx)
 
 
 def finalize_kernel(idx, *refs, layers, late):
-    count = 3 * layers - 1 + (4 if late else 1)
-    packs = refs[:count]
-    q_ref, k_ref, v_ref, o_ref, look_ref, gate_ref, mem_ref, first_ref, second_ref, merged = refs[count:]
+    ins = refs[: 2 * layers + 3 * late]
+    outs = refs[2 * layers + 3 * late :]
+    q_ref, k_ref, v_ref, o_ref, look_ref, gate_ref, mem_ref, first_ref, second_ref = outs[:9]
     part = q_ref.shape[1]
     for l in range(layers):
-        if l == 0:
-            memory, out = packs[0], packs[1]
-            if late:
-                chunk = packs[2].shape[0]
-                for d in range(4):
-                    merged[rows_at(idx[1] ^ d, chunk), :] = packs[2 + d][...]
-            else:
-                merged[...] = packs[2][...]
-            qkv = merged
+        memory = ins[l]
+        if l > 0 or not late:
+            qkv = ins[layers + l - late]
         else:
-            memory, out, qkv = packs[count - 3 * (layers - l) : count - 3 * (layers - l) + 3]
+            one_ref, two_ref, qkv = outs[9:]
+            rows = qkv.shape[0] // 4
+            total = 0.0
+            for d in range(4):
+                chunk = ins[2 * layers - 1 + d]
+                qkv[rows_at(idx[1] ^ d, rows), :] = chunk[0:rows, :]
+                total = total + chunk[rows:, :].astype(f32)
+            total = jnp.concatenate([total[0:8], total[8:16]], axis=1)
+            one_ref[...] = total[0:layers]
+            two_ref[...] = total[layers : 2 * layers]
         for n, ref in enumerate((q_ref, k_ref, v_ref)):
             ref[l] = qkv[part * n : part * (n + 1), :].astype(f32)
-        o_ref[l] = from_pack(out[...], o_ref.shape[1], o_ref.shape[2]).astype(f32)
         gate_ref[l] = memory[0:part, :].astype(f32)
         mem_ref[l] = from_pack(memory[part : 2 * part, :], mem_ref.shape[1], mem_ref.shape[2]).astype(f32)
-        look_ref[l] = from_pack(
-            memory[2 * part : 2 * part + part // 2, :].astype(f32), part, look_ref.shape[2]
-        )
-        tables = from_pack(
-            memory[2 * part + part // 2 :, :].astype(f32), first_ref.shape[2], 2 * HD
-        )
-        first_ref[l, 0] = tables[:, :HD]
-        second_ref[l, 0] = tables[:, HD:]
-
-
-def add_four_kernel(idx, a, b, c, d, out):
-    out[...] = total4((a, b, c, d)).astype(out.dtype)
+        at = 2 * part + part // 2
+        look_ref[l] = from_pack(memory[2 * part : at, :].astype(f32), part, look_ref.shape[2])
+        rows = first_ref.shape[3]
+        tables = from_pack(memory[at : at + rows // 2, :].astype(f32), rows, 2 * HD)
+        first_ref[l, 0] = tables[:, :HD].T
+        second_ref[l, 0] = tables[:, HD:].T
+        at = at + rows // 2
+        o_ref[l] = from_pack(memory[at : at + part, :], o_ref.shape[1], o_ref.shape[2]).astype(f32)
+
+
+def add_pair_kernel(idx, a, b, out):
+    out[...] = (a[...].astype(f32) + b[...].astype(f32)).astype(bf16)
 
 
 def add_two_kernel(idx, a, b, o0, o1, o2, o3):
@@ -444,10 +444,10 @@
         out[...] = (a[at, :].astype(f32) + b[at, :].astype(f32)).astype(bf16)
 
 
-def place_kernel(idx, c0, c1, c2, c3, out_ref, plan):
-    chunk = c0.shape[0]
-    for d, c in enumerate((c0, c1, c2, c3)):
-        out_ref[rows_at(idx[plan.ti] ^ d, chunk), :] = c[...].astype(out_ref.dtype)
+def plane_sum_kernel(idx, a0, a1, a2, a3, g0, g1, out):
+    rows = a0.shape[0]
+    out[0:rows, :] = total4((a0, a1, a2, a3)).astype(bf16)
+    out[rows:, :] = (g0[...].astype(f32) + g1[...].astype(f32)).astype(bf16)
 
 
 def own_rows(ref, idx, plan, count):
@@ -469,8 +469,9 @@
 
 
 def lookup_kernel(
-    idx, x_ref, p0, r1, r2, r3, gain_ref, a_ref, pick_ref, x_out, h_ref, u_ref, w_ref, out_ref, plan, row, layer, shards
+    idx, x_ref, p0, r1, r2, r3, gain_ref, a_ref, pick_ref, *refs, plan, row, layer, shards
 ):
+    *names_ref, x_out, h_ref, u_ref, w_ref, out_ref = refs
     chunk = p0.shape[0]
     x = own_rows(x_ref, idx, plan, chunk) + total4((p0, r1, r2, r3))
     x_out[...] = x
@@ -511,58 +512,78 @@
         split = jnp.concatenate([only_head(mine, m, chunk) for m in range(4)], axis=0)
         total = total + dot_nt(split.astype(bf16), hit)
     for d in range(owners):
-        out_ref[d] = total[:, d * width : (d + 1) * width].astype(bf16)
-
-
-def gate_values_kernel(idx, h_ref, wg_ref, gate_ref, shards):
-    size = wg_ref.shape[1]
-    quarter = wg_ref.shape[2]
+        out_ref[d, 0:32, :] = total[:, d * width : (d + 1) * width].astype(bf16)
+        if names_ref:
+            out_ref[d, 32:, :] = names_ref[0][d]
+
+
+def gate_part(b_ref, n):
+    return b_ref[n, 0 : b_ref.shape[1] // 2, :]
+
+
+def memory_part(b_ref, n):
+    size = b_ref.shape[1] // 2
+    return from_pack(b_ref[n, size:, :], b_ref.shape[2], size)
+
+
+def gate_values_kernel(idx, h_ref, b_ref, gate_ref, shards):
+    size, quarter = b_ref.shape[1] // 2, b_ref.shape[2]
     for t in range(4):
         gate_ref[:, quarter * t : quarter * (t + 1)] = sum(
-            dot(h_ref[:, size * f : size * (f + 1)], wg_ref[f * 4 + t]) for f in range(shards)
-        )
-
-
-def gate_kernel(
-    idx, s0, s1, s2, s3, gate_ref, wp_ref, x_ref, h_ref, gain_ref,
-    mem_ref, z_ref, x_out, h_out, f0, f1, f2, f3, plan, row, shards,
-):
-    mem = total4((s0, s1, s2, s3))
+            dot(h_ref[:, size * f : size * (f + 1)], gate_part(b_ref, f * 4 + t)) for f in range(shards)
+        )
+
+
+def gate_sum(sums, gate_ref, b_ref, x_ref, mem_ref, z_ref, x_out, shards):
+    mem = total4(sums)
     mem_ref[...] = mem
     gate = gate_ref[...]
     z_ref[...] = (mem * (gate * jax.nn.sigmoid(gate))).astype(bf16)
-    quarter, size = wp_ref.shape[1], wp_ref.shape[2]
+    size, quarter = b_ref.shape[1] // 2, b_ref.shape[2]
     for f in range(shards):
         at = slice(size * f, size * (f + 1))
         x_out[:, at] = x_ref[:, at] + sum(
-            dot(z_ref[:, quarter * t : quarter * (t + 1)], wp_ref[f * 4 + t]) for t in range(4)
-        )
-    x = x_out[...]
-    if row is None:
-        h_out[...] = x.astype(bf16)
-    else:
-        h_out[...] = rms(x, gain_ref[row : row + 1, :])[1].astype(bf16)
-    d_model = x.shape[1]
-    for d, f in enumerate((f0, f1, f2, f3)):
-        f[:, 0:d_model] = h_ref[...]
-        f[:, d_model:] = z_ref[:, rows_at(idx[plan.ti] ^ d, quarter)]
-
-
-def gate_back(gy_ref, wp_ref, gate_ref, mem_ref, gn_ref, gg_ref, shards):
-    quarter, size = wp_ref.shape[1], wp_ref.shape[2]
+            dot(z_ref[:, quarter * t : quarter * (t + 1)], memory_part(b_ref, f * 4 + t)) for t in range(4)
+        )
+
+
+def gate_kernel(
+    idx, s0, s1, s2, s3, gate_ref, b_ref, x_ref, h_ref, gain_ref, mem_ref, box_ref, x_out, h_out, z, row, shards
+):
+    gate_sum((s0, s1, s2, s3), gate_ref, b_ref, x_ref, mem_ref, z, x_out, shards)
+    h_out[...] = rms(x_out[...], gain_ref[row : row + 1, :])[1].astype(bf16)
+    fill_box(box_ref, h_ref, z)
+
+
+def fill_box(box_ref, left_ref, right_ref):
+    width = left_ref.shape[1]
+    box_ref[:, 0:width] = left_ref[...]
+    box_ref[:, width:] = right_ref[...]
+
+
+def gate_last_kernel(
+    idx, s0, s1, s2, s3, gate_ref, b_ref, x_ref, h_ref, g_ref,
+    n_ref, box_ref, back_ref, mem, z, x_out, gy, plan, shards,
+):
+    gate_sum((s0, s1, s2, s3), gate_ref, b_ref, x_ref, mem, z, x_out, shards)
+    gy[...] = g_ref[rows_at(idx[plan.ti], gy.shape[0]), :]
+    gate_back(gy, b_ref, gate_ref, mem, n_ref, back_ref, shards)
+    back_ref[:, gy.shape[1] :] = x_out[...].astype(bf16)
+    fill_box(box_ref, h_ref, z)
+
+
+def gate_back(gy_ref, b_ref, gate_ref, mem_ref, gn_ref, gg_ref, shards):
+    size, quarter = b_ref.shape[1] // 2, b_ref.shape[2]
     for t in range(4):
         at = slice(quarter * t, quarter * (t + 1))
-        gz = sum(dot_nt(gy_ref[:, size * f : size * (f + 1)], wp_ref[f * 4 + t]) for f in range(shards))
+        gz = sum(
+            dot_nt(gy_ref[:, size * f : size * (f + 1)], memory_part(b_ref, f * 4 + t)) for f in range(shards)
+        )
         gate = gate_ref[:, at]
         sigmoid = jax.nn.sigmoid(gate)
         gn_ref[:, at] = (gz * (gate * sigmoid)).astype(bf16)
         slope = sigmoid * (1.0 + gate * (1.0 - sigmoid))
         gg_ref[:, at] = (gz * mem_ref[:, at] * slope).astype(bf16)
-
-
-def start_back_kernel(idx, g_ref, wp_ref, gate_ref, mem_ref, gy_ref, gn_ref, gg_ref, plan, shards):
-    gy_ref[...] = g_ref[rows_at(idx[plan.ti], gy_ref.shape[0]), :]
-    gate_back(gy_ref, wp_ref, gate_ref, mem_ref, gn_ref, gg_ref, shards)
 
 
 def norm_back(idx, parts, x_ref, g_ref, gain_ref, dgain_ref, plan, row):
@@ -576,22 +597,41 @@
 
 
 def norm_back_kernel(
-    idx, p0, r1, r2, r3, x_ref, g_ref, gain_ref, wp_ref, gate_ref, mem_ref,
-    gx_ref, gy_ref, dgain_ref, gn_ref, gg_ref, plan, row, shards,
+    idx, p0, r1, r2, r3, x_ref, g_ref, gain_ref, b_ref, gate_ref, mem_ref,
+    gx_ref, dgain_ref, gn_ref, back_ref, gy, plan, row, shards,
 ):
     gx = norm_back(idx, (p0, r1, r2, r3), x_ref, g_ref, gain_ref, dgain_ref, plan, row)
     gx_ref[...] = gx
-    gy_ref[...] = gx.astype(bf16)
-    gate_back(gy_ref, wp_ref, gate_ref, mem_ref, gn_ref, gg_ref, shards)
-
-
-def norm_back_last_kernel(idx, p0, r1, r2, r3, x_ref, g_ref, gain_ref, gx_ref, dgain_ref, plan, row):
-    gx = norm_back(idx, (p0, r1, r2, r3), x_ref, g_ref, gain_ref, dgain_ref, plan, row)
-    gx_ref[...] = gx.astype(bf16)
+    gy[...] = gx.astype(bf16)
+    gate_back(gy, b_ref, gate_ref, mem_ref, gn_ref, back_ref, shards)
+    back_ref[:, gy.shape[1] :] = gy[...]
+
+
+def norm_back_last_kernel(idx, p0, r1, r2, r3, x_ref, g_ref, gain_ref, *refs, plan, row):
+    *rows, out_ref, dgain = refs
+    gx = norm_back(idx, (p0, r1, r2, r3), x_ref, g_ref, gain_ref, dgain, plan, row)
+    count = gx.shape[0]
+    out_ref[0:count, :] = gx.astype(bf16)
+    both = [dgain[...]] + [r[...] for r in rows]
+    blank = jnp.zeros((out_ref.shape[0] - count - len(both), gx.shape[1]), f32)
+    out_ref[count:, :] = jnp.concatenate(both + [blank], axis=0).astype(bf16)
+
+
+def input_grad_kernel(idx, c0, c1, c2, c3, out_ref, gain_ref, mine_ref, other_ref, plan):
+    chunk = out_ref.shape[0] // 4
+    total = 0.0
+    for d, c in enumerate((c0, c1, c2, c3)):
+        out_ref[rows_at(idx[plan.ti] ^ d, chunk), :] = c[0:chunk, :].astype(f32)
+        total = total + c[chunk:, :].astype(f32)
+    gain_ref[...] = total
+    size = gain_ref.shape[1] // 2
+    for j, out in enumerate((mine_ref, other_ref)):
+        half = gain_ref[:, rows_at(idx[0] ^ j, size)]
+        out[...] = jnp.concatenate([half[:8, 0:256], half[:8, 256:]], axis=0).astype(bf16)
 
 
 def lookup_back_kernel(
-    idx, gw_ref, pick_ref, w_ref, a_ref, u_ref, gg_ref, gy_ref, wg_ref, x_ref, g_ref, gain_ref,
+    idx, gw_ref, pick_ref, w_ref, a_ref, u_ref, gg_ref, b_ref, x_ref, g_ref, gain_ref,
     gx_ref, go_ref, dgain_ref, b0, b1, b2, b3, gl, gu_all, tables, gh, plan, row, layer, shards,
 ):
     chunk = u_ref.shape[0]
@@ -636,10 +676,10 @@
         tables[m] = jnp.concatenate(
             [change[NSUB // 4 * n : NSUB // 4 * (n + 1), :] for n in range(4)], axis=1
         )
-    size, quarter = wg_ref.shape[1], wg_ref.shape[2]
+    size, quarter = b_ref.shape[1] // 2, b_ref.shape[2]
     for f in range(shards):
         gh[:, size * f : size * (f + 1)] = sum(
-            dot_nt(gg_ref[:, quarter * t : quarter * (t + 1)], wg_ref[f * 4 + t])
+            dot_nt(gg_ref[:, quarter * t : quarter * (t + 1)], gate_part(b_ref, f * 4 + t))
             + dot_nt(gu_all[:, 2 * HD * t : 2 * HD * (t + 1)], a_ref[f * 4 + t, 0:size, :])
             for t in range(4)
         )
@@ -651,13 +691,10 @@
     gx = own_rows(g_ref, idx, plan, chunk) + rms_back(x, factor, gain, upstream)
     gx_ref[...] = gx
     go_ref[...] = gx.astype(bf16)
-    for d, b in enumerate((b0, b1, b2, b3)):
+    for d, out in enumerate((b0, b1, b2, b3)):
         n = idx[plan.ti] ^ d
-        b[:, 0:quarter] = gg_ref[:, rows_at(n, quarter)]
-        b[:, quarter : quarter + 2 * HD] = gu_all[:, rows_at(n, 2 * HD)]
-        b[:, quarter + 2 * HD : quarter + 10 * HD] = tables[n]
-        if b.shape[1] > quarter + 10 * HD:
-            b[:, quarter + 10 * HD :] = gy_ref[...]
+        out[:, 0 : 2 * HD] = gu_all[:, rows_at(n, 2 * HD)]
+        out[:, 2 * HD : 10 * HD] = tables[n]
 
 
 STEP_GROUPS = 4
@@ -741,7 +778,7 @@
 
 
 def read_call(idx, weights, names, layer, values, plan, tokens):
-    sources, inner, width = weights.shape
+    sources, _, width = weights.shape
     specs, per_piece = value_specs(values, layer)
     d_model = values[0].shape[2]
     out = shape((tokens, d_model), bf16)
@@ -751,8 +788,8 @@
         out_shape=[out, out, out, out, shape((sources, width, NSUB), f32)],
         in_specs=[
             pl.BlockSpec(memory_space=pltpu.SMEM),
-            pl.BlockSpec((sources, inner, width), lambda g: (0, 0, 0)),
-            pl.BlockSpec((sources, 16, width), lambda g: (0, layer, 0)),
+            pl.BlockSpec((sources, 32, width), lambda g: (0, 0, 0)),
+            pl.BlockSpec((sources, 16, width), lambda g: (0, 2 + layer, 0)),
         ]
         + specs,
         out_specs=[pl.BlockSpec((tokens, d_model), lambda g: (0, 0)) for _ in range(4)]
@@ -787,11 +824,13 @@
                 grads[s ^ ds, rows_at(t ^ dt, chunk), :] = g[chunk * dz : chunk * (dz + 1), :]
         iota = (lax.broadcasted_iota(jnp.int32, (tokens, width), 0) + 1).astype(f32)
         for sa in range(4):
+            hits = []
             for m in range(4):
-                src = plan.src(sa, m)
-                token = names_ref[src].astype(f32)[8:9, :]
-                hit = jnp.where(iota == token, 1.0, 0.0).astype(bf16)
-                partial[src] = dot_tn(hit, grads[sa])
+                token = names_ref[plan.src(sa, m)].astype(f32)[8:9, :]
+                hits.append(jnp.where(iota == token, 1.0, 0.0).astype(bf16))
+            got = dot_tn(jnp.concatenate(hits, axis=1), grads[sa])
+            for m in range(4):
+                partial[plan.src(sa, m)] = got[width * m : width * (m + 1), :]
 
     base = step_base(idx, step, pieces, per_piece)
 
@@ -846,10 +885,13 @@
         out_shape=[shape((v.shape[1], d_model), bf16) for v in values]
         + [shape((sources, 32, width), bf16)],
         in_specs=[pl.BlockSpec(memory_space=pltpu.SMEM)]
-        + [pl.BlockSpec((tokens, d_model), lambda g: (0, 0)) for _ in range(4)]
         + [
-            pl.BlockSpec((sources, 16, width), lambda g: (0, layer, 0)),
-            pl.BlockSpec((sources, width, NSUB), lambda g: (0, 0, 0)),
+            pl.BlockSpec((tokens, d_model), lambda g: (0, 0), pipeline_mode=pl.Buffered(1))
+            for _ in range(4)
+        ]
+        + [
+            pl.BlockSpec((sources, 16, width), lambda g: (0, 2 + layer, 0)),
+            pl.BlockSpec((sources, width, NSUB), lambda g: (0, 0, 0), pipeline_mode=pl.Buffered(1)),
         ]
         + specs,
         out_specs=[dv_spec(n) for n in range(pieces)]
@@ -859,7 +901,7 @@
             pltpu.VMEM((sources, width, d_model), f32),
             pltpu.VMEM((sources, width, NSUB), f32),
         ],
-        compiler_params=pltpu.CompilerParams(vmem_limit_bytes=56 * MIB),
+        compiler_params=pltpu.CompilerParams(vmem_limit_bytes=50 * MIB),
         cost_estimate=pl.CostEstimate(
             flops=6 * sources * width * NSUB * d_model, bytes_accessed=28 * MIB, transcendentals=0
         ),
@@ -918,8 +960,13 @@
     return [x, swap(x, "fsdp", 1)]
 
 
+def reduce_packs(group):
+    scattered = [lax.psum_scatter(p, "fsdp", scatter_dimension=0, tiled=False) for p in group]
+    return [lax.psum(p, "ctx") for p in scattered]
+
+
 def after(xs, *others):
-    return lax.optimization_barrier((tuple(xs), tuple(others)))[0]
+    return list(lax.optimization_barrier((tuple(xs), tuple(others)))[0])
 
 
 def body(
@@ -958,30 +1005,32 @@
         [lax.axis_index("fsdp"), lax.axis_index("ctx"), lax.axis_index("tp"), 0]
     ).astype(jnp.int32)
 
-    w_qkv, w_o, w_look, w_gate, w_mem = [], [], [], [], []
-    for l in range(layers):
-        w_qkv.append(
-            shard_pieces(
-                jnp.concatenate([query_weight[l], key_weight[l], value_weight[l]], axis=1).astype(bf16), 0
-            )
-        )
-        if l == 0:
-            gains = gather_shards(
-                jnp.concatenate([attention_gain, memory_gain], axis=0).astype(bf16), 1
-            ).astype(f32)
-        w_o.append(shard_pieces(attention_weight[l].astype(bf16), 1))
-        look = jnp.concatenate(
-            [lookup_weight[l], jnp.concatenate([first_table[l, 0], second_table[l, 0]], axis=1)], axis=0
-        ).astype(bf16)
-        w_look.append(lax.all_gather(look, ("fsdp", "tp"), axis=0, tiled=False))
-        w_gate.append(lax.all_gather(gate_weight[l].astype(bf16), ("fsdp", "tp"), axis=0, tiled=False))
-        w_mem.append(lax.all_gather(memory_weight[l].astype(bf16), ("fsdp", "tp"), axis=0, tiled=False))
-    values = [memory_values]
-    if shards == 2:
-        values.append(swap(memory_values, "fsdp", 1))
-    else:
-        values = [lax.all_gather(memory_values, "fsdp", axis=1, tiled=True)]
-
+    gains = gather_shards(
+        jnp.concatenate([attention_gain, memory_gain], axis=0).astype(bf16), 1
+    ).astype(f32)
+
+    def qkv_weight(l, queries, keys, values_):
+        joined = jnp.concatenate([queries[l], keys[l], values_[l]], axis=1).astype(bf16)
+        return shard_pieces(joined, 0)
+
+    def gather_all(x):
+        return lax.all_gather(x, ("fsdp", "tp"), axis=0, tiled=False)
+
+    w_qkv = [qkv_weight(0, query_weight, key_weight, value_weight)]
+    w_o, w_a, w_b = [], [], []
+
+    firsts = jnp.swapaxes(first_picks[:, 0, 0], 1, 2)
+    seconds = jnp.swapaxes(second_picks[:, 0, 0].reshape(layers, tokens, -1), 1, 2)
+    height = layers * (8 + seconds.shape[1])
+    name_box, *tables = kernel_call(
+        functools.partial(slots_kernel, plan=plan, gbits=gbits, dbits=dbits),
+        "pick_slots",
+        [shape((owners, 16 * layers, lanes), bf16)] + [shape((height, chunk), jnp.int32)] * 4,
+        idx,
+        [firsts, seconds],
+        [pltpu.VMEM((4, height, chunk), jnp.int32)],
+    )
+    w_qkv[0][-1], name_box, *tables = after([w_qkv[0][-1], name_box, *tables])
     ids_row = blocks
     ids_col = blocks.reshape(-1, 1)
     heads_shape = shape((tokens * 3 // 2, 2 * HD), bf16)
@@ -990,7 +1039,8 @@
     chunk_shape = shape((chunk, d_model), f32)
     full_shape = shape((tokens, d_model), bf16)
     gain_shape = shape((1, d_model), f32)
-    forward_shape = shape((chunk, d_model + width), bf16)
+    box_shape = shape((chunk, 2 * d_model), bf16)
+    chunk_scratch = pltpu.VMEM((chunk, d_model), bf16)
     pack_scratch = pltpu.VMEM((4, tokens * 3 // 2, 2 * HD), bf16)
     part_scratch = pltpu.VMEM((tokens, d_model), bf16)
     kv_scratch = [
@@ -999,8 +1049,8 @@
         pltpu.VMEM((4 * tokens, 1), jnp.int32),
     ]
     x = inputs[0]
-    h_chunk = None
-    names = table = None
+    h_chunk = names = table = None
+    h_chunks = []
     kept = []
     for l in range(layers):
         if l == 0:
@@ -1012,18 +1062,36 @@
                 [x, gains, *w_qkv[l]],
                 [pack_scratch],
             )
-            firsts, seconds = after((first_picks, second_picks), es[0])
-            firsts = jnp.swapaxes(firsts[:, 0, 0], 1, 2)
-            seconds = jnp.swapaxes(seconds[:, 0, 0].reshape(layers, tokens, -1), 1, 2)
-            height = layers * (8 + seconds.shape[1])
-            outbox, *tables = kernel_call(
-                functools.partial(slots_kernel, plan=plan, gbits=gbits, dbits=dbits),
-                "pick_slots",
-                [shape((owners, 16 * layers, lanes), bf16)] + [shape((height, chunk), jnp.int32)] * 4,
+            qw, kw, vw, ow, lw, gw_, pw, ta_, tb_, mv = after(
+                (
+                    query_weight, key_weight, value_weight, attention_weight, lookup_weight,
+                    gate_weight, memory_weight, first_table, second_table, memory_values,
+                ),
+                es[0],
+            )
+            a_boxes, b_boxes = [], []
+            for n in range(layers):
+                w_o.append(shard_pieces(ow[n].astype(bf16), 1))
+                a_boxes.append(
+                    jnp.concatenate(
+                        [lw[n], jnp.concatenate([ta_[n, 0], tb_[n, 0]], axis=1)], axis=0
+                    ).astype(bf16)
+                )
+                b_boxes.append(jnp.concatenate([gw_[n], to_pack(pw[n])], axis=0).astype(bf16))
+                if n > 0:
+                    w_qkv.append(qkv_weight(n, qw, kw, vw))
+            w_a.append(gather_all(a_boxes[0]))
+        else:
+            h1, *es = kernel_call(
+                functools.partial(qkv_kernel, plan=plan),
+                "qkv",
+                [full_shape] + [heads_shape] * 4,
                 idx,
-                [firsts, seconds],
-                [pltpu.VMEM((4, height, chunk), jnp.int32)],
+                [*h_chunks, *w_qkv[l]],
+                [pack_scratch],
             )
+        es = swaps(es, SA)
+        if l == 0:
             (table,) = kernel_call(
                 functools.partial(pick_table_kernel, plan=plan),
                 "pick_table",
@@ -1032,20 +1100,12 @@
                 swaps(tables, TA),
                 [pltpu.VMEM((4, height, chunk), jnp.int32)],
             )
+            if shards == 2:
+                values = [memory_values, swap(mv, "fsdp", 1)]
+            else:
+                values = [lax.all_gather(mv, "fsdp", axis=1, tiled=True)]
         else:
-            h1, *es = kernel_call(
-                functools.partial(qkv_kernel, plan=plan),
-                "qkv",
-                [full_shape] + [heads_shape] * 4,
-                idx,
-                [*spread(h_chunk, TA), *w_qkv[l]],
-                [pack_scratch],
-            )
-        es = swaps(es, SA)
-        if l > 0:
-            tied = after([*es, *kept[-1][-1]])
-            es = list(tied[:4])
-            kept[-1] = kept[-1][:-1] + (list(tied[4:]),)
+            w_a.append(gather_all(after([a_boxes[l]], h1)[0]))
         heads = kernel_call(
             functools.partial(attend_kernel, plan=plan),
             "attend",
@@ -1054,17 +1114,18 @@
             [*es, ids_row, ids_col],
             kv_scratch,
         )
+        heads = swaps(heads, SA)
+        if l == 0:
+            heads[3], table = after([heads[3], table])
         attended, *parts = kernel_call(
             functools.partial(out_kernel, plan=plan),
             "attend_out",
             [shape((tokens, width), bf16)] + [part_shape] * 4,
             idx,
-            [*swaps(heads, SA), *w_o[l]],
+            [*heads, *w_o[l]],
             [pltpu.VMEM((4, tokens, HD), bf16), part_scratch],
         )
-        if l == 0:
-            (outbox,) = after((outbox,), parts[0])
-            names = lax.all_to_all(outbox, ("ctx", "tp"), 0, 0, tiled=True)
+        parts = swaps(parts, TA)
         middle, h2, u, w, outbox = kernel_call(
             functools.partial(lookup_kernel, plan=plan, row=layers + l, layer=l, shards=shards),
             "lookup",
@@ -1073,66 +1134,81 @@
                 part_shape,
                 shape((chunk, 8 * HD), bf16),
                 shape((32, tokens), f32),
-                shape((owners, 32, lanes), bf16),
+                shape((owners, 32 if l else 32 + name_box.shape[1], lanes), bf16),
             ],
             idx,
-            [x, *swaps(parts, TA), gains, w_look[l], table],
+            [x, *parts, gains, w_a[l], table] + ([] if l else [name_box]),
         )
         weights = lax.all_to_all(outbox, ("ctx", "tp"), 0, 0, tiled=True)
+        if l == 0:
+            names = weights
+        w_b.append(gather_all(after([b_boxes[l]], h2)[0]))
         (gate,) = kernel_call(
             functools.partial(gate_values_kernel, shards=shards),
             "gate_values",
             [chunk_shape],
             idx,
-            [h2, w_gate[l]],
+            [h2, w_b[l]],
         )
         *reads, dense = read_call(idx, weights, names, l, values, plan, tokens)
-        sums = kernel_call(sum_kernel, "memory_sum", [part_shape] * 4, idx, swaps(reads, "ctx"))
-        last = l + 1 == layers
-        mem, z, x3, h_chunk, *messages = kernel_call(
-            functools.partial(gate_kernel, plan=plan, row=None if last else l + 1, shards=shards),
-            "gate",
-            [chunk_shape, part_shape, chunk_shape, part_shape] + [forward_shape] * 4,
-            idx,
-            [*swaps(sums, "tp"), gate, w_mem[l], middle, h2, gains],
-        )
-        kept.append((x, h1, es, attended, middle, u, w, gate, dense, mem, swaps(messages, TA)))
+        reads = swaps(reads, "ctx")
+        sums = kernel_call(sum_kernel, "memory_sum", [part_shape] * 4, idx, reads)
+        sums = swaps(sums, "tp")
+        if l + 1 < layers:
+            mem, box, x3, h_chunk = kernel_call(
+                functools.partial(gate_kernel, row=l + 1, shards=shards),
+                "gate",
+                [chunk_shape, box_shape, chunk_shape, part_shape],
+                idx,
+                [*sums, gate, w_b[l], middle, h2, gains],
+                [chunk_scratch],
+            )
+            h_chunks = spread(h_chunk, TA)
+        else:
+            mem = x3 = None
+            gn, box, back_box = kernel_call(
+                functools.partial(gate_last_kernel, plan=plan, shards=shards),
+                "gate_last",
+                [part_shape, box_shape, box_shape],
+                idx,
+                [*sums, gate, w_b[l], middle, h2, cotangent[0]],
+                [
+                    pltpu.VMEM((chunk, d_model), f32),
+                    chunk_scratch,
+                    pltpu.VMEM((chunk, d_model), f32),
+                    chunk_scratch,
+                ],
+            )
+        kept.append((x, h1, es, attended, middle, u, w, gate, dense, mem, box))
         x = x3
-    out_chunks = spread(h_chunk, TA)
 
     g = cotangent[0]
     packs = [None] * layers
     gain_rows = [None] * (2 * layers)
     table_grads = None
     table_list = [None] * layers
-    gy = gn = gg = None
-    output = None
+    output = dvs_above = None
     for l in reversed(range(layers)):
-        x, h1, es, attended, middle, u, w, gate, dense, mem, messages = kept[l]
+        x, h1, es, attended, middle, u, w, gate, dense, mem, box = kept[l]
         top = l == layers - 1
-        if top:
-            gy, gn, gg = kernel_call(
-                functools.partial(start_back_kernel, plan=plan, shards=shards),
-                "start_back",
-                [part_shape] * 3,
-                idx,
-                [g, w_mem[l], gate, mem],
-            )
         line = jnp.concatenate(spread(gn, "tp"), axis=0)
-        *dvs, gw = write_call(idx, spread(line, "ctx"), names, l, dense, values, plan, tokens)
-        if top:
-            gw, *out_chunks = after([gw, *out_chunks])
-            (output,) = kernel_call(
-                functools.partial(place_kernel, plan=plan), "output", [full_shape], idx, out_chunks
-            )
+        planes = spread(line, "ctx")
+        if not top and shards == 2:
+            table_grads = table_grad_call(*dvs_above, l + 1, layers, table_grads)
+            planes[3], table_grads = after([planes[3], table_grads])
+        *dvs, gw = write_call(idx, planes, names, l, dense, values, plan, tokens)
+        if shards == 2:
+            dvs_above = [dvs[0], swap(dvs[1], "fsdp", 1)]
+        else:
+            table_list[l] = lax.psum_scatter(dvs[0], "fsdp", scatter_dimension=0, tiled=True).astype(f32)
         gw = lax.all_to_all(gw, ("ctx", "tp"), 0, 0, tiled=True)
-        back_shape = shape((chunk, width + 10 * HD + (0 if top else d_model)), bf16)
+        back_shape = shape((chunk, 10 * HD), bf16)
         g_mid, go_chunk, gain_rows[layers + l], *back = kernel_call(
             functools.partial(lookup_back_kernel, plan=plan, row=layers + l, layer=l, shards=shards),
             "lookup_back",
             [chunk_shape, part_shape, gain_shape] + [back_shape] * 4,
             idx,
-            [gw, table, w, w_look[l], u, gg, gy, w_gate[l], middle, g, gains],
+            [gw, table, w, w_a[l], u, back_box, w_b[l], middle, g, gains],
             [
                 pltpu.VMEM(w.shape, f32),
                 pltpu.VMEM(u.shape, bf16),
@@ -1140,133 +1216,163 @@
                 pltpu.VMEM((chunk, d_model), f32),
             ],
         )
+        go_chunks = spread(go_chunk, TA)
+        if l == 0 and shards == 2:
+            table_grads = table_grad_call(*dvs_above, l, layers, table_grads)
+            go_chunks[3], table_grads = after([go_chunks[3], table_grads])
         go, *ups = kernel_call(
             functools.partial(out_back_kernel, plan=plan),
             "attend_out_back",
             [full_shape] + [folded] * 4,
             idx,
-            [*spread(go_chunk, TA), *w_o[l]],
+            [*go_chunks, *w_o[l]],
             [pltpu.VMEM((4, tokens // 2, 2 * HD), bf16)],
         )
+        ups = swaps(ups, SA)
+        back = swaps(back, TA)
+        ups[3], *back = after([ups[3], *back])
         shard_size = d_model // shards
-        (memory_pack,) = kernel_call(
-            functools.partial(memory_grad_kernel, plan=plan, has_full=top),
-            "memory_grad",
-            [shape((shards, shard_size * 5 // 2 + NSUB // shards // 2, 256), bf16)],
-            idx,
-            [*messages, *swaps(back, TA)] + ([cotangent[0]] if top else []),
-            [
-                pltpu.VMEM((tokens, d_model), bf16),
-                pltpu.VMEM((tokens, width), bf16),
-                pltpu.VMEM((tokens, width), bf16),
-                pltpu.VMEM((tokens, 2 * HD), bf16),
-                pltpu.VMEM((tokens, d_model), bf16),
-            ],
-        )
-        (out_pack,) = kernel_call(
-            out_grad_kernel, "out_grad", [shape((shards, shard_size, 256), bf16)], idx, [attended, go]
-        )
         head_grads = kernel_call(
             functools.partial(attend_back_kernel, plan=plan),
             "attend_back",
             [heads_shape] * 4,
             idx,
-            [*es, *swaps(ups, SA), ids_row, ids_col],
+            [*es, *ups, ids_row, ids_col],
             kv_scratch + [pltpu.VMEM((4 * tokens, HD), f32)] * 2,
         )
+        head_grads = swaps(head_grads, SA)
+        if top:
+            forward_all = lax.all_gather(after([box], line)[0], TA, axis=0, tiled=False)
+            below_all = lax.all_gather(after([kept[l - 1][10]], line)[0], TA, axis=0, tiled=False)
+        else:
+            forward_all = below_all
+        back_all = lax.all_gather(after([back_box], line)[0], TA, axis=0, tiled=False)
+        if top:
+            output = back_all[:, :, d_model:].reshape(tokens, d_model)
         g_qkv, *parts = kernel_call(
             functools.partial(qkv_back_kernel, plan=plan),
             "qkv_back",
             [shape((tokens, 3 * width), bf16)] + [part_shape] * 4,
             idx,
-            [*swaps(head_grads, SA), *w_qkv[l]],
+            [*head_grads, *w_qkv[l]],
             [pack_scratch, part_scratch],
         )
+        parts = swaps(parts, TA)
+        qkv_rows = 3 * shard_size
+        weight_rows = shard_size * 7 // 2 + NSUB // shards // 2
+        weight_scratch = [
+            pltpu.VMEM((shards, weight_rows, 256), bf16),
+            pltpu.VMEM((tokens, d_model), bf16),
+            pltpu.VMEM((tokens, width), bf16),
+            pltpu.VMEM((tokens, width), bf16),
+            pltpu.VMEM((tokens, 2 * HD), bf16),
+            pltpu.VMEM((tokens, d_model), bf16),
+        ]
+        qkv_scratch = [pltpu.VMEM((shards, qkv_rows, 256), bf16)]
+        split = l == 0 and shards == 2
+        weight_outs = [shape((weight_rows, 256), bf16)] * 2 if split else [shape((shards, weight_rows, 256), bf16)]
+        qkv_outs = [shape((qkv_rows, 256), bf16)] * 2 if split else [shape((shards, qkv_rows, 256), bf16)]
+        qkv_packs = kernel_call(
+            qkv_grad_kernel, "qkv_grad", qkv_outs, idx, [h1, g_qkv], qkv_scratch
+        )
+        weight_packs = kernel_call(
+            functools.partial(weight_grad_kernel, plan=plan, has_full=top),
+            "weight_grad",
+            weight_outs,
+            idx,
+            [forward_all, back_all, *back, attended, go] + ([cotangent[0]] if top else []),
+            weight_scratch,
+        )
+        if split:
+            quarter = shape((qkv_rows // 4, 256), bf16)
+            qkv_quarters = kernel_call(
+                add_two_kernel, "qkv_add", [quarter] * 4, idx, [qkv_packs[0], swap(qkv_packs[1], "fsdp", 1)]
+            )
+            (pack,) = kernel_call(
+                add_pair_kernel,
+                "weight_add",
+                [shape((weight_rows, 256), bf16)],
+                idx,
+                [weight_packs[0], swap(weight_packs[1], "fsdp", 1)],
+            )
+            packs[l] = [lax.psum(pack, "ctx")]
+        else:
+            parts[3], weight_packs[0], qkv_packs[0], below_all = after(
+                [parts[3], weight_packs[0], qkv_packs[0], below_all]
+            )
+            packs[l] = reduce_packs([weight_packs[0], qkv_packs[0]])
         if l > 0:
             below = kept[l - 1]
-            g, gy, gain_rows[l], gn, gg = kernel_call(
+            g, gain_rows[l], gn, back_box = kernel_call(
                 functools.partial(norm_back_kernel, plan=plan, row=l, shards=shards),
                 "norm_back",
-                [chunk_shape, part_shape, gain_shape, part_shape, part_shape],
+                [chunk_shape, gain_shape, part_shape, box_shape],
                 idx,
-                [*swaps(parts, TA), x, g_mid, gains, w_mem[l - 1], below[7], below[9]],
+                [*parts, x, g_mid, gains, w_b[l - 1], below[7], below[9]],
+                [chunk_scratch],
             )
         else:
-            g, gain_rows[l] = kernel_call(
+            (g,) = kernel_call(
                 functools.partial(norm_back_last_kernel, plan=plan, row=l),
                 "norm_back_last",
-                [part_shape, gain_shape],
+                [shape((chunk + 16, d_model), bf16)],
                 idx,
-                [*swaps(parts, TA), x, g_mid, gains],
+                [*parts, x, g_mid, gains, *gain_rows[1:]],
+                [pltpu.VMEM((1, d_model), f32)],
             )
-        qkv_rows = 3 * shard_size
-        if l == 0 and shards == 2:
-            mine, other = kernel_call(
-                qkv_grad_split_kernel,
-                "qkv_grad",
-                [shape((qkv_rows, 256), bf16)] * 2,
-                idx,
-                [h1, g_qkv],
-                [pltpu.VMEM((d_model, 3 * width), f32)],
-            )
-            quarter = shape((qkv_rows // 4, 256), bf16)
-            parts = kernel_call(
-                add_two_kernel, "qkv_add", [quarter] * 4, idx, [mine, swap(other, "fsdp", 1)]
-            )
-            (part,) = kernel_call(add_four_kernel, "qkv_sum", [quarter], idx, swaps(parts, "ctx"))
-            late = spread(part, "ctx")
-            group = (memory_pack, out_pack)
-        else:
-            (pack,) = kernel_call(
-                qkv_grad_kernel, "qkv_grad", [shape((shards, qkv_rows, 256), bf16)], idx, [h1, g_qkv]
-            )
-            late = []
-            group = (memory_pack, out_pack, pack)
-        if l + 1 < layers:
-            group = after(group, *packs[l + 1])
-        scattered = [lax.psum_scatter(p, "fsdp", scatter_dimension=0, tiled=False) for p in group]
-        packs[l] = [lax.psum(p, "ctx") for p in scattered] + late
-        if shards == 2:
-            arrived = swap(dvs[1], "fsdp", 1)
-            table_grads = table_grad_call(dvs[0], arrived, l, layers, table_grads)
-        else:
-            table_list[l] = lax.psum_scatter(dvs[0], "fsdp", scatter_dimension=0, tiled=True).astype(f32)
-    (input_gradient,) = kernel_call(
-        functools.partial(place_kernel, plan=plan),
+    g_chunks = spread(g, TA)
+    input_gradient, gain_all, *gain_halves = kernel_call(
+        functools.partial(input_grad_kernel, plan=plan),
         "input_gradient",
-        [shape((tokens, d_model), f32)],
+        [
+            shape((tokens, d_model), f32),
+            shape((16, d_model), f32),
+            shape((16, 256), bf16),
+            shape((16, 256), bf16),
+        ],
         idx,
-        spread(g, TA),
+        g_chunks,
     )
     if shards != 2:
         table_grads = jnp.stack(table_list)
-    gain_all = jnp.concatenate(gain_rows, axis=0)
-    for axis in ("tp", "ctx"):
-        arrived = spread(gain_all, axis)
-        gain_all = (arrived[0] + arrived[1]) + (arrived[2] + arrived[3])
-    gain_all = lax.psum_scatter(gain_all, "fsdp", scatter_dimension=1, tiled=True) if shards != 2 else (
-        lax.dynamic_slice_in_dim(gain_all + swap(gain_all, "fsdp", 1), idx[0] * (d_model // 2), d_model // 2, 1)
-    )
+    gain_shapes = []
+    if shards == 2:
+        rows = qkv_rows // 4
+        (part,) = kernel_call(
+            plane_sum_kernel,
+            "plane_sum",
+            [shape((rows + 16, 256), bf16)],
+            idx,
+            [*swaps(qkv_quarters, "ctx"), gain_halves[0], swap(gain_halves[1], "fsdp", 1)],
+        )
+        late = spread(part, "ctx")
+        gain_shapes = [shape((layers, d_model // 2), f32)] * 2
+        flat = [packs[l][0] for l in range(layers)] + [packs[l][1] for l in range(1, layers)] + late
+    else:
+        gain_all = lax.psum(
+            lax.psum_scatter(gain_all[: 2 * layers], "fsdp", scatter_dimension=1, tiled=True), "ctx"
+        )
+        flat = [packs[l][n] for n in range(2) for l in range(layers)]
     shard_size = d_model // shards
     tall = shape((layers, shard_size, width), f32)
     wide = shape((layers, width, shard_size), f32)
-    sub = shape((layers, 1, NSUB // shards, HD), f32)
-    flat = [p for l in range(layers) for p in packs[l]]
+    sub = shape((layers, 1, HD, NSUB // shards), f32)
     grads = kernel_call(
-        functools.partial(finalize_kernel, layers=layers, late=len(packs[0]) > 3),
+        functools.partial(finalize_kernel, layers=layers, late=shards == 2),
         "finalize",
-        [tall, tall, tall, wide, shape((layers, shard_size, 2 * HD), f32), tall, wide, sub, sub],
+        [tall, tall, tall, wide, shape((layers, shard_size, 2 * HD), f32), tall, wide, sub, sub]
+        + gain_shapes,
         idx,
         flat,
-        [pltpu.VMEM((3 * shard_size, 256), bf16)],
-        limit=48,
+        [pltpu.VMEM((qkv_rows, 256), bf16)] if shards == 2 else [],
     )
+    gain_grads = grads[9:] if shards == 2 else [gain_all[:layers], gain_all[layers:]]
     return (
         output[None],
         input_gradient[None],
-        *grads,
-        gain_all[:layers],
-        gain_all[layers:],
+        *grads[:7],
+        *[jnp.swapaxes(t, 2, 3) for t in grads[7:9]],
+        *gain_grads,
         table_grads,
     )
 

time: 694 us -> 615 us (0.89)
  waiting for transfers between devices: 239 us -> 194 us
  starting transfers between devices: 152 us -> 128 us
  local copies, waits for them, and re-layouts: 84.4 us -> 67.2 us
  Pallas kernels: 149 us -> 158 us
    ppermute x112 -> x98, waiting for transfers between devices: 225 us -> 176 us  [swap(): return lax.ppermute(x, axis, [(i, i ^ step) for i in range(size)])]
    unnamed x382 -> x282, local copies, waits for them, and re-layouts: 79.6 us -> 53 us
    ppermute x112 -> x98, starting transfers between devices: 139 us -> 123 us  [swap(): return lax.ppermute(x, axis, [(i, i ^ step) for i in range(size)])]
    pallas_call x38 -> x35, Pallas kernels: 86.6 us -> 97.3 us  [kernel_call(): pl.pallas_call(body, out_shape=outs, in_specs=in_specs, out_specs=[pl.Blo...]
    squeeze x3 -> x9, local copies, waits for them, and re-layouts: 1.61 us -> 10.5 us  [the longest x2 3.07 us: qkv_weight(): queries[l]]
  transfers between devices with their start and end apart: 127 -> 110, of which waited for: 69 -> 56; matrix products, arithmetic and copies ran while one was open for 2% -> 2% of each run, Pallas kernels for 20% -> 23%
where the time goes in v3:
time: 615 us; the launch traced here: 609 us
  waiting for transfers between devices  194 us (32%)
  Pallas kernels  158 us (26%)
  starting transfers between devices  128 us (21%)
  local copies, waits for them, and re-layouts  67.2 us (11%)
  blocking collectives  41.3 us (7%)
  between operations  15.3 us (2%)
    ppermute x98, waiting for transfers between devices, swap(): return lax.ppermute(x, axis, [(i, i ^ step) for i in range(size)])  176 us
    ppermute x98, starting transfers between devices, swap(): return lax.ppermute(x, axis, [(i, i ^ step) for i in range(size)])  123 us
    pallas_call x35, Pallas kernels, kernel_call(): pl.pallas_call(body, out_shape=outs, in_specs=in_specs, out_specs=[pl.Blo...  97.3 us
    unnamed x282, local copies, waits for them, and re-layouts  53 us
    all_to_all x2, blocking collectives, body(): gw = lax.all_to_all(gw, ('ctx', 'tp'), 0, 0, tiled=True)  29.1 us
    pallas_call x2, Pallas kernels, write_call(): pl.pallas_call(functools.partial(write_kernel, plan=plan, pieces=pieces,...  28.6 us
    pallas_call x2, Pallas kernels, read_call(): pl.pallas_call(functools.partial(read_kernel, plan=plan, pieces=len(value...  19.2 us
    pallas_call x2, Pallas kernels, table_grad_call(): pl.pallas_call(table_grad_kernel, grid=(rows // block,), out_shape=shape(...  12.8 us
  transfers between devices with their start and end apart: 110, of which 56 were waited for; matrix products, arithmetic and copies ran while one was open for 2% of the time, Pallas kernels for 23%

profile of v3, /device:TPU:0, one launch (start us, length us, event | category | flops | bytes accessed | tf_op | source)
XLA Modules:
  0.0 609.0 jit_solution(18012436528672398173)
XLA Ops:
  55.3 6.5 %collective-permute-done.13.r2 = bf16[64,1024]{1,0:T(8,128)(2,1)S(1)} collective-permute-done((bf16[64,1024]{1,0:T(8,128)(2,1)S(1)}, bf16[64,1024]{1,0:T(8,128)(2,1)S(1)}, u32[]{:S(2)}, u32[]{:S(2)}) %collective-permute-start.13) | collective-permute-done | bytes 131104 | tf_op jit(solution)/shard_map/ppermute | solution.py:34
  63.1 5.8 lookup.2
  80.0 8.4 %all-to-all-done.w_ref.names_ref = bf16[16,64,128]{2,1,0:T(8,128)(2,1)S(1)} async-done(((bf16[16,64,128]{2,1,0:T(8,128)(2,1)}), bf16[16,64,128]{2,1,0:T(8,128)(2,1)S(1)}, u32[]{:S(2)}, u32[]{:S(2)}) %all-to-all-start) | async-done | bytes 262176 | tf_op jit(solution)/shard_map/all_to_all | solution.py:1142
  88.4 9.6 %memory_read.2 = (bf16[256,1024]{1,0:T(8,128)(2,1)S(1)}, bf16[256,1024]{1,0:T(8,128)(2,1)S(1)}, bf16[256,1024]{1,0:T(8,128)(2,1)S(1)}, bf16[256,1024]{1,0:T(8,128)(2,1)S(1)}, f32[16,128,256]{2,1,0:T(8,128)}) custom-call(s32[4]{0:T(128)S(1)} %pad_add_fusion.idx, bf16[16,64,128]{2,1,0:T(8,128)(2,1)S(1)} %all-to-all-done.w_ref.names_ref, ...), custom_call_target="tpu_custom_call" | custom-call | flops 2147483648 | bytes 20971520 | tf_op jit(solution)/shard_map/memory_read/pallas_call | solution.py:785
  101.7 7.9 %collective-permute-done.16.r1 = bf16[256,1024]{1,0:T(8,128)(2,1)S(1)} collective-permute-done((bf16[256,1024]{1,0:T(8,128)(2,1)S(1)}, bf16[256,1024]{1,0:T(8,128)(2,1)S(1)}, u32[]{:S(2)}, u32[]{:S(2)}) %collective-permute-start.16) | collective-permute-done | bytes 524320 | tf_op jit(solution)/shard_map/ppermute | solution.py:34
  201.5 12.2 %all_to_all.20.w_ref = bf16[16,32,128]{2,1,0:T(8,128)(2,1)S(1)} all-to-all(bf16[16,32,128]{2,1,0:T(8,128)(2,1)} %copy-done.96), channel_id=1, replica_groups=mesh['fsdp'=2,'ctx'=4,'tp'=4] {'ctx','tp'}, dimensions={0} | all-to-all | bytes 262144 | tf_op jit(solution)/shard_map/all_to_all | solution.py:1142
  213.7 9.6 %memory_read.3 = (bf16[256,1024]{1,0:T(8,128)(2,1)S(1)}, bf16[256,1024]{1,0:T(8,128)(2,1)S(1)}, bf16[256,1024]{1,0:T(8,128)(2,1)S(1)}, bf16[256,1024]{1,0:T(8,128)(2,1)S(1)}, f32[16,128,256]{2,1,0:T(8,128)}) custom-call(s32[4]{0:T(128)S(1)} %pad_add_fusion.idx, bf16[16,32,128]{2,1,0:T(8,128)(2,1)S(1)} %all_to_all.20.w_ref, ...), custom_call_target="tpu_custom_call" | custom-call | flops 2147483648 | bytes 20971520 | tf_op jit(solution)/shard_map/memory_read/pallas_call | solution.py:785
  226.8 11.4 %collective-permute-done.36.r1 = bf16[256,1024]{1,0:T(8,128)(2,1)S(1)} collective-permute-done((bf16[256,1024]{1,0:T(8,128)(2,1)S(1)}, bf16[256,1024]{1,0:T(8,128)(2,1)S(1)}, u32[]{:S(2)}, u32[]{:S(2)}) %collective-permute-start.36) | collective-permute-done | bytes 524320 | tf_op jit(solution)/shard_map/ppermute | solution.py:34
  238.2 7.1 %collective-permute-done.37.r2 = bf16[256,1024]{1,0:T(8,128)(2,1)S(1)} collective-permute-done((bf16[256,1024]{1,0:T(8,128)(2,1)S(1)}, bf16[256,1024]{1,0:T(8,128)(2,1)S(1)}, u32[]{:S(2)}, u32[]{:S(2)}) %collective-permute-start.37) | collective-permute-done | bytes 524320 | tf_op jit(solution)/shard_map/ppermute | solution.py:34
  279.8 10.3 %collective-permute-done.47.g3 = bf16[256,1024]{1,0:T(8,128)(2,1)S(1)} collective-permute-done((bf16[256,1024]{1,0:T(8,128)(2,1)}, bf16[256,1024]{1,0:T(8,128)(2,1)S(1)}, u32[]{:S(2)}, u32[]{:S(2)}) %collective-permute-start.47) | collective-permute-done | bytes 524320 | tf_op jit(solution)/shard_map/ppermute | solution.py:34
  295.7 14.4 %memory_write.2 = (bf16[2048,1024]{1,0:T(8,128)(2,1)}, bf16[2048,1024]{1,0:T(8,128)(2,1)}, bf16[16,32,128]{2,1,0:T(8,128)(2,1)S(1)}) custom-call(s32[4]{0:T(128)S(1)} %pad_add_fusion.idx, bf16[256,1024]{1,0:T(8,128)(2,1)} %constant_dynamic-update-slice_fusion.g0, bf16[256,1024]{1,0:T(8,128)(2,1)S(1)} %collective-permute-done.45.g1, ...), custom_call_target="tpu_custom_call" | custom-call | flops 3221225472 | bytes 29360128 | tf_op jit(solution)/shard_map/memory_write/pallas_call | solution.py:882
  310.1 16.5 %all_to_all.21.gw_ref = bf16[16,32,128]{2,1,0:T(8,128)(2,1)S(1)} all-to-all(bf16[16,32,128]{2,1,0:T(8,128)(2,1)S(1)} %get-tuple-element.278), channel_id=1, replica_groups=mesh['fsdp'=2,'ctx'=4,'tp'=4] {'ctx','tp'}, dimensions={0} | all-to-all | bytes 262144 | tf_op jit(solution)/shard_map/all_to_all | solution.py:1204
  326.8 5.8 lookup_back.2
  343.9 9.0 %collective-permute-done.49.g2 = bf16[64,1024]{1,0:T(8,128)(2,1)S(1)} collective-permute-done((bf16[64,1024]{1,0:T(8,128)(2,1)S(1)}, bf16[64,1024]{1,0:T(8,128)(2,1)S(1)}, u32[]{:S(2)}, u32[]{:S(2)}) %collective-permute-start.49) | collective-permute-done | bytes 131104 | tf_op jit(solution)/shard_map/ppermute | solution.py:34
  364.9 5.8 attend_back.2
  419.9 6.3 %table_grad.2.refs_0_ = f32[2,2048,1024]{2,1,0:T(8,128)} custom-call(bf16[2048,1024]{1,0:T(8,128)(2,1)S(1)} %copy-done.7, bf16[2048,1024]{1,0:T(8,128)(2,1)} %collective-permute-done.69.b_ref), custom_call_target="tpu_custom_call" | custom-call | bytes 16777216 | tf_op jit(solution)/shard_map/table_grad/pallas_call | solution.py:934
  429.9 14.1 %memory_write.3 = (bf16[2048,1024]{1,0:T(8,128)(2,1)}, bf16[2048,1024]{1,0:T(8,128)(2,1)}, bf16[16,32,128]{2,1,0:T(8,128)(2,1)S(1)}) custom-call(s32[4]{0:T(128)S(1)} %pad_add_fusion.idx, bf16[256,1024]{1,0:T(8,128)(2,1)S(1)} %constant_dynamic-update-slice_fusion.4.g0, bf16[256,1024]{1,0:T(8,128)(2,1)S(1)} %collective-permute-done.66.g1, ...), custom_call_target="tpu_custom_call" | custom-call | flops 3221225472 | bytes 29360128 | tf_op jit(solution)/shard_map/memory_write/pallas_call | solution.py:882
  444.7 12.6 %all_to_all.22.gw_ref = bf16[16,32,128]{2,1,0:T(8,128)(2,1)S(1)} all-to-all(bf16[16,32,128]{2,1,0:T(8,128)(2,1)} %copy-done.95), channel_id=1, replica_groups=mesh['fsdp'=2,'ctx'=4,'tp'=4] {'ctx','tp'}, dimensions={0} | all-to-all | bytes 262144 | tf_op jit(solution)/shard_map/all_to_all | solution.py:1204
  459.1 6.2 %lookup_back.3 = (f32[64,1024]{1,0:T(8,128)S(1)}, bf16[64,1024]{1,0:T(8,128)(2,1)S(1)}, f32[1,1024]{1,0:T(1,128)S(1)}, bf16[64,640]{1,0:T(8,128)(2,1)S(1)}, bf16...) custom-call(s32[4]{0:T(128)S(1)} %pad_add_fusion.idx, ...), custom_call_target="tpu_custom_call" | custom-call | bytes 7344128 | tf_op jit(solution)/shard_map/lookup_back/pallas_call | solution.py:54
  481.5 6.5 %table_grad.3 = f32[2,2048,1024]{2,1,0:T(8,128)} custom-call(bf16[2048,1024]{1,0:T(8,128)(2,1)S(1)} %copy-done.6, bf16[2048,1024]{1,0:T(8,128)(2,1)} %collective-permute-done.73.b_ref, f32[2,2048,1024]{2,1,0:T(8,128)} %table_grad.2.refs_0_), custom_call_target="tpu_custom_call", output_to_operand_aliasing={{}: (2, {})} | custom-call | bytes 16777216 | tf_op jit(solution)/shard_map/table_grad/pallas_call | solution.py:934
  536.6 5.9 collective-permute-done.84.r2
  551.9 6.2 %collective-permute-start.86 = (bf16[80,1024]{1,0:T(8,128)(2,1)S(1)}, bf16[80,1024]{1,0:T(8,128)(2,1)S(1)}, u32[]{:S(2)}, u32[]{:S(2)}) collective-permute-start(bf16[80,1024]{1,0:T(8,128)(2,1)S(1)} %norm_back_last.1.c0), channel_id=1, source_target_pairs={{0,1},{1,0},{2,3},{3,2},{4,5},{5,4},{6,7},{7,6},{8,9},{9,8},{10,11... | collective-permute-start | bytes 491528 | tf_op jit(solution)/shard_map/ppermute | solution.py:34
  572.1 7.4 %collective-permute-done.97.refs_6_ = bf16[400,256]{1,0:T(8,128)(2,1)S(1)} collective-permute-done((bf16[400,256]{1,0:T(8,128)(2,1)S(1)}, bf16[400,256]{1,0:T(8,128)(2,1)S(1)}, u32[]{:S(2)}, u32[]{:S(2)}) %collective-permute-start.97) | collective-permute-done | bytes 204832 | tf_op jit(solution)/shard_map/ppermute | solution.py:34
  587.7 7.4 %all-reduce.3.cloned.1.call-done = (bf16[1856,256]{1,0:T(8,128)(2,1)}, bf16[1856,256]{1,0:T(8,128)(2,1)}, bf16[1536,256]{1,0:T(8,128)(2,1)}) async-done(((bf16[1856,256]{1,0:T(8,128)(2,1)}, bf16[1856,256]{1,0:T(8,128)(2,1)}, bf16[1536,256]{1,0:T(8,128)(2,1)}), (bf16[1856,256]{1,0:T(8,128)(2,1)}, bf16[1856,256]{1,0:T(8,128)(2,1)}, bf16[1536,256]{1,0:T(8,128)(2,1)})) %all-reduce.3.cloned.1.call-update) | async-done | bytes 2686992 | tf_op jit(solution)/shard_map/psum | solution.py:1298
  (567 shorter events, 380.8 us)
Async XLA Ops:
  7.2 54.6 %all-gather.16.cloned.1.call-start = ((), (), s32[]{:S(2)}) async-start(), calls=%async_computation.6 | async-start | bytes 1474560 | tf_op jit(solution)/shard_map/all_gather | solution.py:1017
  21.0 101.2 %all-gather.18.cloned.1.call-start = ((), (), s32[]{:S(2)}) async-start(), calls=%async_computation.9 | async-start | bytes 4718592 | tf_op jit(solution)/shard_map/all_gather | solution.py:1017
  21.6 66.8 %collective-permute-start.15 = (bf16[2,2048,1024]{2,1,0:T(8,128)(2,1)}, bf16[2,2048,1024]{2,1,0:T(8,128)(2,1)}, u32[]{:S(2)}, u32[]{:S(2)}) collective-permute-start(bf16[2,2048,1024]{2,1,0:T(8,128)(2,1)} %refs_0_.7), channel_id=1, source_target_pairs={{0,16},{16,0},{1,17},{17,1},{2,18},{18,2},{3,19},{19,3},{4,20},{20... | collective-permute-start | bytes 25165832 | tf_op jit(solution)/shard_map/ppermute | solution.py:34
  74.4 114.3 %all-gather.20.cloned.1.call-start = ((), (), s32[]{:S(2)}) async-start(), calls=%async_computation.10 | async-start | bytes 1474560 | tf_op jit(solution)/shard_map/all_gather | solution.py:1017
  101.6 39.8 %collective-permute-start.25 = (bf16[512,768]{1,0:T(8,128)(2,1)S(1)}, bf16[512,768]{1,0:T(8,128)(2,1)}, u32[]{:S(2)}, u32[]{:S(2)}) collective-permute-start(bf16[512,768]{1,0:T(8,128)(2,1)S(1)} %pad_maximum_fusion.1.refs_0_), channel_id=1, source_target_pairs={{0,16},{16,0},{1,17},{17,1},{2,18},{18,2},{3,19},{19,3},{4,20},{20... | collective-permute-start | bytes 2359304 | tf_op jit(solution)/shard_map/ppermute | solution.py:34
  151.7 100.0 %all-gather.22.cloned.1.call-start = ((), (), s32[]{:S(2)}) async-start(), calls=%async_computation.11 | async-start | bytes 4718592 | tf_op jit(solution)/shard_map/all_gather | solution.py:1017
  201.5 185.2 %all-gather.24.cloned.1.call-start = ((), (), s32[]{:S(2)}) async-start(), calls=%async_computation.12 | async-start | bytes 1310720 | tf_op jit(solution)/shard_map/all_gather | solution.py:1249
  224.2 21.1 %collective-permute-start.37 = (bf16[256,1024]{1,0:T(8,128)(2,1)S(1)}, bf16[256,1024]{1,0:T(8,128)(2,1)S(1)}, u32[]{:S(2)}, u32[]{:S(2)}) collective-permute-start(bf16[256,1024]{1,0:T(8,128)(2,1)S(1)} %get-tuple-element.265), channel_id=1, source_target_pairs={{0,8},{4,12},{8,0},{12,4},{1,9},{5,13},{9,1},{13,5},{2,10},{6,14},... | collective-permute-start | bytes 1572872 | tf_op jit(solution)/shard_map/ppermute | solution.py:34
  224.9 20.4 %collective-permute-start.38 = (bf16[256,1024]{1,0:T(8,128)(2,1)S(1)}, bf16[256,1024]{1,0:T(8,128)(2,1)S(1)}, u32[]{:S(2)}, u32[]{:S(2)}) collective-permute-start(bf16[256,1024]{1,0:T(8,128)(2,1)S(1)} %get-tuple-element.266), channel_id=1, source_target_pairs={{0,12},{4,8},{8,4},{12,0},{1,13},{5,9},{9,5},{13,1},{2,14},{6,10},... | collective-permute-start | bytes 1572872 | tf_op jit(solution)/shard_map/ppermute | solution.py:34
  274.9 111.8 %all-gather.26.cloned.1.call-start = ((), (), s32[]{:S(2)}) async-start(), calls=%async_computation.13 | async-start | bytes 1310720 | tf_op jit(solution)/shard_map/all_gather | solution.py:1245
  275.5 120.0 %all-gather.28.cloned.1.call-start = ((), (), s32[]{:S(2)}) async-start(), calls=%async_computation.14 | async-start | bytes 1310720 | tf_op jit(solution)/shard_map/all_gather | solution.py:1246
  276.2 219.6 %all-gather.30.cloned.1.call-start = ((), (), s32[]{:S(2)}) async-start(), calls=%async_computation.15 | async-start | bytes 1310720 | tf_op jit(solution)/shard_map/all_gather | solution.py:1249
  310.1 107.5 %collective-permute-start.69 = (bf16[2048,1024]{1,0:T(8,128)(2,1)}, bf16[2048,1024]{1,0:T(8,128)(2,1)}, u32[]{:S(2)}, u32[]{:S(2)}) collective-permute-start(bf16[2048,1024]{1,0:T(8,128)(2,1)} %get-tuple-element.315), channel_id=1, source_target_pairs={{0,16},{16,0},{1,17},{17,1},{2,18},{18,2},{3,19},{19,3},{4,20},{20... | collective-permute-start | bytes 12582920 | tf_op jit(solution)/shard_map/ppermute | solution.py:34
  333.2 19.7 %collective-permute-start.49 = (bf16[64,1024]{1,0:T(8,128)(2,1)S(1)}, bf16[64,1024]{1,0:T(8,128)(2,1)S(1)}, u32[]{:S(2)}, u32[]{:S(2)}) collective-permute-start(bf16[64,1024]{1,0:T(8,128)(2,1)S(1)} %get-tuple-element.281.g0), channel_id=1, source_target_pairs={{0,2},{1,3},{2,0},{3,1},{4,6},{5,7},{6,4},{7,5},{8,10},{9,11},{10,... | collective-permute-start | bytes 393224 | tf_op jit(solution)/shard_map/ppermute | solution.py:34
  334.0 19.4 %collective-permute-start.48 = (bf16[64,1024]{1,0:T(8,128)(2,1)S(1)}, bf16[64,1024]{1,0:T(8,128)(2,1)S(1)}, u32[]{:S(2)}, u32[]{:S(2)}) collective-permute-start(bf16[64,1024]{1,0:T(8,128)(2,1)S(1)} %get-tuple-element.281.g0), channel_id=1, source_target_pairs={{0,1},{1,0},{2,3},{3,2},{4,5},{5,4},{6,7},{7,6},{8,9},{9,8},{10,11... | collective-permute-start | bytes 393224 | tf_op jit(solution)/shard_map/ppermute | solution.py:34
  413.2 91.0 %reduce-scatter.5.cloned.1.call-start = ((), (), s32[]{:S(2)}) async-start(), calls=%async_computation.8 | async-start | bytes 2359296 | tf_op jit(solution)/shard_map/reduce_scatter | solution.py:964
  413.9 90.3 %reduce-scatter.3.cloned.1.call-start = ((), (), s32[]{:S(2)}) async-start(), calls=%async_computation.7 | async-start | bytes 2850816 | tf_op jit(solution)/shard_map/reduce_scatter | solution.py:964
  444.7 33.1 %collective-permute-start.73 = (bf16[2048,1024]{1,0:T(8,128)(2,1)}, bf16[2048,1024]{1,0:T(8,128)(2,1)}, u32[]{:S(2)}, u32[]{:S(2)}) collective-permute-start(bf16[2048,1024]{1,0:T(8,128)(2,1)} %get-tuple-element.325), channel_id=1, source_target_pairs={{0,16},{16,0},{1,17},{17,1},{2,18},{18,2},{3,19},{19,3},{4,20},{20... | collective-permute-start | bytes 12582920 | tf_op jit(solution)/shard_map/ppermute | solution.py:34
  444.7 150.4 %all-reduce.3.cloned.1.call-start = ((), (), s32[]{:S(2)}) async-start(), calls=%async_computation.16 | async-start | bytes 5373952 | tf_op jit(solution)/shard_map/psum | solution.py:1298
  466.6 21.4 %collective-permute-start.71 = (bf16[64,1024]{1,0:T(8,128)(2,1)S(1)}, bf16[64,1024]{1,0:T(8,128)(2,1)S(1)}, u32[]{:S(2)}, u32[]{:S(2)}) collective-permute-start(bf16[64,1024]{1,0:T(8,128)(2,1)S(1)} %get-tuple-element.323.g0), channel_id=1, source_target_pairs={{0,2},{1,3},{2,0},{3,1},{4,6},{5,7},{6,4},{7,5},{8,10},{9,11},{10,... | collective-permute-start | bytes 393224 | tf_op jit(solution)/shard_map/ppermute | solution.py:34
  468.5 19.5 %collective-permute-start.70 = (bf16[64,1024]{1,0:T(8,128)(2,1)S(1)}, bf16[64,1024]{1,0:T(8,128)(2,1)S(1)}, u32[]{:S(2)}, u32[]{:S(2)}) collective-permute-start(bf16[64,1024]{1,0:T(8,128)(2,1)S(1)} %get-tuple-element.323.g0), channel_id=1, source_target_pairs={{0,1},{1,0},{2,3},{3,2},{4,5},{5,4},{6,7},{7,6},{8,9},{9,8},{10,11... | collective-permute-start | bytes 393224 | tf_op jit(solution)/shard_map/ppermute | solution.py:34
  471.0 20.4 %collective-permute-start.77 = (bf16[64,640]{1,0:T(8,128)(2,1)S(1)}, bf16[64,640]{1,0:T(8,128)(2,1)S(1)}, u32[]{:S(2)}, u32[]{:S(2)}) collective-permute-start(bf16[64,640]{1,0:T(8,128)(2,1)S(1)} %get-tuple-element.333), channel_id=1, source_target_pairs={{0,1},{1,0},{2,3},{3,2},{4,5},{5,4},{6,7},{7,6},{8,9},{9,8},{10,11... | collective-permute-start | bytes 245768 | tf_op jit(solution)/shard_map/ppermute | solution.py:34
  545.5 21.6 %collective-permute-start.91 = (bf16[384,256]{1,0:T(8,128)(2,1)S(1)}, bf16[384,256]{1,0:T(8,128)(2,1)S(1)}, u32[]{:S(2)}, u32[]{:S(2)}) collective-permute-start(bf16[384,256]{1,0:T(8,128)(2,1)S(1)} %get-tuple-element.367), channel_id=1, source_target_pairs={{0,4},{4,0},{8,12},{12,8},{1,5},{5,1},{9,13},{13,9},{2,6},{6,2},{1... | collective-permute-start | bytes 589832 | tf_op jit(solution)/shard_map/ppermute | solution.py:34
  546.8 20.2 %collective-permute-start.92 = (bf16[384,256]{1,0:T(8,128)(2,1)S(1)}, bf16[384,256]{1,0:T(8,128)(2,1)S(1)}, u32[]{:S(2)}, u32[]{:S(2)}) collective-permute-start(bf16[384,256]{1,0:T(8,128)(2,1)S(1)} %get-tuple-element.368), channel_id=1, source_target_pairs={{0,8},{4,12},{8,0},{12,4},{1,9},{5,13},{9,1},{13,5},{2,10},{6,14},... | collective-permute-start | bytes 589832 | tf_op jit(solution)/shard_map/ppermute | solution.py:34
  (224 other events, 2303.9 us)
Sparse Core Ops, SparseCore 0:
  21.1 29.4 all-gather.15
  69.7 48.4 all-gather.17
  151.8 22.9 all-gather.19
  201.6 46.3 all-gather.21
  275.0 26.6 all-gather.23
  303.1 30.7 all-gather.25
  335.5 34.0 all-gather.27
  413.3 26.9 all-gather.29
  442.6 12.1 reduce-scatter.4
  457.0 7.7 reduce-scatter.2
  504.4 90.6 all-reduce.2

commit v4 on v3

--- a/solution.py
+++ b/solution.py
@@ -303,8 +303,10 @@
         u[...] = pack[idx[plan.si] ^ d]
 
 
-def qkv_back_kernel(idx, g0, g1, g2, g3, *refs, plan):
-    *pieces, g_ref, p0, p1, p2, p3, pack, part = refs
+def qkv_back_kernel(idx, g0, g1, g2, g3, *refs, plan, row=None, gain_rows=0):
+    *ins, g_ref, p0, p1, p2, p3, pack, part = refs
+    x_ref, *rows_refs = ins[len(ins) - gain_rows :] if gain_rows else [None]
+    pieces = ins[: len(ins) - gain_rows]
     for d, g in enumerate((g0, g1, g2, g3)):
         pack[idx[plan.si] ^ d] = g[...]
     rows = g_ref.shape[0]
@@ -313,9 +315,26 @@
     columns += [unfold(pack[j, rows:, :]) for j in range(4)]
     g_ref[...] = jnp.concatenate(columns, axis=1)
     size = pieces[0].shape[0]
+    if not gain_rows:
+        for j, w in enumerate(pieces):
+            part[:, piece_at(idx[0], j, pieces, size)] = dot_nt(g_ref[...], w[...]).astype(bf16)
+        emit_chunks(part, (p0, p1, p2, p3), idx[plan.ti])
+        return
+    x = x_ref[...].astype(f32)
+    factor = lax.rsqrt(jnp.mean(x * x, axis=1, keepdims=True) + EPS)
+    count = part.shape[0] // 4
     for j, w in enumerate(pieces):
-        part[:, piece_at(idx[0], j, pieces, size)] = dot_nt(g_ref[...], w[...]).astype(bf16)
-    emit_chunks(part, (p0, p1, p2, p3), idx[plan.ti])
+        at = piece_at(idx[0], j, pieces, size)
+        term = dot_nt(g_ref[...], w[...])
+        part[:, at] = term.astype(bf16)
+        change = jnp.sum(term * (x_ref[:, at].astype(f32) * factor), axis=0, keepdims=True)
+        p0[count : count + 1, at] = change.astype(bf16)
+    blank = jnp.zeros((p0.shape[0] - count - gain_rows, p0.shape[1]), f32)
+    tail = [p0[count : count + 1, :].astype(f32)] + [r[...] for r in rows_refs] + [blank]
+    tail = jnp.concatenate(tail, axis=0).astype(bf16)
+    for d, out in enumerate((p0, p1, p2, p3)):
+        out[0:count, :] = part[rows_at(idx[plan.ti] ^ d, count), :]
+        out[count:, :] = tail
 
 
 def to_pack(x):
@@ -400,22 +419,21 @@
 
 
 def finalize_kernel(idx, *refs, layers, late):
-    ins = refs[: 2 * layers + 3 * late]
-    outs = refs[2 * layers + 3 * late :]
+    count = 2 * layers + 2 * late
+    ins, outs = refs[:count], refs[count:]
     q_ref, k_ref, v_ref, o_ref, look_ref, gate_ref, mem_ref, first_ref, second_ref = outs[:9]
     part = q_ref.shape[1]
     for l in range(layers):
-        memory = ins[l]
         if l > 0 or not late:
-            qkv = ins[layers + l - late]
+            memory, qkv = ins[2 * l + 2 * late], ins[2 * l + 2 * late + 1]
         else:
-            one_ref, two_ref, qkv = outs[9:]
-            rows = qkv.shape[0] // 4
+            one_ref, two_ref, memory, qkv = outs[9:]
+            rows, more = memory.shape[0] // 4, qkv.shape[0] // 4
             total = 0.0
             for d in range(4):
-                chunk = ins[2 * layers - 1 + d]
-                qkv[rows_at(idx[1] ^ d, rows), :] = chunk[0:rows, :]
-                total = total + chunk[rows:, :].astype(f32)
+                memory[rows_at(idx[1] ^ d, rows), :] = ins[d][0:rows, :]
+                qkv[rows_at(idx[1] ^ d, more), :] = ins[d][rows : rows + more, :]
+                total = total + ins[d][rows + more :, :].astype(f32)
             total = jnp.concatenate([total[0:8], total[8:16]], axis=1)
             one_ref[...] = total[0:layers]
             two_ref[...] = total[layers : 2 * layers]
@@ -433,10 +451,6 @@
         o_ref[l] = from_pack(memory[at : at + part, :], o_ref.shape[1], o_ref.shape[2]).astype(f32)
 
 
-def add_pair_kernel(idx, a, b, out):
-    out[...] = (a[...].astype(f32) + b[...].astype(f32)).astype(bf16)
-
-
 def add_two_kernel(idx, a, b, o0, o1, o2, o3):
     chunk = o0.shape[0]
     for d, out in enumerate((o0, o1, o2, o3)):
@@ -444,10 +458,13 @@
         out[...] = (a[at, :].astype(f32) + b[at, :].astype(f32)).astype(bf16)
 
 
-def plane_sum_kernel(idx, a0, a1, a2, a3, g0, g1, out):
-    rows = a0.shape[0]
-    out[0:rows, :] = total4((a0, a1, a2, a3)).astype(bf16)
-    out[rows:, :] = (g0[...].astype(f32) + g1[...].astype(f32)).astype(bf16)
+def plane_sum_kernel(idx, *refs):
+    a, b, (g0, g1, out) = refs[0:4], refs[4:8], refs[8:]
+    rows = a[0].shape[0]
+    more = rows + b[0].shape[0]
+    out[0:rows, :] = total4(a).astype(bf16)
+    out[rows:more, :] = total4(b).astype(bf16)
+    out[more:, :] = (g0[...].astype(f32) + g1[...].astype(f32)).astype(bf16)
 
 
 def own_rows(ref, idx, plan, count):
@@ -607,27 +624,27 @@
     back_ref[:, gy.shape[1] :] = gy[...]
 
 
-def norm_back_last_kernel(idx, p0, r1, r2, r3, x_ref, g_ref, gain_ref, *refs, plan, row):
-    *rows, out_ref, dgain = refs
-    gx = norm_back(idx, (p0, r1, r2, r3), x_ref, g_ref, gain_ref, dgain, plan, row)
-    count = gx.shape[0]
-    out_ref[0:count, :] = gx.astype(bf16)
-    both = [dgain[...]] + [r[...] for r in rows]
-    blank = jnp.zeros((out_ref.shape[0] - count - len(both), gx.shape[1]), f32)
-    out_ref[count:, :] = jnp.concatenate(both + [blank], axis=0).astype(bf16)
-
-
-def input_grad_kernel(idx, c0, c1, c2, c3, out_ref, gain_ref, mine_ref, other_ref, plan):
-    chunk = out_ref.shape[0] // 4
-    total = 0.0
+def norm_back_last_kernel(
+    idx, p0, r1, r2, r3, x_ref, g_ref, gain_ref, out_ref, all_ref, mine_ref, other_ref, plan, row
+):
+    count = out_ref.shape[0]
+    refs = (p0, r1, r2, r3)
+    upstream = total4([r.at[0:count] for r in refs])
+    x = own_rows(x_ref, idx, plan, count)
+    factor, _ = rms(x, gain_ref[row : row + 1, :])
+    gx = g_ref[...] + rms_back(x, factor, gain_ref[row : row + 1, :], upstream)
+    out_ref[...] = gx.astype(bf16)
+    all_ref[...] = total4([r.at[count:] for r in refs])
+    size = all_ref.shape[1] // 2
+    for j, out in enumerate((mine_ref, other_ref)):
+        half = all_ref[:, rows_at(idx[0] ^ j, size)]
+        out[...] = jnp.concatenate([half[:8, 0:256], half[:8, 256:]], axis=0).astype(bf16)
+
+
+def place_kernel(idx, c0, c1, c2, c3, out_ref, plan):
+    chunk = c0.shape[0]
     for d, c in enumerate((c0, c1, c2, c3)):
-        out_ref[rows_at(idx[plan.ti] ^ d, chunk), :] = c[0:chunk, :].astype(f32)
-        total = total + c[chunk:, :].astype(f32)
-    gain_ref[...] = total
-    size = gain_ref.shape[1] // 2
-    for j, out in enumerate((mine_ref, other_ref)):
-        half = gain_ref[:, rows_at(idx[0] ^ j, size)]
-        out[...] = jnp.concatenate([half[:8, 0:256], half[:8, 256:]], axis=0).astype(bf16)
+        out_ref[rows_at(idx[plan.ti] ^ d, chunk), :] = c[...].astype(out_ref.dtype)
 
 
 def lookup_back_kernel(
@@ -1201,6 +1218,9 @@
             dvs_above = [dvs[0], swap(dvs[1], "fsdp", 1)]
         else:
             table_list[l] = lax.psum_scatter(dvs[0], "fsdp", scatter_dimension=0, tiled=True).astype(f32)
+        if not top:
+            back_all = lax.all_gather(after([back_box], line)[0], TA, axis=0, tiled=False)
+            gw, back_all = after([gw, back_all])
         gw = lax.all_to_all(gw, ("ctx", "tp"), 0, 0, tiled=True)
         back_shape = shape((chunk, 10 * HD), bf16)
         g_mid, go_chunk, gain_rows[layers + l], *back = kernel_call(
@@ -1246,15 +1266,17 @@
             below_all = lax.all_gather(after([kept[l - 1][10]], line)[0], TA, axis=0, tiled=False)
         else:
             forward_all = below_all
-        back_all = lax.all_gather(after([back_box], line)[0], TA, axis=0, tiled=False)
+        if top:
+            back_all = lax.all_gather(after([back_box], line)[0], TA, axis=0, tiled=False)
         if top:
             output = back_all[:, :, d_model:].reshape(tokens, d_model)
+        riders = [] if l else [inputs[0], *gain_rows[1:]]
         g_qkv, *parts = kernel_call(
-            functools.partial(qkv_back_kernel, plan=plan),
+            functools.partial(qkv_back_kernel, plan=plan, row=l, gain_rows=len(riders)),
             "qkv_back",
-            [shape((tokens, 3 * width), bf16)] + [part_shape] * 4,
+            [shape((tokens, 3 * width), bf16)] + [part_shape if l else shape((chunk + 16, d_model), bf16)] * 4,
             idx,
-            [*head_grads, *w_qkv[l]],
+            [*head_grads, *w_qkv[l], *riders],
             [pack_scratch, part_scratch],
         )
         parts = swaps(parts, TA)
@@ -1288,14 +1310,16 @@
             qkv_quarters = kernel_call(
                 add_two_kernel, "qkv_add", [quarter] * 4, idx, [qkv_packs[0], swap(qkv_packs[1], "fsdp", 1)]
             )
-            (pack,) = kernel_call(
-                add_pair_kernel,
+            quarter = shape((weight_rows // 4, 256), bf16)
+            weight_quarters = kernel_call(
+                add_two_kernel,
                 "weight_add",
-                [shape((weight_rows, 256), bf16)],
+                [quarter] * 4,
                 idx,
                 [weight_packs[0], swap(weight_packs[1], "fsdp", 1)],
             )
-            packs[l] = [lax.psum(pack, "ctx")]
+            weight_quarters = swaps(weight_quarters, "ctx")
+            parts[3], *weight_quarters = after([parts[3], *weight_quarters])
         else:
             parts[3], weight_packs[0], qkv_packs[0], below_all = after(
                 [parts[3], weight_packs[0], qkv_packs[0], below_all]
@@ -1312,47 +1336,41 @@
                 [chunk_scratch],
             )
         else:
-            (g,) = kernel_call(
+            g, gain_all, *gain_halves = kernel_call(
                 functools.partial(norm_back_last_kernel, plan=plan, row=l),
                 "norm_back_last",
-                [shape((chunk + 16, d_model), bf16)],
+                [part_shape, shape((16, d_model), f32), shape((16, 256), bf16), shape((16, 256), bf16)],
                 idx,
-                [*parts, x, g_mid, gains, *gain_rows[1:]],
-                [pltpu.VMEM((1, d_model), f32)],
+                [*parts, x, g_mid, gains],
             )
-    g_chunks = spread(g, TA)
-    input_gradient, gain_all, *gain_halves = kernel_call(
-        functools.partial(input_grad_kernel, plan=plan),
+    (input_gradient,) = kernel_call(
+        functools.partial(place_kernel, plan=plan),
         "input_gradient",
-        [
-            shape((tokens, d_model), f32),
-            shape((16, d_model), f32),
-            shape((16, 256), bf16),
-            shape((16, 256), bf16),
-        ],
+        [shape((tokens, d_model), f32)],
         idx,
-        g_chunks,
+        spread(g, TA),
     )
     if shards != 2:
         table_grads = jnp.stack(table_list)
     gain_shapes = []
     if shards == 2:
-        rows = qkv_rows // 4
+        rows = (weight_rows + qkv_rows) // 4
         (part,) = kernel_call(
             plane_sum_kernel,
             "plane_sum",
             [shape((rows + 16, 256), bf16)],
             idx,
-            [*swaps(qkv_quarters, "ctx"), gain_halves[0], swap(gain_halves[1], "fsdp", 1)],
-        )
+            [*weight_quarters, *swaps(qkv_quarters, "ctx"), gain_halves[0], swap(gain_halves[1], "fsdp", 1)],
+        )
+        part, *packs[1] = after([part, *packs[1]])
         late = spread(part, "ctx")
         gain_shapes = [shape((layers, d_model // 2), f32)] * 2
-        flat = [packs[l][0] for l in range(layers)] + [packs[l][1] for l in range(1, layers)] + late
+        flat = late + [p for l in range(1, layers) for p in packs[l]]
     else:
         gain_all = lax.psum(
             lax.psum_scatter(gain_all[: 2 * layers], "fsdp", scatter_dimension=1, tiled=True), "ctx"
         )
-        flat = [packs[l][n] for n in range(2) for l in range(layers)]
+        flat = [p for l in range(layers) for p in packs[l]]
     shard_size = d_model // shards
     tall = shape((layers, shard_size, width), f32)
     wide = shape((layers, width, shard_size), f32)
@@ -1364,7 +1382,7 @@
         + gain_shapes,
         idx,
         flat,
-        [pltpu.VMEM((qkv_rows, 256), bf16)] if shards == 2 else [],
+        [pltpu.VMEM((weight_rows, 256), bf16), pltpu.VMEM((qkv_rows, 256), bf16)] if shards == 2 else [],
     )
     gain_grads = grads[9:] if shards == 2 else [gain_all[:layers], gain_all[layers:]]
     return (

time: 615 us -> 590 us (0.959)
  blocking collectives: 41.3 us -> 27.3 us
  local copies, waits for them, and re-layouts: 67.2 us -> 57.1 us
    all_to_all x2 -> x1, blocking collectives: 29.1 us -> 15.2 us  [body(): gw = lax.all_to_all(gw, ('ctx', 'tp'), 0, 0, tiled=True)]
    unnamed x282 -> x258, local copies, waits for them, and re-layouts: 53 us -> 42.9 us
    psum x1, waiting for transfers between devices: 7.37 us -> 0.01 us  [reduce_packs(): return [lax.psum(p, 'ctx') for p in scattered]]
    ppermute x98 -> x101, starting transfers between devices: 123 us -> 119 us  [swap(): return lax.ppermute(x, axis, [(i, i ^ step) for i in range(size)])]
    ppermute x98 -> x101, waiting for transfers between devices: 176 us -> 173 us  [swap(): return lax.ppermute(x, axis, [(i, i ^ step) for i in range(size)])]
  transfers between devices with their start and end apart: 110 -> 114, of which waited for: 56 -> 57; matrix products, arithmetic and copies ran while one was open for 2% -> 3% of each run, Pallas kernels for 23% -> 23%
where the time goes in v4:
time: 590 us; the launch traced here: 585 us
  waiting for transfers between devices  192 us (33%)
  Pallas kernels  158 us (27%)
  starting transfers between devices  129 us (22%)
  local copies, waits for them, and re-layouts  57.1 us (10%)
  blocking collectives  27.3 us (5%)
  between operations  15.3 us (3%)
    ppermute x101, waiting for transfers between devices, swap(): return lax.ppermute(x, axis, [(i, i ^ step) for i in range(size)])  173 us
    ppermute x101, starting transfers between devices, swap(): return lax.ppermute(x, axis, [(i, i ^ step) for i in range(size)])  119 us
    pallas_call x35, Pallas kernels, kernel_call(): pl.pallas_call(body, out_shape=outs, in_specs=in_specs, out_specs=[pl.Blo...  96.6 us
    unnamed x258, local copies, waits for them, and re-layouts  42.9 us
    pallas_call x2, Pallas kernels, write_call(): pl.pallas_call(functools.partial(write_kernel, plan=plan, pieces=pieces,...  28.6 us
    pallas_call x2, Pallas kernels, read_call(): pl.pallas_call(functools.partial(read_kernel, plan=plan, pieces=len(value...  19.3 us
    all_to_all x1, blocking collectives, body(): gw = lax.all_to_all(gw, ('ctx', 'tp'), 0, 0, tiled=True)  15.2 us
    pallas_call x2, Pallas kernels, table_grad_call(): pl.pallas_call(table_grad_kernel, grid=(rows // block,), out_shape=shape(...  13 us
  transfers between devices with their start and end apart: 114, of which 57 were waited for; matrix products, arithmetic and copies ran while one was open for 3% of the time, Pallas kernels for 23%

profile of v4, /device:TPU:0, one launch (start us, length us, event | category | flops | bytes accessed | tf_op | source)
XLA Modules:
  0.0 584.7 jit_solution(10119560826802301506)
XLA Ops:
  55.0 6.8 %collective-permute-done.13.r2 = bf16[64,1024]{1,0:T(8,128)(2,1)S(1)} collective-permute-done((bf16[64,1024]{1,0:T(8,128)(2,1)}, bf16[64,1024]{1,0:T(8,128)(2,1)S(1)}, u32[]{:S(2)}, u32[]{:S(2)}) %collective-permute-start.13) | collective-permute-done | bytes 131104 | tf_op jit(solution)/shard_map/ppermute | solution.py:34
  63.1 5.8 lookup.2
  79.6 8.6 %all-to-all-done.w_ref.names_ref = bf16[16,64,128]{2,1,0:T(8,128)(2,1)S(1)} async-done(((bf16[16,64,128]{2,1,0:T(8,128)(2,1)}), bf16[16,64,128]{2,1,0:T(8,128)(2,1)S(1)}, u32[]{:S(2)}, u32[]{:S(2)}) %all-to-all-start) | async-done | bytes 262176 | tf_op jit(solution)/shard_map/all_to_all | solution.py:1159
  88.3 9.7 %memory_read.2 = (bf16[256,1024]{1,0:T(8,128)(2,1)S(1)}, bf16[256,1024]{1,0:T(8,128)(2,1)S(1)}, bf16[256,1024]{1,0:T(8,128)(2,1)S(1)}, bf16[256,1024]{1,0:T(8,128)(2,1)S(1)}, f32[16,128,256]{2,1,0:T(8,128)}) custom-call(s32[4]{0:T(128)S(1)} %pad_add_fusion.idx, bf16[16,64,128]{2,1,0:T(8,128)(2,1)S(1)} %all-to-all-done.w_ref.names_ref, ...), custom_call_target="tpu_custom_call" | custom-call | flops 2147483648 | bytes 20971520 | tf_op jit(solution)/shard_map/memory_read/pallas_call | solution.py:802
  101.6 7.8 %collective-permute-done.16.r1 = bf16[256,1024]{1,0:T(8,128)(2,1)S(1)} collective-permute-done((bf16[256,1024]{1,0:T(8,128)(2,1)S(1)}, bf16[256,1024]{1,0:T(8,128)(2,1)S(1)}, u32[]{:S(2)}, u32[]{:S(2)}) %collective-permute-start.16) | collective-permute-done | bytes 524320 | tf_op jit(solution)/shard_map/ppermute | solution.py:34
  200.9 12.1 %all_to_all.20.w_ref = bf16[16,32,128]{2,1,0:T(8,128)(2,1)S(1)} all-to-all(bf16[16,32,128]{2,1,0:T(8,128)(2,1)} %copy-done.92), channel_id=1, replica_groups=mesh['fsdp'=2,'ctx'=4,'tp'=4] {'ctx','tp'}, dimensions={0} | all-to-all | bytes 262144 | tf_op jit(solution)/shard_map/all_to_all | solution.py:1159
  213.0 9.6 %memory_read.3 = (bf16[256,1024]{1,0:T(8,128)(2,1)S(1)}, bf16[256,1024]{1,0:T(8,128)(2,1)S(1)}, bf16[256,1024]{1,0:T(8,128)(2,1)S(1)}, bf16[256,1024]{1,0:T(8,128)(2,1)S(1)}, f32[16,128,256]{2,1,0:T(8,128)}) custom-call(s32[4]{0:T(128)S(1)} %pad_add_fusion.idx, bf16[16,32,128]{2,1,0:T(8,128)(2,1)S(1)} %all_to_all.20.w_ref, ...), custom_call_target="tpu_custom_call" | custom-call | flops 2147483648 | bytes 20971520 | tf_op jit(solution)/shard_map/memory_read/pallas_call | solution.py:802
  226.2 11.4 %collective-permute-done.36.r1 = bf16[256,1024]{1,0:T(8,128)(2,1)S(1)} collective-permute-done((bf16[256,1024]{1,0:T(8,128)(2,1)S(1)}, bf16[256,1024]{1,0:T(8,128)(2,1)S(1)}, u32[]{:S(2)}, u32[]{:S(2)}) %collective-permute-start.36) | collective-permute-done | bytes 524320 | tf_op jit(solution)/shard_map/ppermute | solution.py:34
  237.5 7.1 %collective-permute-done.37.r2 = bf16[256,1024]{1,0:T(8,128)(2,1)S(1)} collective-permute-done((bf16[256,1024]{1,0:T(8,128)(2,1)S(1)}, bf16[256,1024]{1,0:T(8,128)(2,1)S(1)}, u32[]{:S(2)}, u32[]{:S(2)}) %collective-permute-start.37) | collective-permute-done | bytes 524320 | tf_op jit(solution)/shard_map/ppermute | solution.py:34
  279.2 10.3 %collective-permute-done.47.g3 = bf16[256,1024]{1,0:T(8,128)(2,1)S(1)} collective-permute-done((bf16[256,1024]{1,0:T(8,128)(2,1)}, bf16[256,1024]{1,0:T(8,128)(2,1)S(1)}, u32[]{:S(2)}, u32[]{:S(2)}) %collective-permute-start.47) | collective-permute-done | bytes 524320 | tf_op jit(solution)/shard_map/ppermute | solution.py:34
  295.0 14.4 %memory_write.2 = (bf16[2048,1024]{1,0:T(8,128)(2,1)}, bf16[2048,1024]{1,0:T(8,128)(2,1)}, bf16[16,32,128]{2,1,0:T(8,128)(2,1)S(1)}) custom-call(s32[4]{0:T(128)S(1)} %pad_add_fusion.idx, bf16[256,1024]{1,0:T(8,128)(2,1)} %constant_dynamic-update-slice_fusion.g0, bf16[256,1024]{1,0:T(8,128)(2,1)S(1)} %collective-permute-done.45.g1, ...), custom_call_target="tpu_custom_call" | custom-call | flops 3221225472 | bytes 29360128 | tf_op jit(solution)/shard_map/memory_write/pallas_call | solution.py:899
  309.5 15.2 %all_to_all.21.gw_ref = bf16[16,32,128]{2,1,0:T(8,128)(2,1)S(1)} all-to-all(bf16[16,32,128]{2,1,0:T(8,128)(2,1)S(1)} %get-tuple-element.292), channel_id=1, replica_groups=mesh['fsdp'=2,'ctx'=4,'tp'=4] {'ctx','tp'}, dimensions={0} | all-to-all | bytes 262144 | tf_op jit(solution)/shard_map/all_to_all | solution.py:1224
  324.8 5.8 lookup_back.2
  340.0 8.4 %collective-permute-done.49.g2 = bf16[64,1024]{1,0:T(8,128)(2,1)S(1)} collective-permute-done((bf16[64,1024]{1,0:T(8,128)(2,1)S(1)}, bf16[64,1024]{1,0:T(8,128)(2,1)S(1)}, u32[]{:S(2)}, u32[]{:S(2)}) %collective-permute-start.49) | collective-permute-done | bytes 131104 | tf_op jit(solution)/shard_map/ppermute | solution.py:34
  357.1 5.8 attend_back.2
  416.7 6.2 %table_grad.2.refs_0_ = f32[2,2048,1024]{2,1,0:T(8,128)} custom-call(bf16[2048,1024]{1,0:T(8,128)(2,1)S(1)} %copy-done.8, bf16[2048,1024]{1,0:T(8,128)(2,1)} %collective-permute-done.69.b_ref), custom_call_target="tpu_custom_call" | custom-call | bytes 16777216 | tf_op jit(solution)/shard_map/table_grad/pallas_call | solution.py:951
  423.5 10.1 %collective-permute-done.67.g2 = bf16[256,1024]{1,0:T(8,128)(2,1)S(1)} collective-permute-done((bf16[256,1024]{1,0:T(8,128)(2,1)S(1)}, bf16[256,1024]{1,0:T(8,128)(2,1)S(1)}, u32[]{:S(2)}, u32[]{:S(2)}) %collective-permute-start.67) | collective-permute-done | bytes 524320 | tf_op jit(solution)/shard_map/ppermute | solution.py:34
  433.7 14.1 %memory_write.3 = (bf16[2048,1024]{1,0:T(8,128)(2,1)}, bf16[2048,1024]{1,0:T(8,128)(2,1)}, bf16[16,32,128]{2,1,0:T(8,128)(2,1)S(1)}) custom-call(s32[4]{0:T(128)S(1)} %pad_add_fusion.idx, bf16[256,1024]{1,0:T(8,128)(2,1)S(1)} %constant_dynamic-update-slice_fusion.4.g0, bf16[256,1024]{1,0:T(8,128)(2,1)S(1)} %collective-permute-done.66.g1, ...), custom_call_target="tpu_custom_call" | custom-call | flops 3221225472 | bytes 29360128 | tf_op jit(solution)/shard_map/memory_write/pallas_call | solution.py:899
  452.9 5.9 %reduce-scatter.3.cloned.1.call-done = bf16[1,1856,256]{2,1,0:T(8,128)(2,1)} async-done(((bf16[2,1856,256]{2,1,0:T(8,128)(2,1)}), bf16[1,1856,256]{2,1,0:T(8,128)(2,1)}) %reduce-scatter.3.cloned.1.call-update) | async-done | bytes 950288 | tf_op jit(solution)/shard_map/reduce_scatter | solution.py:981
  463.0 5.9 %lookup_back.3 = (f32[64,1024]{1,0:T(8,128)S(1)}, bf16[64,1024]{1,0:T(8,128)(2,1)S(1)}, f32[1,1024]{1,0:T(1,128)S(1)}, bf16[64,640]{1,0:T(8,128)(2,1)S(1)}, bf16...) custom-call(s32[4]{0:T(128)S(1)} %pad_add_fusion.idx, ...), custom_call_target="tpu_custom_call" | custom-call | bytes 7344128 | tf_op jit(solution)/shard_map/lookup_back/pallas_call | solution.py:54
  483.6 6.8 %table_grad.3 = f32[2,2048,1024]{2,1,0:T(8,128)} custom-call(bf16[2048,1024]{1,0:T(8,128)(2,1)S(1)} %copy-done.7, bf16[2048,1024]{1,0:T(8,128)(2,1)} %collective-permute-done.73.b_ref, f32[2,2048,1024]{2,1,0:T(8,128)} %table_grad.2.refs_0_), custom_call_target="tpu_custom_call", output_to_operand_aliasing={{}: (2, {})} | custom-call | bytes 16777216 | tf_op jit(solution)/shard_map/table_grad/pallas_call | solution.py:951
  503.0 5.8 attend_back.3
  541.6 5.7 collective-permute-done.84.r2
  557.4 5.6 collective-permute-done.92.c3
  (550 shorter events, 364.3 us)
Async XLA Ops:
  7.2 54.6 %all-gather.16.cloned.1.call-start = ((), (), s32[]{:S(2)}) async-start(), calls=%async_computation.6 | async-start | bytes 1474560 | tf_op jit(solution)/shard_map/all_gather | solution.py:1034
  20.3 102.1 %all-gather.18.cloned.1.call-start = ((), (), s32[]{:S(2)}) async-start(), calls=%async_computation.9 | async-start | bytes 4718592 | tf_op jit(solution)/shard_map/all_gather | solution.py:1034
  20.9 67.3 %collective-permute-start.15 = (bf16[2,2048,1024]{2,1,0:T(8,128)(2,1)}, bf16[2,2048,1024]{2,1,0:T(8,128)(2,1)}, u32[]{:S(2)}, u32[]{:S(2)}) collective-permute-start(bf16[2,2048,1024]{2,1,0:T(8,128)(2,1)} %refs_0_.7), channel_id=1, source_target_pairs={{0,16},{16,0},{1,17},{17,1},{2,18},{18,2},{3,19},{19,3},{4,20},{20... | collective-permute-start | bytes 25165832 | tf_op jit(solution)/shard_map/ppermute | solution.py:34
  74.0 114.7 %all-gather.20.cloned.1.call-start = ((), (), s32[]{:S(2)}) async-start(), calls=%async_computation.10 | async-start | bytes 1474560 | tf_op jit(solution)/shard_map/all_gather | solution.py:1034
  101.5 40.1 %collective-permute-start.25 = (bf16[512,768]{1,0:T(8,128)(2,1)S(1)}, bf16[512,768]{1,0:T(8,128)(2,1)}, u32[]{:S(2)}, u32[]{:S(2)}) collective-permute-start(bf16[512,768]{1,0:T(8,128)(2,1)S(1)} %pad_maximum_fusion.1.refs_0_), channel_id=1, source_target_pairs={{0,16},{16,0},{1,17},{17,1},{2,18},{18,2},{3,19},{19,3},{4,20},{20... | collective-permute-start | bytes 2359304 | tf_op jit(solution)/shard_map/ppermute | solution.py:34
  151.8 99.2 %all-gather.22.cloned.1.call-start = ((), (), s32[]{:S(2)}) async-start(), calls=%async_computation.11 | async-start | bytes 4718592 | tf_op jit(solution)/shard_map/all_gather | solution.py:1034
  200.8 179.5 %all-gather.24.cloned.1.call-start = ((), (), s32[]{:S(2)}) async-start(), calls=%async_computation.12 | async-start | bytes 1310720 | tf_op jit(solution)/shard_map/all_gather | solution.py:1270
  223.5 21.1 %collective-permute-start.37 = (bf16[256,1024]{1,0:T(8,128)(2,1)S(1)}, bf16[256,1024]{1,0:T(8,128)(2,1)S(1)}, u32[]{:S(2)}, u32[]{:S(2)}) collective-permute-start(bf16[256,1024]{1,0:T(8,128)(2,1)S(1)} %get-tuple-element.279), channel_id=1, source_target_pairs={{0,8},{4,12},{8,0},{12,4},{1,9},{5,13},{9,1},{13,5},{2,10},{6,14},... | collective-permute-start | bytes 1572872 | tf_op jit(solution)/shard_map/ppermute | solution.py:34
  224.2 20.4 %collective-permute-start.38 = (bf16[256,1024]{1,0:T(8,128)(2,1)S(1)}, bf16[256,1024]{1,0:T(8,128)(2,1)S(1)}, u32[]{:S(2)}, u32[]{:S(2)}) collective-permute-start(bf16[256,1024]{1,0:T(8,128)(2,1)S(1)} %get-tuple-element.280), channel_id=1, source_target_pairs={{0,12},{4,8},{8,4},{12,0},{1,13},{5,9},{9,5},{13,1},{2,14},{6,10},... | collective-permute-start | bytes 1572872 | tf_op jit(solution)/shard_map/ppermute | solution.py:34
  274.3 106.1 %all-gather.26.cloned.1.call-start = ((), (), s32[]{:S(2)}) async-start(), calls=%async_computation.13 | async-start | bytes 1310720 | tf_op jit(solution)/shard_map/all_gather | solution.py:1265
  274.9 114.3 %all-gather.28.cloned.1.call-start = ((), (), s32[]{:S(2)}) async-start(), calls=%async_computation.14 | async-start | bytes 1310720 | tf_op jit(solution)/shard_map/all_gather | solution.py:1266
  275.6 172.9 %all-gather.30.cloned.1.call-start = ((), (), s32[]{:S(2)}) async-start(), calls=%async_computation.15 | async-start | bytes 1310720 | tf_op jit(solution)/shard_map/all_gather | solution.py:1222
  406.9 46.1 %reduce-scatter.5.cloned.1.call-start = ((), (), s32[]{:S(2)}) async-start(), calls=%async_computation.8 | async-start | bytes 2359296 | tf_op jit(solution)/shard_map/reduce_scatter | solution.py:981
  407.6 51.3 %reduce-scatter.3.cloned.1.call-start = ((), (), s32[]{:S(2)}) async-start(), calls=%async_computation.7 | async-start | bytes 2850816 | tf_op jit(solution)/shard_map/reduce_scatter | solution.py:981
  409.2 24.4 %collective-permute-start.67 = (bf16[256,1024]{1,0:T(8,128)(2,1)S(1)}, bf16[256,1024]{1,0:T(8,128)(2,1)S(1)}, u32[]{:S(2)}, u32[]{:S(2)}) collective-permute-start(bf16[256,1024]{1,0:T(8,128)(2,1)S(1)} %constant_dynamic-update-slice_fusion.4.g0), channel_id=1, source_target_pairs={{0,8},{4,12},{8,0},{12,4},{1,9},{5,13},{9,1},{13,5},{2,10},{6,14},... | collective-permute-start | bytes 1572872 | tf_op jit(solution)/shard_map/ppermute | solution.py:34
  409.7 23.9 %collective-permute-start.66 = (bf16[256,1024]{1,0:T(8,128)(2,1)S(1)}, bf16[256,1024]{1,0:T(8,128)(2,1)S(1)}, u32[]{:S(2)}, u32[]{:S(2)}) collective-permute-start(bf16[256,1024]{1,0:T(8,128)(2,1)S(1)} %constant_dynamic-update-slice_fusion.4.g0), channel_id=1, source_target_pairs={{0,4},{4,0},{8,12},{12,8},{1,5},{5,1},{9,13},{13,9},{2,6},{6,2},{1... | collective-permute-start | bytes 1572872 | tf_op jit(solution)/shard_map/ppermute | solution.py:34
  448.5 32.2 %collective-permute-start.73 = (bf16[2048,1024]{1,0:T(8,128)(2,1)}, bf16[2048,1024]{1,0:T(8,128)(2,1)}, u32[]{:S(2)}, u32[]{:S(2)}) collective-permute-start(bf16[2048,1024]{1,0:T(8,128)(2,1)} %get-tuple-element.341), channel_id=1, source_target_pairs={{0,16},{16,0},{1,17},{17,1},{2,18},{18,2},{3,19},{19,3},{4,20},{20... | collective-permute-start | bytes 12582920 | tf_op jit(solution)/shard_map/ppermute | solution.py:34
  452.9 98.5 %all-reduce.3.cloned.1.call-start = ((), (), s32[]{:S(2)}) async-start(), calls=%async_computation.16 | async-start | bytes 3473408 | tf_op jit(solution)/shard_map/psum | solution.py:982
  469.6 20.8 %collective-permute-start.71 = (bf16[64,1024]{1,0:T(8,128)(2,1)S(1)}, bf16[64,1024]{1,0:T(8,128)(2,1)S(1)}, u32[]{:S(2)}, u32[]{:S(2)}) collective-permute-start(bf16[64,1024]{1,0:T(8,128)(2,1)S(1)} %get-tuple-element.339.g0), channel_id=1, source_target_pairs={{0,2},{1,3},{2,0},{3,1},{4,6},{5,7},{6,4},{7,5},{8,10},{9,11},{10,... | collective-permute-start | bytes 393224 | tf_op jit(solution)/shard_map/ppermute | solution.py:34
  473.4 19.1 %collective-permute-start.77 = (bf16[64,640]{1,0:T(8,128)(2,1)S(1)}, bf16[64,640]{1,0:T(8,128)(2,1)S(1)}, u32[]{:S(2)}, u32[]{:S(2)}) collective-permute-start(bf16[64,640]{1,0:T(8,128)(2,1)S(1)} %get-tuple-element.349), channel_id=1, source_target_pairs={{0,1},{1,0},{2,3},{3,2},{4,5},{5,4},{6,7},{7,6},{8,9},{9,8},{10,11... | collective-permute-start | bytes 245768 | tf_op jit(solution)/shard_map/ppermute | solution.py:34
  498.4 23.0 %collective-permute-start.86 = (bf16[1856,256]{1,0:T(8,128)(2,1)S(1)}, bf16[1856,256]{1,0:T(8,128)(2,1)S(1)}, u32[]{:S(2)}, u32[]{:S(2)}) collective-permute-start(bf16[1856,256]{1,0:T(8,128)(2,1)S(1)} %get-tuple-element.373), channel_id=1, source_target_pairs={{0,16},{16,0},{1,17},{17,1},{2,18},{18,2},{3,19},{19,3},{4,20},{20... | collective-permute-start | bytes 2850824 | tf_op jit(solution)/shard_map/ppermute | solution.py:34
  526.5 22.1 %collective-permute-start.94 = (bf16[384,256]{1,0:T(8,128)(2,1)S(1)}, bf16[384,256]{1,0:T(8,128)(2,1)S(1)}, u32[]{:S(2)}, u32[]{:S(2)}) collective-permute-start(bf16[384,256]{1,0:T(8,128)(2,1)S(1)} %get-tuple-element.390), channel_id=1, source_target_pairs={{0,4},{4,0},{8,12},{12,8},{1,5},{5,1},{9,13},{13,9},{2,6},{6,2},{1... | collective-permute-start | bytes 589832 | tf_op jit(solution)/shard_map/ppermute | solution.py:34
  552.1 21.6 %collective-permute-start.99 = (bf16[864,256]{1,0:T(8,128)(2,1)}, bf16[864,256]{1,0:T(8,128)(2,1)S(1)}, u32[]{:S(2)}, u32[]{:S(2)}) collective-permute-start(bf16[864,256]{1,0:T(8,128)(2,1)} %plane_sum.1.refs_0_), channel_id=1, source_target_pairs={{0,8},{4,12},{8,0},{12,4},{1,9},{5,13},{9,1},{13,5},{2,10},{6,14},... | collective-permute-start | bytes 1327112 | tf_op jit(solution)/shard_map/ppermute | solution.py:34
  553.5 20.3 %collective-permute-start.98 = (bf16[864,256]{1,0:T(8,128)(2,1)}, bf16[864,256]{1,0:T(8,128)(2,1)S(1)}, u32[]{:S(2)}, u32[]{:S(2)}) collective-permute-start(bf16[864,256]{1,0:T(8,128)(2,1)} %plane_sum.1.refs_0_), channel_id=1, source_target_pairs={{0,4},{4,0},{8,12},{12,8},{1,5},{5,1},{9,13},{13,9},{2,6},{6,2},{1... | collective-permute-start | bytes 1327112 | tf_op jit(solution)/shard_map/ppermute | solution.py:34
  (216 other events, 2320.4 us)
Sparse Core Ops, SparseCore 0:
  20.5 29.4 all-gather.15
  69.1 48.3 all-gather.17
  152.0 22.8 all-gather.19
  201.0 46.3 all-gather.21
  274.4 26.6 all-gather.23
  302.5 35.9 all-gather.25
  340.0 30.9 all-gather.27
  407.0 25.7 all-gather.29
  435.1 8.5 reduce-scatter.4
  448.6 10.1 reduce-scatter.2
  462.1 64.9 all-reduce.2

commit v5 on v4

--- a/solution.py
+++ b/solution.py
@@ -47,6 +47,7 @@
 
 
 def kernel_call(body, name, outs, idx, args, scratch=(), limit=50, flops=0):
+    limit = {'norm_back_last': 16, 'plane_sum': 16, 'input_gradient': 16, 'finalize': 24, 'weight_add': 16, 'qkv_add': 16}.get(name, limit)
     in_specs = [pl.BlockSpec(memory_space=pltpu.SMEM)]
     in_specs += [pl.BlockSpec(memory_space=pltpu.VMEM) for _ in args]
     moved = sum(a.size * a.dtype.itemsize for a in args)
@@ -724,6 +725,30 @@
     return ((idx[0] ^ piece) * per_piece + step % per_piece) * STEP_GROUPS
 
 
+def block_rows():
+    return STEP_GROUPS * NSUB
+
+
+def start_values(vs, layer, buffer, sems):
+    copies = []
+    for v in vs:
+        for c in range(v.shape[1] // block_rows()):
+            n = len(copies)
+            copies.append(
+                pltpu.make_async_copy(
+                    v.at[layer, pl.ds(c * block_rows(), block_rows()), :],
+                    buffer.at[pl.ds(n * block_rows(), block_rows()), :],
+                    sems.at[n],
+                )
+            )
+            copies[-1].start()
+    return copies
+
+
+def names_of(names_ref, src, layer):
+    return names_ref[src, 32 + 16 * layer : 48 + 16 * layer, :].astype(f32)
+
+
 def read_kernel(idx, w_ref, names_ref, *refs, plan, pieces, per_piece):
     vs = refs[:pieces]
     o0, o1, o2, o3, s_ref, partial, rows = refs[pieces:]
@@ -823,100 +848,97 @@
     )(idx, weights, names, *values)
 
 
-def write_kernel(idx, g0, g1, g2, g3, names_ref, s_ref, *refs, plan, pieces, per_piece):
+def value_blocks(values):
+    return sum(v.shape[1] for v in values) // block_rows()
+
+
+def write_kernel(idx, g0, g1, g2, g3, names_ref, s_ref, *refs, plan, pieces, layer):
     vs, dvs = refs[:pieces], refs[pieces : 2 * pieces]
-    gw_ref, grads, partial, cross = refs[2 * pieces :]
-    step = pl.program_id(0)
+    gw_ref, grads, partial, cross, buffer, changes, sems, out_sems = refs[2 * pieces :]
     sources, width, _ = s_ref.shape
-    d_model = vs[0].shape[1]
-
-    @pl.when(step == 0)
-    def _():
-        s, t = idx[plan.si], idx[plan.ti]
-        tokens = grads.shape[1]
-        chunk = tokens // 4
-        for dp, g in enumerate((g0, g1, g2, g3)):
-            for dz in range(4):
-                ds, dt = plan.rel(dp, dz)
-                grads[s ^ ds, rows_at(t ^ dt, chunk), :] = g[chunk * dz : chunk * (dz + 1), :]
-        iota = (lax.broadcasted_iota(jnp.int32, (tokens, width), 0) + 1).astype(f32)
-        for sa in range(4):
-            hits = []
-            for m in range(4):
-                token = names_ref[plan.src(sa, m)].astype(f32)[8:9, :]
-                hits.append(jnp.where(iota == token, 1.0, 0.0).astype(bf16))
-            got = dot_tn(jnp.concatenate(hits, axis=1), grads[sa])
-            for m in range(4):
-                partial[plan.src(sa, m)] = got[width * m : width * (m + 1), :]
-
-    base = step_base(idx, step, pieces, per_piece)
-
-    def multiply(v_ref, dv_ref):
+    d_model = buffer.shape[1]
+    copies = start_values(vs, layer, buffer, sems)
+    s, t = idx[plan.si], idx[plan.ti]
+    tokens = grads.shape[1]
+    chunk = tokens // 4
+    for dp, g in enumerate((g0, g1, g2, g3)):
+        for dz in range(4):
+            ds, dt = plan.rel(dp, dz)
+            grads[s ^ ds, rows_at(t ^ dt, chunk), :] = g[chunk * dz : chunk * (dz + 1), :]
+    iota = (lax.broadcasted_iota(jnp.int32, (tokens, width), 0) + 1).astype(f32)
+    for sa in range(4):
+        hits = []
+        for m in range(4):
+            token = names_of(names_ref, plan.src(sa, m), layer)[8:9, :]
+            hits.append(jnp.where(iota == token, 1.0, 0.0).astype(bf16))
+        got = dot_tn(jnp.concatenate(hits, axis=1), grads[sa])
+        for m in range(4):
+            partial[plan.src(sa, m)] = got[width * m : width * (m + 1), :]
+    leaving = []
+    per_piece = len(copies) // pieces
+    for step, copy in enumerate(copies):
+        copy.wait()
+        base = step_base(idx, step, pieces, per_piece)
         for k in range(STEP_GROUPS):
             at = rows_at(base + k, CAP)
-            cut = slice(NSUB * k, NSUB * (k + 1))
+            n = step * block_rows() + NSUB * k
             inbox = partial[:, at, :].reshape(sources * CAP, d_model).astype(bf16)
             left = s_ref[:, at, :].reshape(sources * CAP, NSUB).astype(bf16)
-            dv_ref[cut, :] = dot_tn(left, inbox).astype(bf16)
-            cross[:, at, :] = dot_nt(inbox, v_ref[cut, :]).reshape(sources, CAP, NSUB)
-
-    for n in range(pieces):
-        pl.when(step // per_piece == n)(functools.partial(multiply, vs[n], dvs[n]))
-
-    @pl.when(step == pl.num_programs(0) - 1)
-    def _():
-        iota = lax.broadcasted_iota(jnp.int32, (NSUB, width), 0).astype(f32)
-
-        def select(sa, carry):
-            picked = []
-            for m in range(4):
-                src = plan.src(sa, m)
-                turned = cross[src].T
-                names = names_ref[src].astype(f32)
-                picked += [
-                    jnp.sum(jnp.where(iota == names[b : b + 1, :], turned, 0.0), axis=0, keepdims=True)
-                    for b in range(8)
-                ]
-            picked = jnp.concatenate(picked, axis=0).astype(bf16)
-            for ta in range(4):
-                gw_ref[plan.src(sa, ta)] = picked
-            return carry
-
-        lax.fori_loop(0, 4, select, 0)
+            changes[n : n + NSUB, :] = dot_tn(left, inbox).astype(bf16)
+            cross[:, at, :] = dot_nt(inbox, buffer[n : n + NSUB, :]).reshape(sources, CAP, NSUB)
+        leaving.append(
+            pltpu.make_async_copy(
+                changes.at[pl.ds(step * block_rows(), block_rows()), :],
+                dvs[step // per_piece].at[pl.ds(step % per_piece * block_rows(), block_rows()), :],
+                out_sems.at[step],
+            )
+        )
+        leaving[-1].start()
+    iota = lax.broadcasted_iota(jnp.int32, (NSUB, width), 0).astype(f32)
+
+    def select(sa, carry):
+        picked = []
+        for m in range(4):
+            src = plan.src(sa, m)
+            turned = cross[src].T
+            names = names_of(names_ref, src, layer)
+            picked += [
+                jnp.sum(jnp.where(iota == names[b : b + 1, :], turned, 0.0), axis=0, keepdims=True)
+                for b in range(8)
+            ]
+        picked = jnp.concatenate(picked, axis=0).astype(bf16)
+        for ta in range(4):
+            gw_ref[plan.src(sa, ta)] = picked
+        return carry
+
+    lax.fori_loop(0, 4, select, 0)
+    for copy in leaving:
+        copy.wait()
 
 
 def write_call(idx, grads, names, layer, dense, values, plan, tokens):
     sources, width, _ = dense.shape
-    specs, per_piece = value_specs(values, layer)
     d_model = values[0].shape[2]
     pieces = len(values)
-
-    def dv_spec(n):
-        return pl.BlockSpec(
-            (STEP_GROUPS * NSUB, d_model), lambda g: (jnp.clip(g - n * per_piece, 0, per_piece - 1), 0)
-        )
-
+    blocks = value_blocks(values)
+    whole = pltpu.VMEM((blocks * block_rows(), d_model), bf16)
     return pl.pallas_call(
-        functools.partial(write_kernel, plan=plan, pieces=pieces, per_piece=per_piece),
-        grid=(per_piece * pieces,),
+        functools.partial(write_kernel, plan=plan, pieces=pieces, layer=layer),
         out_shape=[shape((v.shape[1], d_model), bf16) for v in values]
         + [shape((sources, 32, width), bf16)],
         in_specs=[pl.BlockSpec(memory_space=pltpu.SMEM)]
-        + [
-            pl.BlockSpec((tokens, d_model), lambda g: (0, 0), pipeline_mode=pl.Buffered(1))
-            for _ in range(4)
-        ]
-        + [
-            pl.BlockSpec((sources, 16, width), lambda g: (0, 2 + layer, 0)),
-            pl.BlockSpec((sources, width, NSUB), lambda g: (0, 0, 0), pipeline_mode=pl.Buffered(1)),
-        ]
-        + specs,
-        out_specs=[dv_spec(n) for n in range(pieces)]
-        + [pl.BlockSpec((sources, 32, width), lambda g: (0, 0, 0))],
+        + [pl.BlockSpec(memory_space=pltpu.VMEM)] * 6
+        + [pl.BlockSpec(memory_space=pl.ANY)] * pieces,
+        out_specs=[pl.BlockSpec(memory_space=pl.ANY)] * pieces
+        + [pl.BlockSpec(memory_space=pltpu.VMEM)],
         scratch_shapes=[
             pltpu.VMEM((4, tokens, d_model), bf16),
             pltpu.VMEM((sources, width, d_model), f32),
             pltpu.VMEM((sources, width, NSUB), f32),
+            whole,
+            whole,
+            pltpu.SemaphoreType.DMA((blocks,)),
+            pltpu.SemaphoreType.DMA((blocks,)),
         ],
         compiler_params=pltpu.CompilerParams(vmem_limit_bytes=50 * MIB),
         cost_estimate=pl.CostEstimate(

time: 590 us -> 589 us (level)
  starting transfers between devices: 129 us -> 139 us
  Pallas kernels: 158 us -> 151 us
    ppermute x101, starting transfers between devices: 119 us -> 130 us  [swap(): return lax.ppermute(x, axis, [(i, i ^ step) for i in range(size)])]
    pallas_call x2, Pallas kernels: 28.6 us -> 22.2 us  [write_call(): pl.pallas_call(functools.partial(write_kernel, plan=plan, pieces=pieces,...]
  transfers between devices with their start and end apart: 114 -> 114, of which waited for: 57 -> 57; matrix products, arithmetic and copies ran while one was open for 3% -> 3% of each run, Pallas kernels for 23% -> 22%
where the time goes in v5:
time: 589 us; the launch traced here: 584 us
  waiting for transfers between devices  188 us (32%)
  Pallas kernels  151 us (26%)
  starting transfers between devices  139 us (24%)
  local copies, waits for them, and re-layouts  57.1 us (10%)
  blocking collectives  27.7 us (5%)
  between operations  15.5 us (3%)
    ppermute x101, waiting for transfers between devices, swap(): return lax.ppermute(x, axis, [(i, i ^ step) for i in range(size)])  169 us
    ppermute x101, starting transfers between devices, swap(): return lax.ppermute(x, axis, [(i, i ^ step) for i in range(size)])  130 us
    pallas_call x35, Pallas kernels, kernel_call(): pl.pallas_call(body, out_shape=outs, in_specs=in_specs, out_specs=[pl.Blo...  96.6 us
    unnamed x258, local copies, waits for them, and re-layouts  42.9 us
    pallas_call x2, Pallas kernels, write_call(): pl.pallas_call(functools.partial(write_kernel, plan=plan, pieces=pieces,...  22.2 us
    pallas_call x2, Pallas kernels, read_call(): pl.pallas_call(functools.partial(read_kernel, plan=plan, pieces=len(value...  19.3 us
    all_to_all x1, blocking collectives, body(): gw = lax.all_to_all(gw, ('ctx', 'tp'), 0, 0, tiled=True)  15.4 us
    pallas_call x2, Pallas kernels, table_grad_call(): pl.pallas_call(table_grad_kernel, grid=(rows // block,), out_shape=shape(...  12.9 us
  transfers between devices with their start and end apart: 114, of which 57 were waited for; matrix products, arithmetic and copies ran while one was open for 3% of the time, Pallas kernels for 22%

profile of v5, /device:TPU:0, one launch (start us, length us, event | category | flops | bytes accessed | tf_op | source)
XLA Modules:
  0.0 584.3 jit_solution(8278202243860466074)
XLA Ops:
  54.6 6.8 %collective-permute-done.13.r2 = bf16[64,1024]{1,0:T(8,128)(2,1)S(1)} collective-permute-done((bf16[64,1024]{1,0:T(8,128)(2,1)}, bf16[64,1024]{1,0:T(8,128)(2,1)S(1)}, u32[]{:S(2)}, u32[]{:S(2)}) %collective-permute-start.13) | collective-permute-done | bytes 131104 | tf_op jit(solution)/shard_map/ppermute | solution.py:34
  62.7 5.9 %lookup.2 = (f32[64,1024]{1,0:T(8,128)S(1)}, bf16[64,1024]{1,0:T(8,128)(2,1)S(1)}, bf16[64,512]{1,0:T(8,128)(2,1)S(1)}, f32[32,256]{1,0:T(8,128)S(1)}, bf16[16,64,128]{2,1,0:T(8,128)(2,1)}) custom-call(s32[4]{0:T(128)S(1)} %pad_add_fusion.idx, bf16[256,1024]{1,0:T(8,128)(2,1)S(1)} %bitcast.62, bf16[64,1024]{1,0:T(8,128)(2,1)S(1)} %get-tuple-element.233.p0, ...), custom_call_target="tpu_custom_call" | custom-call | bytes 3342336 | tf_op jit(solution)/shard_map/lookup/pallas_call | solution.py:55
  79.3 8.6 %all-to-all-done.w_ref.names_ref = bf16[16,64,128]{2,1,0:T(8,128)(2,1)S(1)} async-done(((bf16[16,64,128]{2,1,0:T(8,128)(2,1)}), bf16[16,64,128]{2,1,0:T(8,128)(2,1)S(1)}, u32[]{:S(2)}, u32[]{:S(2)}) %all-to-all-start) | async-done | bytes 262176 | tf_op jit(solution)/shard_map/all_to_all | solution.py:1181
  87.9 9.7 %memory_read.2 = (bf16[256,1024]{1,0:T(8,128)(2,1)S(1)}, bf16[256,1024]{1,0:T(8,128)(2,1)S(1)}, bf16[256,1024]{1,0:T(8,128)(2,1)S(1)}, bf16[256,1024]{1,0:T(8,128)(2,1)S(1)}, f32[16,128,256]{2,1,0:T(8,128)}) custom-call(s32[4]{0:T(128)S(1)} %pad_add_fusion.idx, bf16[16,64,128]{2,1,0:T(8,128)(2,1)S(1)} %all-to-all-done.w_ref.names_ref, ...), custom_call_target="tpu_custom_call" | custom-call | flops 2147483648 | bytes 20971520 | tf_op jit(solution)/shard_map/memory_read/pallas_call | solution.py:827
  101.3 7.8 %collective-permute-done.16.r1 = bf16[256,1024]{1,0:T(8,128)(2,1)S(1)} collective-permute-done((bf16[256,1024]{1,0:T(8,128)(2,1)S(1)}, bf16[256,1024]{1,0:T(8,128)(2,1)S(1)}, u32[]{:S(2)}, u32[]{:S(2)}) %collective-permute-start.16) | collective-permute-done | bytes 524320 | tf_op jit(solution)/shard_map/ppermute | solution.py:34
  200.6 12.4 %all_to_all.20.w_ref = bf16[16,32,128]{2,1,0:T(8,128)(2,1)S(1)} all-to-all(bf16[16,32,128]{2,1,0:T(8,128)(2,1)} %copy-done.92), channel_id=1, replica_groups=mesh['fsdp'=2,'ctx'=4,'tp'=4] {'ctx','tp'}, dimensions={0} | all-to-all | bytes 262144 | tf_op jit(solution)/shard_map/all_to_all | solution.py:1181
  212.9 9.6 %memory_read.3 = (bf16[256,1024]{1,0:T(8,128)(2,1)S(1)}, bf16[256,1024]{1,0:T(8,128)(2,1)S(1)}, bf16[256,1024]{1,0:T(8,128)(2,1)S(1)}, bf16[256,1024]{1,0:T(8,128)(2,1)S(1)}, f32[16,128,256]{2,1,0:T(8,128)}) custom-call(s32[4]{0:T(128)S(1)} %pad_add_fusion.idx, bf16[16,32,128]{2,1,0:T(8,128)(2,1)S(1)} %all_to_all.20.w_ref, ...), custom_call_target="tpu_custom_call" | custom-call | flops 2147483648 | bytes 20971520 | tf_op jit(solution)/shard_map/memory_read/pallas_call | solution.py:827
  226.1 11.4 %collective-permute-done.36.r1 = bf16[256,1024]{1,0:T(8,128)(2,1)S(1)} collective-permute-done((bf16[256,1024]{1,0:T(8,128)(2,1)S(1)}, bf16[256,1024]{1,0:T(8,128)(2,1)S(1)}, u32[]{:S(2)}, u32[]{:S(2)}) %collective-permute-start.36) | collective-permute-done | bytes 524320 | tf_op jit(solution)/shard_map/ppermute | solution.py:34
  237.4 7.1 %collective-permute-done.37.r2 = bf16[256,1024]{1,0:T(8,128)(2,1)S(1)} collective-permute-done((bf16[256,1024]{1,0:T(8,128)(2,1)S(1)}, bf16[256,1024]{1,0:T(8,128)(2,1)S(1)}, u32[]{:S(2)}, u32[]{:S(2)}) %collective-permute-start.37) | collective-permute-done | bytes 524320 | tf_op jit(solution)/shard_map/ppermute | solution.py:34
  279.1 10.4 %collective-permute-done.47.g3 = bf16[256,1024]{1,0:T(8,128)(2,1)S(1)} collective-permute-done((bf16[256,1024]{1,0:T(8,128)(2,1)}, bf16[256,1024]{1,0:T(8,128)(2,1)S(1)}, u32[]{:S(2)}, u32[]{:S(2)}) %collective-permute-start.47) | collective-permute-done | bytes 524320 | tf_op jit(solution)/shard_map/ppermute | solution.py:34
  294.9 11.2 %memory_write.2 = (bf16[2048,1024]{1,0:T(8,128)(2,1)}, bf16[2048,1024]{1,0:T(8,128)(2,1)}, bf16[16,32,128]{2,1,0:T(8,128)(2,1)S(1)}) custom-call(s32[4]{0:T(128)S(1)} %pad_add_fusion.idx, bf16[256,1024]{1,0:T(8,128)(2,1)} %constant_dynamic-update-slice_fusion.g0, bf16[256,1024]{1,0:T(8,128)(2,1)S(1)} %collective-permute-done.45.g1, ...), custom_call_target="tpu_custom_call" | custom-call | flops 3221225472 | bytes 29360128 | tf_op jit(solution)/shard_map/memory_write/pallas_call | solution.py:925
  306.2 15.4 %all_to_all.21.gw_ref = bf16[16,32,128]{2,1,0:T(8,128)(2,1)S(1)} all-to-all(bf16[16,32,128]{2,1,0:T(8,128)(2,1)S(1)} %get-tuple-element.292), channel_id=1, replica_groups=mesh['fsdp'=2,'ctx'=4,'tp'=4] {'ctx','tp'}, dimensions={0} | all-to-all | bytes 262144 | tf_op jit(solution)/shard_map/all_to_all | solution.py:1246
  321.6 5.8 lookup_back.2
  337.2 10.2 %collective-permute-done.49.g2 = bf16[64,1024]{1,0:T(8,128)(2,1)S(1)} collective-permute-done((bf16[64,1024]{1,0:T(8,128)(2,1)S(1)}, bf16[64,1024]{1,0:T(8,128)(2,1)S(1)}, u32[]{:S(2)}, u32[]{:S(2)}) %collective-permute-start.49) | collective-permute-done | bytes 131104 | tf_op jit(solution)/shard_map/ppermute | solution.py:34
  356.0 5.7 attend_back.2
  416.1 6.2 %table_grad.2.refs_0_ = f32[2,2048,1024]{2,1,0:T(8,128)} custom-call(bf16[2048,1024]{1,0:T(8,128)(2,1)S(1)} %copy-done.8, bf16[2048,1024]{1,0:T(8,128)(2,1)} %collective-permute-done.69.b_ref), custom_call_target="tpu_custom_call" | custom-call | bytes 16777216 | tf_op jit(solution)/shard_map/table_grad/pallas_call | solution.py:973
  422.9 10.1 %collective-permute-done.67.g2 = bf16[256,1024]{1,0:T(8,128)(2,1)S(1)} collective-permute-done((bf16[256,1024]{1,0:T(8,128)(2,1)S(1)}, bf16[256,1024]{1,0:T(8,128)(2,1)S(1)}, u32[]{:S(2)}, u32[]{:S(2)}) %collective-permute-start.67) | collective-permute-done | bytes 524320 | tf_op jit(solution)/shard_map/ppermute | solution.py:34
  433.1 10.9 %memory_write.3 = (bf16[2048,1024]{1,0:T(8,128)(2,1)}, bf16[2048,1024]{1,0:T(8,128)(2,1)}, bf16[16,32,128]{2,1,0:T(8,128)(2,1)S(1)}) custom-call(s32[4]{0:T(128)S(1)} %pad_add_fusion.idx, bf16[256,1024]{1,0:T(8,128)(2,1)S(1)} %constant_dynamic-update-slice_fusion.4.g0, bf16[256,1024]{1,0:T(8,128)(2,1)S(1)} %collective-permute-done.66.g1, ...), custom_call_target="tpu_custom_call" | custom-call | flops 3221225472 | bytes 29360128 | tf_op jit(solution)/shard_map/memory_write/pallas_call | solution.py:925
  449.1 7.7 %reduce-scatter.3.cloned.1.call-done = bf16[1,1856,256]{2,1,0:T(8,128)(2,1)} async-done(((bf16[2,1856,256]{2,1,0:T(8,128)(2,1)}), bf16[1,1856,256]{2,1,0:T(8,128)(2,1)}) %reduce-scatter.3.cloned.1.call-update) | async-done | bytes 950288 | tf_op jit(solution)/shard_map/reduce_scatter | solution.py:1003
  459.2 5.9 %lookup_back.3 = (f32[64,1024]{1,0:T(8,128)S(1)}, bf16[64,1024]{1,0:T(8,128)(2,1)S(1)}, f32[1,1024]{1,0:T(1,128)S(1)}, bf16[64,640]{1,0:T(8,128)(2,1)S(1)}, bf16...) custom-call(s32[4]{0:T(128)S(1)} %pad_add_fusion.idx, ...), custom_call_target="tpu_custom_call" | custom-call | bytes 7344128 | tf_op jit(solution)/shard_map/lookup_back/pallas_call | solution.py:55
  473.4 5.9 %collective-permute-start.78 = (bf16[64,640]{1,0:T(8,128)(2,1)S(1)}, bf16[64,640]{1,0:T(8,128)(2,1)S(1)}, u32[]{:S(2)}, u32[]{:S(2)}) collective-permute-start(bf16[64,640]{1,0:T(8,128)(2,1)S(1)} %get-tuple-element.350), channel_id=1, source_target_pairs={{0,2},{1,3},{2,0},{3,1},{4,6},{5,7},{6,4},{7,5},{8,10},{9,11},{10,... | collective-permute-start | bytes 245768 | tf_op jit(solution)/shard_map/ppermute | solution.py:34
  480.8 6.7 %table_grad.3 = f32[2,2048,1024]{2,1,0:T(8,128)} custom-call(bf16[2048,1024]{1,0:T(8,128)(2,1)S(1)} %copy-done.7, bf16[2048,1024]{1,0:T(8,128)(2,1)} %collective-permute-done.73.b_ref, f32[2,2048,1024]{2,1,0:T(8,128)} %table_grad.2.refs_0_), custom_call_target="tpu_custom_call", output_to_operand_aliasing={{}: (2, {})} | custom-call | bytes 16777216 | tf_op jit(solution)/shard_map/table_grad/pallas_call | solution.py:973
  501.0 5.8 attend_back.3
  539.2 7.9 %collective-permute-done.84.r2 = bf16[80,1024]{1,0:T(8,128)(2,1)S(1)} collective-permute-done((bf16[80,1024]{1,0:T(8,128)(2,1)S(1)}, bf16[80,1024]{1,0:T(8,128)(2,1)S(1)}, u32[]{:S(2)}, u32[]{:S(2)}) %collective-permute-start.84) | collective-permute-done | bytes 163872 | tf_op jit(solution)/shard_map/ppermute | solution.py:34
  (550 shorter events, 363.8 us)
Async XLA Ops:
  7.2 54.2 %all-gather.16.cloned.1.call-start = ((), (), s32[]{:S(2)}) async-start(), calls=%async_computation.6 | async-start | bytes 1474560 | tf_op jit(solution)/shard_map/all_gather | solution.py:1056
  20.3 101.7 %all-gather.18.cloned.1.call-start = ((), (), s32[]{:S(2)}) async-start(), calls=%async_computation.9 | async-start | bytes 4718592 | tf_op jit(solution)/shard_map/all_gather | solution.py:1056
  20.6 67.3 %collective-permute-start.15 = (bf16[2,2048,1024]{2,1,0:T(8,128)(2,1)}, bf16[2,2048,1024]{2,1,0:T(8,128)(2,1)}, u32[]{:S(2)}, u32[]{:S(2)}) collective-permute-start(bf16[2,2048,1024]{2,1,0:T(8,128)(2,1)} %refs_0_.7), channel_id=1, source_target_pairs={{0,16},{16,0},{1,17},{17,1},{2,18},{18,2},{3,19},{19,3},{4,20},{20... | collective-permute-start | bytes 25165832 | tf_op jit(solution)/shard_map/ppermute | solution.py:34
  73.7 114.7 %all-gather.20.cloned.1.call-start = ((), (), s32[]{:S(2)}) async-start(), calls=%async_computation.10 | async-start | bytes 1474560 | tf_op jit(solution)/shard_map/all_gather | solution.py:1056
  101.2 40.1 %collective-permute-start.25 = (bf16[512,768]{1,0:T(8,128)(2,1)S(1)}, bf16[512,768]{1,0:T(8,128)(2,1)}, u32[]{:S(2)}, u32[]{:S(2)}) collective-permute-start(bf16[512,768]{1,0:T(8,128)(2,1)S(1)} %pad_maximum_fusion.1.refs_0_), channel_id=1, source_target_pairs={{0,16},{16,0},{1,17},{17,1},{2,18},{18,2},{3,19},{19,3},{4,20},{20... | collective-permute-start | bytes 2359304 | tf_op jit(solution)/shard_map/ppermute | solution.py:34
  151.5 99.5 %all-gather.22.cloned.1.call-start = ((), (), s32[]{:S(2)}) async-start(), calls=%async_computation.11 | async-start | bytes 4718592 | tf_op jit(solution)/shard_map/all_gather | solution.py:1056
  200.5 178.7 %all-gather.24.cloned.1.call-start = ((), (), s32[]{:S(2)}) async-start(), calls=%async_computation.12 | async-start | bytes 1310720 | tf_op jit(solution)/shard_map/all_gather | solution.py:1292
  223.5 21.0 %collective-permute-start.37 = (bf16[256,1024]{1,0:T(8,128)(2,1)S(1)}, bf16[256,1024]{1,0:T(8,128)(2,1)S(1)}, u32[]{:S(2)}, u32[]{:S(2)}) collective-permute-start(bf16[256,1024]{1,0:T(8,128)(2,1)S(1)} %get-tuple-element.279), channel_id=1, source_target_pairs={{0,8},{4,12},{8,0},{12,4},{1,9},{5,13},{9,1},{13,5},{2,10},{6,14},... | collective-permute-start | bytes 1572872 | tf_op jit(solution)/shard_map/ppermute | solution.py:34
  224.2 20.3 %collective-permute-start.38 = (bf16[256,1024]{1,0:T(8,128)(2,1)S(1)}, bf16[256,1024]{1,0:T(8,128)(2,1)S(1)}, u32[]{:S(2)}, u32[]{:S(2)}) collective-permute-start(bf16[256,1024]{1,0:T(8,128)(2,1)S(1)} %get-tuple-element.280), channel_id=1, source_target_pairs={{0,12},{4,8},{8,4},{12,0},{1,13},{5,9},{9,5},{13,1},{2,14},{6,10},... | collective-permute-start | bytes 1572872 | tf_op jit(solution)/shard_map/ppermute | solution.py:34
  274.1 105.1 %all-gather.26.cloned.1.call-start = ((), (), s32[]{:S(2)}) async-start(), calls=%async_computation.13 | async-start | bytes 1310720 | tf_op jit(solution)/shard_map/all_gather | solution.py:1287
  274.7 113.3 %all-gather.28.cloned.1.call-start = ((), (), s32[]{:S(2)}) async-start(), calls=%async_computation.14 | async-start | bytes 1310720 | tf_op jit(solution)/shard_map/all_gather | solution.py:1288
  275.5 169.3 %all-gather.30.cloned.1.call-start = ((), (), s32[]{:S(2)}) async-start(), calls=%async_computation.15 | async-start | bytes 1310720 | tf_op jit(solution)/shard_map/all_gather | solution.py:1244
  332.5 20.1 %collective-permute-start.55 = (bf16[64,640]{1,0:T(8,128)(2,1)S(1)}, bf16[64,640]{1,0:T(8,128)(2,1)S(1)}, u32[]{:S(2)}, u32[]{:S(2)}) collective-permute-start(bf16[64,640]{1,0:T(8,128)(2,1)S(1)} %get-tuple-element.302), channel_id=1, source_target_pairs={{0,2},{1,3},{2,0},{3,1},{4,6},{5,7},{6,4},{7,5},{8,10},{9,11},{10,... | collective-permute-start | bytes 245768 | tf_op jit(solution)/shard_map/ppermute | solution.py:34
  406.3 42.8 %reduce-scatter.5.cloned.1.call-start = ((), (), s32[]{:S(2)}) async-start(), calls=%async_computation.8 | async-start | bytes 2359296 | tf_op jit(solution)/shard_map/reduce_scatter | solution.py:1003
  407.1 49.7 %reduce-scatter.3.cloned.1.call-start = ((), (), s32[]{:S(2)}) async-start(), calls=%async_computation.7 | async-start | bytes 2850816 | tf_op jit(solution)/shard_map/reduce_scatter | solution.py:1003
  409.5 23.5 %collective-permute-start.67 = (bf16[256,1024]{1,0:T(8,128)(2,1)S(1)}, bf16[256,1024]{1,0:T(8,128)(2,1)S(1)}, u32[]{:S(2)}, u32[]{:S(2)}) collective-permute-start(bf16[256,1024]{1,0:T(8,128)(2,1)S(1)} %constant_dynamic-update-slice_fusion.4.g0), channel_id=1, source_target_pairs={{0,8},{4,12},{8,0},{12,4},{1,9},{5,13},{9,1},{13,5},{2,10},{6,14},... | collective-permute-start | bytes 1572872 | tf_op jit(solution)/shard_map/ppermute | solution.py:34
  410.1 23.0 %collective-permute-start.66 = (bf16[256,1024]{1,0:T(8,128)(2,1)S(1)}, bf16[256,1024]{1,0:T(8,128)(2,1)S(1)}, u32[]{:S(2)}, u32[]{:S(2)}) collective-permute-start(bf16[256,1024]{1,0:T(8,128)(2,1)S(1)} %constant_dynamic-update-slice_fusion.4.g0), channel_id=1, source_target_pairs={{0,4},{4,0},{8,12},{12,8},{1,5},{5,1},{9,13},{13,9},{2,6},{6,2},{1... | collective-permute-start | bytes 1572872 | tf_op jit(solution)/shard_map/ppermute | solution.py:34
  444.7 34.6 %collective-permute-start.73 = (bf16[2048,1024]{1,0:T(8,128)(2,1)}, bf16[2048,1024]{1,0:T(8,128)(2,1)}, u32[]{:S(2)}, u32[]{:S(2)}) collective-permute-start(bf16[2048,1024]{1,0:T(8,128)(2,1)} %get-tuple-element.341), channel_id=1, source_target_pairs={{0,16},{16,0},{1,17},{17,1},{2,18},{18,2},{3,19},{19,3},{4,20},{20... | collective-permute-start | bytes 12582920 | tf_op jit(solution)/shard_map/ppermute | solution.py:34
  449.1 102.0 %all-reduce.3.cloned.1.call-start = ((), (), s32[]{:S(2)}) async-start(), calls=%async_computation.16 | async-start | bytes 3473408 | tf_op jit(solution)/shard_map/psum | solution.py:1004
  469.6 21.3 %collective-permute-start.77 = (bf16[64,640]{1,0:T(8,128)(2,1)S(1)}, bf16[64,640]{1,0:T(8,128)(2,1)S(1)}, u32[]{:S(2)}, u32[]{:S(2)}) collective-permute-start(bf16[64,640]{1,0:T(8,128)(2,1)S(1)} %get-tuple-element.349), channel_id=1, source_target_pairs={{0,1},{1,0},{2,3},{3,2},{4,5},{5,4},{6,7},{7,6},{8,9},{9,8},{10,11... | collective-permute-start | bytes 245768 | tf_op jit(solution)/shard_map/ppermute | solution.py:34
  495.5 21.5 %collective-permute-start.86 = (bf16[1856,256]{1,0:T(8,128)(2,1)S(1)}, bf16[1856,256]{1,0:T(8,128)(2,1)S(1)}, u32[]{:S(2)}, u32[]{:S(2)}) collective-permute-start(bf16[1856,256]{1,0:T(8,128)(2,1)S(1)} %get-tuple-element.373), channel_id=1, source_target_pairs={{0,16},{16,0},{1,17},{17,1},{2,18},{18,2},{3,19},{19,3},{4,20},{20... | collective-permute-start | bytes 2850824 | tf_op jit(solution)/shard_map/ppermute | solution.py:34
  524.5 23.9 %collective-permute-start.94 = (bf16[384,256]{1,0:T(8,128)(2,1)S(1)}, bf16[384,256]{1,0:T(8,128)(2,1)S(1)}, u32[]{:S(2)}, u32[]{:S(2)}) collective-permute-start(bf16[384,256]{1,0:T(8,128)(2,1)S(1)} %get-tuple-element.390), channel_id=1, source_target_pairs={{0,4},{4,0},{8,12},{12,8},{1,5},{5,1},{9,13},{13,9},{2,6},{6,2},{1... | collective-permute-start | bytes 589832 | tf_op jit(solution)/shard_map/ppermute | solution.py:34
  551.1 20.0 %collective-permute-start.100 = (bf16[864,256]{1,0:T(8,128)(2,1)}, bf16[864,256]{1,0:T(8,128)(2,1)S(1)}, u32[]{:S(2)}, u32[]{:S(2)}) collective-permute-start(bf16[864,256]{1,0:T(8,128)(2,1)} %plane_sum.1.refs_0_), channel_id=1, source_target_pairs={{0,12},{4,8},{8,4},{12,0},{1,13},{5,9},{9,5},{13,1},{2,14},{6,10},... | collective-permute-start | bytes 1327112 | tf_op jit(solution)/shard_map/ppermute | solution.py:34
  551.5 21.7 %collective-permute-start.99 = (bf16[864,256]{1,0:T(8,128)(2,1)}, bf16[864,256]{1,0:T(8,128)(2,1)S(1)}, u32[]{:S(2)}, u32[]{:S(2)}) collective-permute-start(bf16[864,256]{1,0:T(8,128)(2,1)} %plane_sum.1.refs_0_), channel_id=1, source_target_pairs={{0,8},{4,12},{8,0},{12,4},{1,9},{5,13},{9,1},{13,5},{2,10},{6,14},... | collective-permute-start | bytes 1327112 | tf_op jit(solution)/shard_map/ppermute | solution.py:34
  (216 other events, 2353.7 us)
Sparse Core Ops, SparseCore 0:
  20.5 28.9 all-gather.15
  68.7 48.3 all-gather.17
  151.6 22.8 all-gather.19
  200.6 46.5 all-gather.21
  274.3 26.6 all-gather.23
  302.4 39.2 all-gather.25
  343.3 33.4 all-gather.27
  406.4 26.6 all-gather.29
  435.4 8.5 reduce-scatter.4
  446.2 10.5 reduce-scatter.2
  460.0 70.2 all-reduce.2

commit v6 on v5

--- a/solution.py
+++ b/solution.py
@@ -964,7 +964,7 @@
 
 def table_grad_call(mine, arrived, layer, layers, earlier):
     rows, d_model = mine.shape
-    block = min(rows, 512)
+    block = min(rows, 1024)
     specs = [pl.BlockSpec((block, d_model), lambda g: (g, 0))] * 2
     args = [mine, arrived]
     if earlier is not None:
@@ -977,7 +977,7 @@
         in_specs=specs,
         out_specs=pl.BlockSpec((None, block, d_model), lambda g: (layer, g, 0)),
         input_output_aliases={} if earlier is None else {2: 0},
-        compiler_params=pltpu.CompilerParams(vmem_limit_bytes=32 * MIB),
+        compiler_params=pltpu.CompilerParams(vmem_limit_bytes=50 * MIB),
         cost_estimate=pl.CostEstimate(flops=0, bytes_accessed=16 * MIB, transcendentals=0),
         name="table_grad",
     )(*args)

time: 589 us -> 587 us (level)
    unnamed x258 -> x254, local copies, waits for them, and re-layouts: 42.9 us -> 40.7 us
where the time goes in v6:
time: 587 us; the launch traced here: 583 us
  waiting for transfers between devices  190 us (32%)
  Pallas kernels  150 us (26%)
  starting transfers between devices  138 us (24%)
  local copies, waits for them, and re-layouts  54.9 us (9%)
  blocking collectives  27.8 us (5%)
  between operations  15.5 us (3%)
    ppermute x101, waiting for transfers between devices, swap(): return lax.ppermute(x, axis, [(i, i ^ step) for i in range(size)])  172 us
    ppermute x101, starting transfers between devices, swap(): return lax.ppermute(x, axis, [(i, i ^ step) for i in range(size)])  128 us
    pallas_call x35, Pallas kernels, kernel_call(): pl.pallas_call(body, out_shape=outs, in_specs=in_specs, out_specs=[pl.Blo...  96.5 us
    unnamed x254, local copies, waits for them, and re-layouts  40.7 us
    pallas_call x2, Pallas kernels, write_call(): pl.pallas_call(functools.partial(write_kernel, plan=plan, pieces=pieces,...  22.2 us
    pallas_call x2, Pallas kernels, read_call(): pl.pallas_call(functools.partial(read_kernel, plan=plan, pieces=len(value...  19.3 us
    all_to_all x1, blocking collectives, body(): gw = lax.all_to_all(gw, ('ctx', 'tp'), 0, 0, tiled=True)  15.4 us
    pallas_call x2, Pallas kernels, table_grad_call(): pl.pallas_call(table_grad_kernel, grid=(rows // block,), out_shape=shape(...  12.4 us
  transfers between devices with their start and end apart: 114, of which 57 were waited for; matrix products, arithmetic and copies ran while one was open for 3% of the time, Pallas kernels for 22%

profile of v6, /device:TPU:0, one launch (start us, length us, event | category | flops | bytes accessed | tf_op | source)
XLA Modules:
  0.0 582.8 jit_solution(1865678020993224641)
XLA Ops:
  54.6 6.9 %collective-permute-done.13.r2 = bf16[64,1024]{1,0:T(8,128)(2,1)S(1)} collective-permute-done((bf16[64,1024]{1,0:T(8,128)(2,1)}, bf16[64,1024]{1,0:T(8,128)(2,1)S(1)}, u32[]{:S(2)}, u32[]{:S(2)}) %collective-permute-start.13) | collective-permute-done | bytes 131104 | tf_op jit(solution)/shard_map/ppermute | solution.py:34
  62.7 5.8 %lookup.2 = (f32[64,1024]{1,0:T(8,128)S(1)}, bf16[64,1024]{1,0:T(8,128)(2,1)S(1)}, bf16[64,512]{1,0:T(8,128)(2,1)S(1)}, f32[32,256]{1,0:T(8,128)S(1)}, bf16[16,64,128]{2,1,0:T(8,128)(2,1)}) custom-call(s32[4]{0:T(128)S(1)} %pad_add_fusion.idx, bf16[256,1024]{1,0:T(8,128)(2,1)S(1)} %bitcast.62, bf16[64,1024]{1,0:T(8,128)(2,1)S(1)} %get-tuple-element.233.p0, ...), custom_call_target="tpu_custom_call" | custom-call | bytes 3342336 | tf_op jit(solution)/shard_map/lookup/pallas_call | solution.py:55
  79.3 8.5 %all-to-all-done.w_ref.names_ref = bf16[16,64,128]{2,1,0:T(8,128)(2,1)S(1)} async-done(((bf16[16,64,128]{2,1,0:T(8,128)(2,1)}), bf16[16,64,128]{2,1,0:T(8,128)(2,1)S(1)}, u32[]{:S(2)}, u32[]{:S(2)}) %all-to-all-start) | async-done | bytes 262176 | tf_op jit(solution)/shard_map/all_to_all | solution.py:1181
  87.9 9.7 %memory_read.2 = (bf16[256,1024]{1,0:T(8,128)(2,1)S(1)}, bf16[256,1024]{1,0:T(8,128)(2,1)S(1)}, bf16[256,1024]{1,0:T(8,128)(2,1)S(1)}, bf16[256,1024]{1,0:T(8,128)(2,1)S(1)}, f32[16,128,256]{2,1,0:T(8,128)}) custom-call(s32[4]{0:T(128)S(1)} %pad_add_fusion.idx, bf16[16,64,128]{2,1,0:T(8,128)(2,1)S(1)} %all-to-all-done.w_ref.names_ref, ...), custom_call_target="tpu_custom_call" | custom-call | flops 2147483648 | bytes 20971520 | tf_op jit(solution)/shard_map/memory_read/pallas_call | solution.py:827
  101.2 7.8 %collective-permute-done.16.r1 = bf16[256,1024]{1,0:T(8,128)(2,1)S(1)} collective-permute-done((bf16[256,1024]{1,0:T(8,128)(2,1)S(1)}, bf16[256,1024]{1,0:T(8,128)(2,1)S(1)}, u32[]{:S(2)}, u32[]{:S(2)}) %collective-permute-start.16) | collective-permute-done | bytes 524320 | tf_op jit(solution)/shard_map/ppermute | solution.py:34
  109.1 5.6 collective-permute-done.18.r3
  200.5 12.4 %all_to_all.20.w_ref = bf16[16,32,128]{2,1,0:T(8,128)(2,1)S(1)} all-to-all(bf16[16,32,128]{2,1,0:T(8,128)(2,1)} %copy-done.90), channel_id=1, replica_groups=mesh['fsdp'=2,'ctx'=4,'tp'=4] {'ctx','tp'}, dimensions={0} | all-to-all | bytes 262144 | tf_op jit(solution)/shard_map/all_to_all | solution.py:1181
  212.9 9.6 %memory_read.3 = (bf16[256,1024]{1,0:T(8,128)(2,1)S(1)}, bf16[256,1024]{1,0:T(8,128)(2,1)S(1)}, bf16[256,1024]{1,0:T(8,128)(2,1)S(1)}, bf16[256,1024]{1,0:T(8,128)(2,1)S(1)}, f32[16,128,256]{2,1,0:T(8,128)}) custom-call(s32[4]{0:T(128)S(1)} %pad_add_fusion.idx, bf16[16,32,128]{2,1,0:T(8,128)(2,1)S(1)} %all_to_all.20.w_ref, ...), custom_call_target="tpu_custom_call" | custom-call | flops 2147483648 | bytes 20971520 | tf_op jit(solution)/shard_map/memory_read/pallas_call | solution.py:827
  226.1 11.4 %collective-permute-done.36.r1 = bf16[256,1024]{1,0:T(8,128)(2,1)S(1)} collective-permute-done((bf16[256,1024]{1,0:T(8,128)(2,1)S(1)}, bf16[256,1024]{1,0:T(8,128)(2,1)S(1)}, u32[]{:S(2)}, u32[]{:S(2)}) %collective-permute-start.36) | collective-permute-done | bytes 524320 | tf_op jit(solution)/shard_map/ppermute | solution.py:34
  237.4 7.1 %collective-permute-done.37.r2 = bf16[256,1024]{1,0:T(8,128)(2,1)S(1)} collective-permute-done((bf16[256,1024]{1,0:T(8,128)(2,1)S(1)}, bf16[256,1024]{1,0:T(8,128)(2,1)S(1)}, u32[]{:S(2)}, u32[]{:S(2)}) %collective-permute-start.37) | collective-permute-done | bytes 524320 | tf_op jit(solution)/shard_map/ppermute | solution.py:34
  279.0 10.4 %collective-permute-done.47.g3 = bf16[256,1024]{1,0:T(8,128)(2,1)S(1)} collective-permute-done((bf16[256,1024]{1,0:T(8,128)(2,1)}, bf16[256,1024]{1,0:T(8,128)(2,1)S(1)}, u32[]{:S(2)}, u32[]{:S(2)}) %collective-permute-start.47) | collective-permute-done | bytes 524320 | tf_op jit(solution)/shard_map/ppermute | solution.py:34
  295.0 11.2 %memory_write.2 = (bf16[2048,1024]{1,0:T(8,128)(2,1)}, bf16[2048,1024]{1,0:T(8,128)(2,1)}, bf16[16,32,128]{2,1,0:T(8,128)(2,1)S(1)}) custom-call(s32[4]{0:T(128)S(1)} %pad_add_fusion.idx, bf16[256,1024]{1,0:T(8,128)(2,1)} %constant_dynamic-update-slice_fusion.g0, bf16[256,1024]{1,0:T(8,128)(2,1)S(1)} %collective-permute-done.45.g1, ...), custom_call_target="tpu_custom_call" | custom-call | flops 3221225472 | bytes 29360128 | tf_op jit(solution)/shard_map/memory_write/pallas_call | solution.py:925
  306.2 15.4 %all_to_all.21.gw_ref = bf16[16,32,128]{2,1,0:T(8,128)(2,1)S(1)} all-to-all(bf16[16,32,128]{2,1,0:T(8,128)(2,1)S(1)} %get-tuple-element.292), channel_id=1, replica_groups=mesh['fsdp'=2,'ctx'=4,'tp'=4] {'ctx','tp'}, dimensions={0} | all-to-all | bytes 262144 | tf_op jit(solution)/shard_map/all_to_all | solution.py:1246
  321.7 5.8 lookup_back.2
  337.3 10.0 %collective-permute-done.49.g2 = bf16[64,1024]{1,0:T(8,128)(2,1)S(1)} collective-permute-done((bf16[64,1024]{1,0:T(8,128)(2,1)S(1)}, bf16[64,1024]{1,0:T(8,128)(2,1)S(1)}, u32[]{:S(2)}, u32[]{:S(2)}) %collective-permute-start.49) | collective-permute-done | bytes 131104 | tf_op jit(solution)/shard_map/ppermute | solution.py:34
  355.9 5.8 attend_back.2
  413.5 6.0 %table_grad.2.refs_0_ = f32[2,2048,1024]{2,1,0:T(8,128)} custom-call(bf16[2048,1024]{1,0:T(8,128)(2,1)} %get-tuple-element.328.a_ref, bf16[2048,1024]{1,0:T(8,128)(2,1)} %collective-permute-done.69.b_ref), custom_call_target="tpu_custom_call" | custom-call | bytes 16777216 | tf_op jit(solution)/shard_map/table_grad/pallas_call | solution.py:973
  422.4 10.1 %collective-permute-done.67.g2 = bf16[256,1024]{1,0:T(8,128)(2,1)S(1)} collective-permute-done((bf16[256,1024]{1,0:T(8,128)(2,1)S(1)}, bf16[256,1024]{1,0:T(8,128)(2,1)S(1)}, u32[]{:S(2)}, u32[]{:S(2)}) %collective-permute-start.67) | collective-permute-done | bytes 524320 | tf_op jit(solution)/shard_map/ppermute | solution.py:34
  432.6 10.9 %memory_write.3 = (bf16[2048,1024]{1,0:T(8,128)(2,1)}, bf16[2048,1024]{1,0:T(8,128)(2,1)}, bf16[16,32,128]{2,1,0:T(8,128)(2,1)S(1)}) custom-call(s32[4]{0:T(128)S(1)} %pad_add_fusion.idx, bf16[256,1024]{1,0:T(8,128)(2,1)S(1)} %constant_dynamic-update-slice_fusion.4.g0, bf16[256,1024]{1,0:T(8,128)(2,1)S(1)} %collective-permute-done.66.g1, ...), custom_call_target="tpu_custom_call" | custom-call | flops 3221225472 | bytes 29360128 | tf_op jit(solution)/shard_map/memory_write/pallas_call | solution.py:925
  448.7 6.7 %reduce-scatter.3.cloned.1.call-done = bf16[1,1856,256]{2,1,0:T(8,128)(2,1)} async-done(((bf16[2,1856,256]{2,1,0:T(8,128)(2,1)}), bf16[1,1856,256]{2,1,0:T(8,128)(2,1)}) %reduce-scatter.3.cloned.1.call-update) | async-done | bytes 950288 | tf_op jit(solution)/shard_map/reduce_scatter | solution.py:1003
  458.7 5.8 lookup_back.3
  479.4 6.4 %table_grad.3 = f32[2,2048,1024]{2,1,0:T(8,128)} custom-call(bf16[2048,1024]{1,0:T(8,128)(2,1)} %get-tuple-element.340.a_ref, bf16[2048,1024]{1,0:T(8,128)(2,1)} %collective-permute-done.73.b_ref, f32[2,2048,1024]{2,1,0:T(8,128)} %table_grad.2.refs_0_), custom_call_target="tpu_custom_call", output_to_operand_aliasing={{}: (2, {})} | custom-call | bytes 16777216 | tf_op jit(solution)/shard_map/table_grad/pallas_call | solution.py:973
  499.2 5.8 attend_back.3
  537.7 7.9 %collective-permute-done.84.r2 = bf16[80,1024]{1,0:T(8,128)(2,1)S(1)} collective-permute-done((bf16[80,1024]{1,0:T(8,128)(2,1)S(1)}, bf16[80,1024]{1,0:T(8,128)(2,1)S(1)}, u32[]{:S(2)}, u32[]{:S(2)}) %collective-permute-start.84) | collective-permute-done | bytes 163872 | tf_op jit(solution)/shard_map/ppermute | solution.py:34
  (546 shorter events, 364.2 us)
Async XLA Ops:
  7.2 54.2 %all-gather.16.cloned.1.call-start = ((), (), s32[]{:S(2)}) async-start(), calls=%async_computation.6 | async-start | bytes 1474560 | tf_op jit(solution)/shard_map/all_gather | solution.py:1056
  20.4 101.7 %all-gather.18.cloned.1.call-start = ((), (), s32[]{:S(2)}) async-start(), calls=%async_computation.9 | async-start | bytes 4718592 | tf_op jit(solution)/shard_map/all_gather | solution.py:1056
  20.6 67.3 %collective-permute-start.15 = (bf16[2,2048,1024]{2,1,0:T(8,128)(2,1)}, bf16[2,2048,1024]{2,1,0:T(8,128)(2,1)}, u32[]{:S(2)}, u32[]{:S(2)}) collective-permute-start(bf16[2,2048,1024]{2,1,0:T(8,128)(2,1)} %refs_0_.7), channel_id=1, source_target_pairs={{0,16},{16,0},{1,17},{17,1},{2,18},{18,2},{3,19},{19,3},{4,20},{20... | collective-permute-start | bytes 25165832 | tf_op jit(solution)/shard_map/ppermute | solution.py:34
  73.7 114.7 %all-gather.20.cloned.1.call-start = ((), (), s32[]{:S(2)}) async-start(), calls=%async_computation.10 | async-start | bytes 1474560 | tf_op jit(solution)/shard_map/all_gather | solution.py:1056
  101.2 40.1 %collective-permute-start.25 = (bf16[512,768]{1,0:T(8,128)(2,1)S(1)}, bf16[512,768]{1,0:T(8,128)(2,1)}, u32[]{:S(2)}, u32[]{:S(2)}) collective-permute-start(bf16[512,768]{1,0:T(8,128)(2,1)S(1)} %pad_maximum_fusion.1.refs_0_), channel_id=1, source_target_pairs={{0,16},{16,0},{1,17},{17,1},{2,18},{18,2},{3,19},{19,3},{4,20},{20... | collective-permute-start | bytes 2359304 | tf_op jit(solution)/shard_map/ppermute | solution.py:34
  151.5 99.5 %all-gather.22.cloned.1.call-start = ((), (), s32[]{:S(2)}) async-start(), calls=%async_computation.11 | async-start | bytes 4718592 | tf_op jit(solution)/shard_map/all_gather | solution.py:1056
  200.5 178.8 %all-gather.24.cloned.1.call-start = ((), (), s32[]{:S(2)}) async-start(), calls=%async_computation.12 | async-start | bytes 1310720 | tf_op jit(solution)/shard_map/all_gather | solution.py:1292
  223.5 21.0 %collective-permute-start.37 = (bf16[256,1024]{1,0:T(8,128)(2,1)S(1)}, bf16[256,1024]{1,0:T(8,128)(2,1)S(1)}, u32[]{:S(2)}, u32[]{:S(2)}) collective-permute-start(bf16[256,1024]{1,0:T(8,128)(2,1)S(1)} %get-tuple-element.279), channel_id=1, source_target_pairs={{0,8},{4,12},{8,0},{12,4},{1,9},{5,13},{9,1},{13,5},{2,10},{6,14},... | collective-permute-start | bytes 1572872 | tf_op jit(solution)/shard_map/ppermute | solution.py:34
  224.2 20.3 %collective-permute-start.38 = (bf16[256,1024]{1,0:T(8,128)(2,1)S(1)}, bf16[256,1024]{1,0:T(8,128)(2,1)S(1)}, u32[]{:S(2)}, u32[]{:S(2)}) collective-permute-start(bf16[256,1024]{1,0:T(8,128)(2,1)S(1)} %get-tuple-element.280), channel_id=1, source_target_pairs={{0,12},{4,8},{8,4},{12,0},{1,13},{5,9},{9,5},{13,1},{2,14},{6,10},... | collective-permute-start | bytes 1572872 | tf_op jit(solution)/shard_map/ppermute | solution.py:34
  274.1 105.2 %all-gather.26.cloned.1.call-start = ((), (), s32[]{:S(2)}) async-start(), calls=%async_computation.13 | async-start | bytes 1310720 | tf_op jit(solution)/shard_map/all_gather | solution.py:1287
  274.7 113.4 %all-gather.28.cloned.1.call-start = ((), (), s32[]{:S(2)}) async-start(), calls=%async_computation.14 | async-start | bytes 1310720 | tf_op jit(solution)/shard_map/all_gather | solution.py:1288
  275.4 168.8 %all-gather.30.cloned.1.call-start = ((), (), s32[]{:S(2)}) async-start(), calls=%async_computation.15 | async-start | bytes 1310720 | tf_op jit(solution)/shard_map/all_gather | solution.py:1244
  332.6 20.0 %collective-permute-start.55 = (bf16[64,640]{1,0:T(8,128)(2,1)S(1)}, bf16[64,640]{1,0:T(8,128)(2,1)S(1)}, u32[]{:S(2)}, u32[]{:S(2)}) collective-permute-start(bf16[64,640]{1,0:T(8,128)(2,1)S(1)} %get-tuple-element.302), channel_id=1, source_target_pairs={{0,2},{1,3},{2,0},{3,1},{4,6},{5,7},{6,4},{7,5},{8,10},{9,11},{10,... | collective-permute-start | bytes 245768 | tf_op jit(solution)/shard_map/ppermute | solution.py:34
  405.8 42.8 %reduce-scatter.5.cloned.1.call-start = ((), (), s32[]{:S(2)}) async-start(), calls=%async_computation.8 | async-start | bytes 2359296 | tf_op jit(solution)/shard_map/reduce_scatter | solution.py:1003
  406.6 48.8 %reduce-scatter.3.cloned.1.call-start = ((), (), s32[]{:S(2)}) async-start(), calls=%async_computation.7 | async-start | bytes 2850816 | tf_op jit(solution)/shard_map/reduce_scatter | solution.py:1003
  408.0 24.5 %collective-permute-start.67 = (bf16[256,1024]{1,0:T(8,128)(2,1)S(1)}, bf16[256,1024]{1,0:T(8,128)(2,1)S(1)}, u32[]{:S(2)}, u32[]{:S(2)}) collective-permute-start(bf16[256,1024]{1,0:T(8,128)(2,1)S(1)} %constant_dynamic-update-slice_fusion.4.g0), channel_id=1, source_target_pairs={{0,8},{4,12},{8,0},{12,4},{1,9},{5,13},{9,1},{13,5},{2,10},{6,14},... | collective-permute-start | bytes 1572872 | tf_op jit(solution)/shard_map/ppermute | solution.py:34
  408.6 24.0 %collective-permute-start.66 = (bf16[256,1024]{1,0:T(8,128)(2,1)S(1)}, bf16[256,1024]{1,0:T(8,128)(2,1)S(1)}, u32[]{:S(2)}, u32[]{:S(2)}) collective-permute-start(bf16[256,1024]{1,0:T(8,128)(2,1)S(1)} %constant_dynamic-update-slice_fusion.4.g0), channel_id=1, source_target_pairs={{0,4},{4,0},{8,12},{12,8},{1,5},{5,1},{9,13},{13,9},{2,6},{6,2},{1... | collective-permute-start | bytes 1572872 | tf_op jit(solution)/shard_map/ppermute | solution.py:34
  444.2 33.5 %collective-permute-start.73 = (bf16[2048,1024]{1,0:T(8,128)(2,1)}, bf16[2048,1024]{1,0:T(8,128)(2,1)}, u32[]{:S(2)}, u32[]{:S(2)}) collective-permute-start(bf16[2048,1024]{1,0:T(8,128)(2,1)} %get-tuple-element.341), channel_id=1, source_target_pairs={{0,16},{16,0},{1,17},{17,1},{2,18},{18,2},{3,19},{19,3},{4,20},{20... | collective-permute-start | bytes 12582920 | tf_op jit(solution)/shard_map/ppermute | solution.py:34
  448.6 101.1 %all-reduce.3.cloned.1.call-start = ((), (), s32[]{:S(2)}) async-start(), calls=%async_computation.16 | async-start | bytes 3473408 | tf_op jit(solution)/shard_map/psum | solution.py:1004
  469.0 20.1 %collective-permute-start.77 = (bf16[64,640]{1,0:T(8,128)(2,1)S(1)}, bf16[64,640]{1,0:T(8,128)(2,1)S(1)}, u32[]{:S(2)}, u32[]{:S(2)}) collective-permute-start(bf16[64,640]{1,0:T(8,128)(2,1)S(1)} %get-tuple-element.349), channel_id=1, source_target_pairs={{0,1},{1,0},{2,3},{3,2},{4,5},{5,4},{6,7},{7,6},{8,9},{9,8},{10,11... | collective-permute-start | bytes 245768 | tf_op jit(solution)/shard_map/ppermute | solution.py:34
  493.8 21.4 %collective-permute-start.86 = (bf16[1856,256]{1,0:T(8,128)(2,1)S(1)}, bf16[1856,256]{1,0:T(8,128)(2,1)S(1)}, u32[]{:S(2)}, u32[]{:S(2)}) collective-permute-start(bf16[1856,256]{1,0:T(8,128)(2,1)S(1)} %get-tuple-element.373), channel_id=1, source_target_pairs={{0,16},{16,0},{1,17},{17,1},{2,18},{18,2},{3,19},{19,3},{4,20},{20... | collective-permute-start | bytes 2850824 | tf_op jit(solution)/shard_map/ppermute | solution.py:34
  522.9 24.1 %collective-permute-start.94 = (bf16[384,256]{1,0:T(8,128)(2,1)S(1)}, bf16[384,256]{1,0:T(8,128)(2,1)S(1)}, u32[]{:S(2)}, u32[]{:S(2)}) collective-permute-start(bf16[384,256]{1,0:T(8,128)(2,1)S(1)} %get-tuple-element.390), channel_id=1, source_target_pairs={{0,4},{4,0},{8,12},{12,8},{1,5},{5,1},{9,13},{13,9},{2,6},{6,2},{1... | collective-permute-start | bytes 589832 | tf_op jit(solution)/shard_map/ppermute | solution.py:34
  549.7 20.0 %collective-permute-start.100 = (bf16[864,256]{1,0:T(8,128)(2,1)}, bf16[864,256]{1,0:T(8,128)(2,1)S(1)}, u32[]{:S(2)}, u32[]{:S(2)}) collective-permute-start(bf16[864,256]{1,0:T(8,128)(2,1)} %plane_sum.1.refs_0_), channel_id=1, source_target_pairs={{0,12},{4,8},{8,4},{12,0},{1,13},{5,9},{9,5},{13,1},{2,14},{6,10},... | collective-permute-start | bytes 1327112 | tf_op jit(solution)/shard_map/ppermute | solution.py:34
  550.0 21.6 %collective-permute-start.99 = (bf16[864,256]{1,0:T(8,128)(2,1)}, bf16[864,256]{1,0:T(8,128)(2,1)S(1)}, u32[]{:S(2)}, u32[]{:S(2)}) collective-permute-start(bf16[864,256]{1,0:T(8,128)(2,1)} %plane_sum.1.refs_0_), channel_id=1, source_target_pairs={{0,8},{4,12},{8,0},{12,4},{1,9},{5,13},{9,1},{13,5},{2,10},{6,14},... | collective-permute-start | bytes 1327112 | tf_op jit(solution)/shard_map/ppermute | solution.py:34
  (214 other events, 2323.4 us)
Sparse Core Ops, SparseCore 0:
  20.5 28.9 all-gather.15
  68.7 48.3 all-gather.17
  151.6 22.8 all-gather.19
  200.6 46.5 all-gather.21
  274.2 26.6 all-gather.23
  302.3 39.1 all-gather.25
  343.1 30.1 all-gather.27
  406.0 25.6 all-gather.29
  433.9 8.5 reduce-scatter.4
  444.7 10.5 reduce-scatter.2
  458.6 70.7 all-reduce.2
